TPU v7x, 128 devices: a whole 4x4x4 slice. The times are simulated.
128 devices in a mesh: dp: 8 (over x, z_lo), ctx: 8 (over y, core), tensor: 2 (over z_hi).
Axes of the slice: x: 4, y: 4, z: 4 (z_hi: 2, z_lo: 2; z = z_hi * 2 + z_lo), core: 2. Of those that a mesh axis runs over, the one named last changes fastest.
Arguments:
- tokens: bfloat16 [32768, 768], P(('dp', 'ctx', 'tensor')), may hold values from -24 to 24
- cotangent: bfloat16 [32768, 768], P(('dp', 'ctx', 'tensor')), may hold values from -24 to 24
- w_qkv: bfloat16 [3, 768, 768], P(None, ('dp', 'ctx'), 'tensor'), may hold values from -0.21875 to 0.21875
- w_out: bfloat16 [768, 768], P('tensor', ('dp', 'ctx')), may hold values from -1.25 to 1.25
- w_up: bfloat16 [768, 3072], P(('dp', 'ctx'), 'tensor'), may hold values from -0.21875 to 0.21875
- w_down: bfloat16 [3072, 768], P('tensor', ('dp', 'ctx')), may hold values from -0.109375 to 0.109375
- norm_gains: bfloat16 [2, 768], P(None, ('dp', 'ctx')), may hold values from 0.099609375 to 1.8984375
Outputs:
- result: bfloat16 [32768, 768], P(('dp', 'ctx', 'tensor'))
- grad_tokens: float32 [32768, 768], P(('dp', 'ctx', 'tensor'))
- grad_qkv: float32 [3, 768, 768], P(None, ('dp', 'ctx'), 'tensor')
- grad_out: float32 [768, 768], P('tensor', ('dp', 'ctx'))
- grad_up: float32 [768, 3072], P(('dp', 'ctx'), 'tensor')
- grad_down: float32 [3072, 768], P('tensor', ('dp', 'ctx'))
- grad_gains: float32 [2, 768], P(None, ('dp', 'ctx'))
All inputs are finite; a program needn't handle non-finite values.
Results may differ from a plain program's by a relative error of at most 0.03.
Values may be sent and summed in bfloat16 or wider, within the bound.
A program may use at most 192 MiB of HBM per device.

v0:
```python
import jax
import jax.numpy as jnp
from jax import lax
from jax.sharding import PartitionSpec as P

HEAD_DIM = 64


epsilon = 1e-05
neg_large = -1e30


def passed_along(array, axis, by):
    length = lax.axis_size(axis)
    return lax.ppermute(array, axis, [(i, (i + by) % length) for i in range(length)])


def from_behind(array, axis, by):
    length = lax.axis_size(axis)
    pairs = [(i, i + by) for i in range(length) if 0 <= i + by < length]
    return lax.ppermute(array, axis, pairs)


def normalize(values):
    center = values - jnp.mean(values, axis=-1, keepdims=True)
    inv_std = lax.rsqrt(jnp.mean(center * center, axis=-1, keepdims=True) + epsilon)
    return (center * inv_std, inv_std)


def norm_back(upstream, gain_row, normed, inv_std):
    scaled = upstream * gain_row
    return inv_std * (
        scaled
        - jnp.mean(scaled, axis=-1, keepdims=True)
        - normed * jnp.mean(scaled * normed, axis=-1, keepdims=True)
    )


def gelu_tanh(values):
    return jax.nn.gelu(values, approximate=True)


def gather_rows(values):
    return lax.all_gather(values, "tensor", axis=0, tiled=True)


def spread_rows(left, right, form):
    return lax.psum_scatter(
        jnp.einsum(form, left, right, preferred_element_type=jnp.float32).astype(jnp.bfloat16),
        "tensor",
        scatter_dimension=0,
        tiled=True,
    ).astype(jnp.float32)


def attend_piece(running, pieces, queries, query_pos):
    row_top, row_total, weighted = running
    key_rows = pieces[0].reshape(pieces[0].shape[0], -1, HEAD_DIM)
    value_rows = pieces[1].reshape(pieces[1].shape[0], -1, HEAD_DIM)
    scores = jnp.einsum(
        "bhe,phe->hbp", queries, key_rows, preferred_element_type=jnp.float32
    ) * HEAD_DIM ** (-0.5)
    key_pos = jnp.arange(key_rows.shape[0], dtype=jnp.int32)
    allowed = query_pos[None, :, None] >= key_pos[None, None, :]
    new_top = jnp.maximum(row_top, jnp.max(jnp.where(allowed, scores, neg_large), axis=-1))
    shares = jnp.where(allowed, jnp.exp(scores - new_top[..., None]), 0.0)
    row_total = jnp.sum(shares, axis=-1)
    weighted = jnp.einsum(
        "hbp,phe->hbe", shares.astype(jnp.bfloat16), value_rows, preferred_element_type=jnp.float32
    )
    return (new_top, row_total, weighted)


def grad_piece(queries, grad_heads, row_lse, row_delta, key_flat, value_flat, query_pos, first_key):
    key_rows = key_flat.reshape(key_flat.shape[0], -1, HEAD_DIM)
    value_rows = value_flat.reshape(value_flat.shape[0], -1, HEAD_DIM)
    score_scale = HEAD_DIM ** (-0.5)
    scores = (
        jnp.einsum("bhe,phe->hbp", queries, key_rows, preferred_element_type=jnp.float32)
        * score_scale
    )
    key_pos = first_key + jnp.arange(key_rows.shape[0], dtype=jnp.int32)
    allowed = query_pos[None, :, None] >= key_pos[None, None, :]
    shares = jnp.where(allowed, jnp.exp(scores - row_lse[..., None]), 0.0)
    grad_shares = jnp.einsum(
        "bhe,phe->hbp", grad_heads, value_rows, preferred_element_type=jnp.float32
    )
    grad_scores = (shares * (grad_shares - row_delta[..., None]) * score_scale).astype(jnp.bfloat16)
    query_add = jnp.einsum(
        "hbp,phe->bhe", grad_scores, key_rows, preferred_element_type=jnp.float32
    )
    key_add = jnp.einsum(
        "hbp,bhe->phe", grad_scores, queries, preferred_element_type=jnp.float32
    ).reshape(key_flat.shape)
    value_add = jnp.einsum(
        "hbp,bhe->phe", shares.astype(jnp.bfloat16), grad_heads, preferred_element_type=jnp.float32
    ).reshape(key_flat.shape)
    return (query_add, key_add, value_add)


def grad_or_nothing(
    needed, queries, grad_heads, row_lse, row_delta, key_flat, value_flat, query_pos, first_key
):

    def compute(operands):
        return grad_piece(
            queries, grad_heads, row_lse, row_delta, operands[0], operands[1], query_pos, first_key
        )

    def nothing(operands):
        return (
            jnp.zeros(queries.shape, jnp.float32),
            jnp.zeros(operands[0].shape, jnp.float32),
            jnp.zeros(operands[1].shape, jnp.float32),
        )

    return lax.cond(needed, compute, nothing, (key_flat, value_flat))


def per_device(tokens, cotangent, w_qkv, w_out, w_up, w_down, norm_gains):
    qkv_full, out_full, up_full, down_full, gain_full = (
        lax.all_gather(w_qkv, ("dp", "ctx"), axis=1, tiled=True),
        lax.all_gather(w_out, ("dp", "ctx"), axis=1, tiled=True),
        lax.all_gather(w_up, ("dp", "ctx"), axis=0, tiled=True),
        lax.all_gather(w_down, ("dp", "ctx"), axis=1, tiled=True),
        lax.all_gather(norm_gains, ("dp", "ctx"), axis=1, tiled=True),
    )
    gain_one = gain_full[0].astype(jnp.float32)
    gain_two = gain_full[1].astype(jnp.float32)
    inputs = tokens.astype(jnp.float32)
    normed_one, inv_one = normalize(inputs)
    first_in = gather_rows((normed_one * gain_one).astype(jnp.bfloat16))
    block_len = first_in.shape[0]
    width_local = qkv_full.shape[2]
    heads_local = width_local // HEAD_DIM
    projected = jnp.einsum(
        "bd,kdc->kbc", first_in, qkv_full, preferred_element_type=jnp.float32
    ).astype(jnp.bfloat16)
    queries = projected[0].reshape(block_len, heads_local, HEAD_DIM)
    ctx_pos = lax.axis_index("ctx")
    ctx_count = lax.axis_size("ctx")
    query_pos = ctx_pos * block_len + jnp.arange(block_len, dtype=jnp.int32)
    last_query = ctx_pos * block_len + block_len - 1
    start_state = (
        jnp.full((heads_local, block_len), neg_large, jnp.float32),
        jnp.zeros((heads_local, block_len), jnp.float32),
        jnp.zeros((heads_local, block_len, HEAD_DIM), jnp.float32),
    )
    pieces = (
        lax.all_gather(projected[1], "ctx", axis=0, tiled=True),
        lax.all_gather(projected[2], "ctx", axis=0, tiled=True),
    )
    row_top, row_total, weighted = lax.cond(
        jnp.int32(0) <= last_query,
        lambda state: attend_piece(state, pieces, queries, query_pos),
        lambda state: state,
        start_state,
    )
    row_lse = row_top + jnp.log(row_total)
    attended_heads = jnp.transpose(weighted / row_total[..., None], (1, 0, 2)).astype(jnp.bfloat16)
    attended = attended_heads.reshape(block_len, width_local)
    middle = inputs + spread_rows(attended, out_full, "bc,cd->bd")
    normed_two, inv_two = normalize(middle)
    second_in = gather_rows((normed_two * gain_two).astype(jnp.bfloat16))
    hidden = jnp.dot(second_in, up_full, preferred_element_type=jnp.float32)
    activated, gelu_pull = jax.vjp(gelu_tanh, hidden)
    act_low = activated.astype(jnp.bfloat16)
    result = (middle + spread_rows(act_low, down_full, "bf,fd->bd")).astype(jnp.bfloat16)
    qkv_back, out_back, up_back, down_back = (
        lax.all_gather(w_qkv, ("dp", "ctx"), axis=1, tiled=True),
        lax.all_gather(w_out, ("dp", "ctx"), axis=1, tiled=True),
        lax.all_gather(w_up, ("dp", "ctx"), axis=0, tiled=True),
        lax.all_gather(w_down, ("dp", "ctx"), axis=1, tiled=True),
    )
    grad_full = gather_rows(cotangent)
    grad_down = jnp.einsum("bf,bd->fd", act_low, grad_full, preferred_element_type=jnp.float32)
    grad_act = jnp.einsum("bd,fd->bf", grad_full, down_back, preferred_element_type=jnp.float32)
    grad_hidden = gelu_pull(grad_act)[0].astype(jnp.bfloat16)
    grad_up = jnp.einsum("bd,bf->df", second_in, grad_hidden, preferred_element_type=jnp.float32)
    grad_second = spread_rows(grad_hidden, up_back, "bf,df->bd")
    grad_middle = cotangent.astype(jnp.float32) + norm_back(
        grad_second, gain_two, normed_two, inv_two
    )
    gain_two_term = jnp.sum(grad_second * normed_two, axis=0)
    mid_full = gather_rows(grad_middle.astype(jnp.bfloat16))
    grad_outw = jnp.einsum("bc,bd->cd", attended, mid_full, preferred_element_type=jnp.float32)
    grad_heads = (
        jnp.einsum("bd,cd->bc", mid_full, out_back, preferred_element_type=jnp.float32)
        .astype(jnp.bfloat16)
        .reshape(block_len, heads_local, HEAD_DIM)
    )
    row_delta = jnp.einsum(
        "bhe,bhe->hb", grad_heads, attended_heads, preferred_element_type=jnp.float32
    )
    empty_query = jnp.zeros((block_len, heads_local, HEAD_DIM), jnp.float32)

    def cycle_turn(step_index, running):
        query_sum, key_now, value_now, key_grad, value_grad = running
        source = (ctx_pos - step_index) % ctx_count
        query_add, key_add, value_add = grad_or_nothing(
            source <= ctx_pos,
            queries,
            grad_heads,
            row_lse,
            row_delta,
            key_now,
            value_now,
            query_pos,
            source * block_len,
        )
        key_grad, value_grad = (
            passed_along((key_grad + key_add).astype(jnp.bfloat16), "ctx", 1).astype(jnp.float32),
            passed_along((value_grad + value_add).astype(jnp.bfloat16), "ctx", 1).astype(
                jnp.float32
            ),
        )
        key_now, value_now = from_behind((key_now, value_now), "ctx", 1)
        return (query_sum + query_add, key_now, value_now, key_grad, value_grad)

    empty_keys = jnp.zeros((block_len, width_local), jnp.float32)
    cycle_state = lax.fori_loop(
        0, ctx_count, cycle_turn, (empty_query, projected[1], projected[2], empty_keys, empty_keys)
    )
    query_sum, key_grad, value_grad = (cycle_state[0], cycle_state[3], cycle_state[4])
    grad_projected = jnp.stack(
        [query_sum.reshape(block_len, width_local), key_grad, value_grad], axis=1
    ).astype(jnp.bfloat16)
    grad_qkvw = jnp.einsum(
        "bd,bkc->kdc", first_in, grad_projected, preferred_element_type=jnp.float32
    )
    grad_first = spread_rows(grad_projected, qkv_back, "bkc,kdc->bd")
    grad_tokens = grad_middle + norm_back(grad_first, gain_one, normed_one, inv_one)
    gain_one_term = jnp.sum(grad_first * normed_one, axis=0)
    gain_terms = lax.psum(jnp.stack([gain_one_term, gain_two_term]), "tensor")
    grad_qkv, grad_out, grad_upw, grad_downw, grad_gains = (
        lax.psum_scatter(grad_qkvw, ("dp", "ctx"), scatter_dimension=1, tiled=True),
        lax.psum_scatter(grad_outw, ("dp", "ctx"), scatter_dimension=1, tiled=True),
        lax.psum_scatter(grad_up, ("dp", "ctx"), scatter_dimension=0, tiled=True),
        lax.psum_scatter(grad_down, ("dp", "ctx"), scatter_dimension=1, tiled=True),
        lax.psum_scatter(gain_terms, ("dp", "ctx"), scatter_dimension=1, tiled=True),
    )
    return (result, grad_tokens, grad_qkv, grad_out, grad_upw, grad_downw, grad_gains)


def solution(mesh):
    return jax.shard_map(
        per_device,
        mesh=mesh,
        in_specs=(
            P(("dp", "ctx", "tensor"), None),
            P(("dp", "ctx", "tensor"), None),
            P(None, ("dp", "ctx"), "tensor"),
            P("tensor", ("dp", "ctx")),
            P(("dp", "ctx"), "tensor"),
            P("tensor", ("dp", "ctx")),
            P(None, ("dp", "ctx")),
        ),
        out_specs=(
            P(("dp", "ctx", "tensor"), None),
            P(("dp", "ctx", "tensor"), None),
            P(None, ("dp", "ctx"), "tensor"),
            P("tensor", ("dp", "ctx")),
            P(("dp", "ctx"), "tensor"),
            P("tensor", ("dp", "ctx")),
            P(None, ("dp", "ctx")),
        ),
        check_vma=False,
    )
```

profile of v0, /device:TPU:1, one launch (start us, length us, event | category | flops | bytes accessed | tf_op | source)
XLA Modules:
  0.0 1402.0 jit_solution(4166377259606343943)
XLA Ops:
  8.7 83.8 %all-gather.2 = bf16[64,12,2]{1,2,0:T(2,128)(2,1)S(1)} all-gather(bf16[1,12,2]{1,2,0:T(2,128)(2,1)} %bitcast.117), channel_id=1, replica_groups=mesh['dp'=8,'ctx'=8,'tensor'=2] {'dp','ctx'}, dimensions={0}, use_global_device_ids=true | all-gather | bytes 3120 | tf_op jit(solution)/shard_map/all_gather | solution.py:126
  96.3 13.9 all_gather.38
  124.1 82.1 %all-gather.3 = bf16[64,12,384]{2,1,0:T(8,128)(2,1)S(1)} all-gather(bf16[1,12,384]{2,1,0:T(8,128)(2,1)S(1)} %bitcast.116), channel_id=1, replica_groups=mesh['dp'=8,'ctx'=8,'tensor'=2] {'dp','ctx'}, dimensions={0}, use_global_device_ids=true | all-gather | bytes 599040 | tf_op jit(solution)/shard_map/all_gather | solution.py:123
  207.1 69.8 %conditional.2 = (f32[6,512]{1,0:T(8,128)}, f32[6,512]{1,0:T(8,128)}, f32[6,512,64]{1,2,0:T(8,128)}, f32[6,512]{1,0:T(8,128)S(1)}) conditional(s32[]{:T(128)} %convert_element_type.133, () %tuple.53, (s32[]{:T(128)}, bf16[4096,384]{0,1:T(8,128)(2,1)}, bf16[512,6,64]{0,2,1:T(8,128)(2,1)S(1)}, bf16[4096,384]{0,1:T(8,128)(2,1)}, s32[512]{0:T(512)S(1)}) %tuple.124), branch_computations={%region_2.0_spmd, %region_3.6_spmd} | conditional | flops 3361732096 | bytes 166959136 | solution.py:153
  208.8 23.0 %select_reduce_fusion = (f32[6,512]{1,0:T(8,128)S(1)}, f32[6,512,4096]{2,1,0:T(8,128)}) fusion(pred[512,4096]{1,0:T(8,128)(4,1)S(1)} %iota_compare_fusion, bf16[512,6,64]{0,2,1:T(8,128)(2,1)S(1)} %get-tuple-element.317, bf16[4096,6,64]{0,2,1:T(8,128)(2,1)} %bitcast.107), kind=kOutput, calls=%fused_computation.2 | convolution fusion | flops 1648358400 | bytes 55980032 | tf_op jit(solution)/shard_map/cond/branch_1_fun/bhe,phe->hbp/dot_general | solution.py:60
  232.4 23.6 %fusion.6 = f32[6,512]{1,0:T(8,128)} fusion(f32[6,512,4096]{2,1,0:T(8,128)} %get-tuple-element.476, f32[6,512]{1,0:T(8,128)} %broadcast_maximum_fusion, pred[512,4096]{1,0:T(8,128)(4,1)S(1)} %iota_compare_fusion), kind=kLoop, calls=%fused_computation.4 | loop fusion | flops 50328576 | bytes 52453376 | tf_op jit(solution)/shard_map/cond/branch_1_fun/reduce_sum | solution.py:67
  256.7 20.2 %fusion.7 = f32[6,512,64]{1,2,0:T(8,128)} fusion(bf16[4096,6,64]{0,2,1:T(8,128)(2,1)} %bitcast.119, f32[6,512,4096]{2,1,0:T(8,128)} %get-tuple-element.476, f32[6,512]{1,0:T(8,128)} %broadcast_maximum_fusion, pred[512,4096]{1,0:T(8,128)(4,1)S(1)} %iota_compare_fusion), kind=kOutput, calls=%fused_computation.5 | convolution fusion | flops 1660944384 | bytes 56373248 | tf_op jit(solution)/shard_map/cond/branch_1_fun/hbp,phe->hbe/dot_general | solution.py:68
  281.0 13.5 all_gather.46
  299.6 93.2 %all-gather.18.cloned.1.call-done = bf16[64,12,1536]{2,1,0:T(8,128)(2,1)} async-done(((bf16[1,12,1536]{2,1,0:T(8,128)(2,1)}), bf16[64,12,1536]{2,1,0:T(8,128)(2,1)}) %all-gather.18.cloned.1.call-update) | async-done | bytes 2359312 | tf_op jit(solution)/shard_map/all_gather | solution.py:124
  402.6 13.4 reduce-scatter.12.cloned.1.call-done
  442.9 20.4 %reduce-scatter.16.cloned.1.call-done = bf16[256,768]{1,0:T(8,128)(2,1)} async-done(((bf16[512,768]{1,0:T(8,128)(2,1)}), bf16[256,768]{1,0:T(8,128)(2,1)}) %reduce-scatter.16.cloned.1.call-update) | async-done | bytes 393232 | tf_op jit(solution)/shard_map/reduce_scatter | solution.py:48
  466.1 12.2 all_gather.47
  482.5 274.3 %while.24 = (s32[]{:T(128)}, f32[512,6,64]{0,2,1:T(8,128)}, bf16[512,384]{0,1:T(8,128)(2,1)}, bf16[512,384]{0,1:T(8,128)(2,1)S(1)}, f32[512,384]{0,1:T(8,128)}, ...) while((s32[]{:T(128)}, f32[512,6,64]{0,2,1:T(8,128)}, ...), condition=%wide.region_16.17_spmd.clone, body=%wide.region_13.16_spmd.clone.sunk | while | flops 1026163712 | bytes 69796536 | solution.py:221
  484.2 12.8 conditional.5
  520.1 12.8 conditional.5
  559.2 14.9 %collective-permute-start.2 = (bf16[512,384]{0,1:T(8,128)(2,1)}, bf16[512,384]{0,1:T(8,128)(2,1)}, u32[]{:S(2)}, u32[]{:S(2)}) collective-permute-start(bf16[512,384]{0,1:T(8,128)(2,1)} %fusion.99), channel_id=1, source_target_pairs={{0,2},{2,4},{4,6},{6,8},{8,10},{10,12},{12,14},{14,0},{1,3},{3,5},... | collective-permute-start | bytes 1179656 | tf_op jit(solution)/shard_map/while/body/eval_jaxpr/ppermute | solution.py:15
  636.3 16.8 %collective-permute-start = (bf16[512,384]{0,1:T(8,128)(2,1)S(1)}, bf16[512,384]{0,1:T(8,128)(2,1)}, u32[]{:S(2)}, u32[]{:S(2)}) collective-permute-start(bf16[512,384]{0,1:T(8,128)(2,1)S(1)} %copy.71), channel_id=1, source_target_pairs={{0,2},{2,4},{4,6},{6,8},{8,10},{10,12},{12,14},{1,3},{3,5},{5,7},{... | collective-permute-start | bytes 1179656 | tf_op jit(solution)/shard_map/while/body/eval_jaxpr/ppermute | solution.py:21
  677.3 13.4 collective-permute-start.1
  724.2 14.9 %collective-permute-start.2 = (bf16[512,384]{0,1:T(8,128)(2,1)}, bf16[512,384]{0,1:T(8,128)(2,1)}, u32[]{:S(2)}, u32[]{:S(2)}) collective-permute-start(bf16[512,384]{0,1:T(8,128)(2,1)} %fusion.99), channel_id=1, source_target_pairs={{0,2},{2,4},{4,6},{6,8},{8,10},{10,12},{12,14},{14,0},{1,3},{3,5},... | collective-permute-start | bytes 1179656 | tf_op jit(solution)/shard_map/while/body/eval_jaxpr/ppermute | solution.py:15
  787.1 170.6 %fusion.62 = (f32[384,16]{0,1:T(8,128)S(1)}, f32[16,1536]{1,0:T(8,128)S(1)}, f32[1536,16]{0,1:T(8,128)S(1)}) fusion(f32[384,768]{0,1:T(8,128)S(1)} %fusion.67, f32[768,1536]{1,0:T(8,128)} %fusion.68, f32[1536,768]{0,1:T(8,128)} %fusion.61), kind=kCustom, calls=%all-reduce-scatter.3 | all-reduce-scatter fusion | flops 3538945 | bytes 10838528
  1083.2 16.0 %concatenate.2 = f32[1536,268]{0,1:T(8,128)S(1)} concatenate(f32[1536,12]{0,1:T(8,128)} %copy-done.23, f32[1536,16]{0,1:T(8,128)} %copy-done.40, f32[1536,16]{0,1:T(8,128)} %copy-done.38, f32[1536,16]{0,1:T(8,128)} %copy-done.36, f32[1536,16]{0,1:T(8,128)} %copy-done.35, f32[1536,16]{0,1:T(8,128)} %copy-done.34, f32[1536,16]{0,1:T(8,128)} %copy-done.33, f32[1536,16]{0,1:T(8,128)} %copy-done.32, ...), dimensions={1} | concatenate | bytes 3293184
  1099.3 26.5 %concatenate.1 = f32[268,1536]{1,0:T(8,128)} concatenate(f32[12,1536]{1,0:T(8,128)S(1)} %collective-permute-done.35, f32[16,1536]{1,0:T(8,128)} %collective-permute-done.34, f32[16,1536]{1,0:T(8,128)} %collective-permute-done.33, f32[16,1536]{1,0:T(8,128)} %collective-permute-done.32, f32[16,1536]{1,0:T(8,128)} %collective-permute-done.31, f32[16,1536]{1,0:T(8,128)} %collective-permute-done.30, ...), dimensions={0} | concatenate | bytes 3293184
  1129.6 140.5 %all-reduce.4 = f32[2,768]{1,0:T(2,128)S(1)} all-reduce(f32[2,768]{1,0:T(2,128)S(1)} %pad_maximum_fusion.3), channel_id=12, replica_groups=mesh['dp'=8,'ctx'=8,'tensor'=2] {'dp','ctx'}, use_global_device_ids=true, to_apply=%region_27.28.clone | all-reduce | flops 1536 | bytes 12288
  1279.2 114.3 %all-reduce.11.cloned.1.call-done = f32[3,768,384]{2,0,1:T(4,128)} async-done(((f32[3,768,384]{2,0,1:T(4,128)}), f32[3,768,384]{2,0,1:T(4,128)}) %all-reduce.11.cloned.1.call-update) | async-done | bytes 3538960
  (505 shorter events, 458.7 us)
Async XLA Ops:
  7.2 111.0 %all-gather.12.cloned.1.call-start = ((), (), s32[]{:S(2)}) async-start(), calls=%async_computation.4 | async-start | bytes 2396160 | tf_op jit(solution)/shard_map/all_gather | solution.py:122
  8.6 198.5 %all-gather.14.cloned.1.call-start = ((), (), s32[]{:S(2)}) async-start(), calls=%async_computation.9 | async-start | bytes 3538944 | tf_op jit(solution)/shard_map/all_gather | solution.py:150
  122.1 85.0 %all-gather.16.cloned.1.call-start = ((), (), s32[]{:S(2)}) async-start(), calls=%async_computation.10 | async-start | bytes 3538944 | tf_op jit(solution)/shard_map/all_gather | solution.py:151
  122.9 171.6 %all-gather.20.cloned.1.call-start = ((), (), s32[]{:S(2)}) async-start(), calls=%async_computation.12 | async-start | bytes 3194880 | tf_op jit(solution)/shard_map/all_gather | solution.py:125
  123.4 269.4 %all-gather.18.cloned.1.call-start = ((), (), s32[]{:S(2)}) async-start(), calls=%async_computation.11 | async-start | bytes 3194880 | tf_op jit(solution)/shard_map/all_gather | solution.py:124
  124.0 291.9 %reduce-scatter.12.cloned.1.call-start = ((), (), s32[]{:S(2)}) async-start(), calls=%async_computation.5 | async-start | bytes 1179648 | tf_op jit(solution)/shard_map/reduce_scatter | solution.py:48
  280.9 182.3 %reduce-scatter.16.cloned.1.call-start = ((), (), s32[]{:S(2)}) async-start(), calls=%async_computation.7 | async-start | bytes 1179648 | tf_op jit(solution)/shard_map/reduce_scatter | solution.py:48
  441.4 686.7 %reduce-scatter.18.cloned.1.call-start = ((), (), s32[]{:S(2)}) async-start(), calls=%async_computation.8 | async-start | bytes 1179648 | tf_op jit(solution)/shard_map/reduce_scatter | solution.py:48
  559.2 24.6 %collective-permute-start.2 = (bf16[512,384]{0,1:T(8,128)(2,1)}, bf16[512,384]{0,1:T(8,128)(2,1)}, u32[]{:S(2)}, u32[]{:S(2)}) collective-permute-start(bf16[512,384]{0,1:T(8,128)(2,1)} %fusion.99), channel_id=1, source_target_pairs={{0,2},{2,4},{4,6},{6,8},{8,10},{10,12},{12,14},{14,0},{1,3},{3,5},... | collective-permute-start | bytes 1179656 | tf_op jit(solution)/shard_map/while/body/eval_jaxpr/ppermute | solution.py:15
  595.9 24.6 %collective-permute-start.2 = (bf16[512,384]{0,1:T(8,128)(2,1)}, bf16[512,384]{0,1:T(8,128)(2,1)}, u32[]{:S(2)}, u32[]{:S(2)}) collective-permute-start(bf16[512,384]{0,1:T(8,128)(2,1)} %fusion.99), channel_id=1, source_target_pairs={{0,2},{2,4},{4,6},{6,8},{8,10},{10,12},{12,14},{14,0},{1,3},{3,5},... | collective-permute-start | bytes 1179656 | tf_op jit(solution)/shard_map/while/body/eval_jaxpr/ppermute | solution.py:15
  629.7 27.5 %collective-permute-start.2 = (bf16[512,384]{0,1:T(8,128)(2,1)}, bf16[512,384]{0,1:T(8,128)(2,1)}, u32[]{:S(2)}, u32[]{:S(2)}) collective-permute-start(bf16[512,384]{0,1:T(8,128)(2,1)} %fusion.99), channel_id=1, source_target_pairs={{0,2},{2,4},{4,6},{6,8},{8,10},{10,12},{12,14},{14,0},{1,3},{3,5},... | collective-permute-start | bytes 1179656 | tf_op jit(solution)/shard_map/while/body/eval_jaxpr/ppermute | solution.py:15
  634.2 25.1 %collective-permute-start.3 = (bf16[512,384]{0,1:T(8,128)(2,1)}, bf16[512,384]{0,1:T(8,128)(2,1)S(1)}, u32[]{:S(2)}, u32[]{:S(2)}) collective-permute-start(bf16[512,384]{0,1:T(8,128)(2,1)} %fusion.100), channel_id=1, source_target_pairs={{0,2},{2,4},{4,6},{6,8},{8,10},{10,12},{12,14},{14,0},{1,3},{3,5},... | collective-permute-start | bytes 1179656 | tf_op jit(solution)/shard_map/while/body/eval_jaxpr/ppermute | solution.py:15
  636.3 23.9 %collective-permute-start = (bf16[512,384]{0,1:T(8,128)(2,1)S(1)}, bf16[512,384]{0,1:T(8,128)(2,1)}, u32[]{:S(2)}, u32[]{:S(2)}) collective-permute-start(bf16[512,384]{0,1:T(8,128)(2,1)S(1)} %copy.71), channel_id=1, source_target_pairs={{0,2},{2,4},{4,6},{6,8},{8,10},{10,12},{12,14},{1,3},{3,5},{5,7},{... | collective-permute-start | bytes 1179656 | tf_op jit(solution)/shard_map/while/body/eval_jaxpr/ppermute | solution.py:21
  666.3 26.6 %collective-permute-start.2 = (bf16[512,384]{0,1:T(8,128)(2,1)}, bf16[512,384]{0,1:T(8,128)(2,1)}, u32[]{:S(2)}, u32[]{:S(2)}) collective-permute-start(bf16[512,384]{0,1:T(8,128)(2,1)} %fusion.99), channel_id=1, source_target_pairs={{0,2},{2,4},{4,6},{6,8},{8,10},{10,12},{12,14},{14,0},{1,3},{3,5},... | collective-permute-start | bytes 1179656 | tf_op jit(solution)/shard_map/while/body/eval_jaxpr/ppermute | solution.py:15
  670.7 24.2 %collective-permute-start.3 = (bf16[512,384]{0,1:T(8,128)(2,1)}, bf16[512,384]{0,1:T(8,128)(2,1)S(1)}, u32[]{:S(2)}, u32[]{:S(2)}) collective-permute-start(bf16[512,384]{0,1:T(8,128)(2,1)} %fusion.100), channel_id=1, source_target_pairs={{0,2},{2,4},{4,6},{6,8},{8,10},{10,12},{12,14},{14,0},{1,3},{3,5},... | collective-permute-start | bytes 1179656 | tf_op jit(solution)/shard_map/while/body/eval_jaxpr/ppermute | solution.py:15
  673.0 22.9 %collective-permute-start = (bf16[512,384]{0,1:T(8,128)(2,1)S(1)}, bf16[512,384]{0,1:T(8,128)(2,1)}, u32[]{:S(2)}, u32[]{:S(2)}) collective-permute-start(bf16[512,384]{0,1:T(8,128)(2,1)S(1)} %copy.71), channel_id=1, source_target_pairs={{0,2},{2,4},{4,6},{6,8},{8,10},{10,12},{12,14},{1,3},{3,5},{5,7},{... | collective-permute-start | bytes 1179656 | tf_op jit(solution)/shard_map/while/body/eval_jaxpr/ppermute | solution.py:21
  724.2 29.6 %collective-permute-start.2 = (bf16[512,384]{0,1:T(8,128)(2,1)}, bf16[512,384]{0,1:T(8,128)(2,1)}, u32[]{:S(2)}, u32[]{:S(2)}) collective-permute-start(bf16[512,384]{0,1:T(8,128)(2,1)} %fusion.99), channel_id=1, source_target_pairs={{0,2},{2,4},{4,6},{6,8},{8,10},{10,12},{12,14},{14,0},{1,3},{3,5},... | collective-permute-start | bytes 1179656 | tf_op jit(solution)/shard_map/while/body/eval_jaxpr/ppermute | solution.py:15
  763.8 512.6 %reduce-scatter.14.cloned.1.call-start = ((), (), s32[]{:S(2)}) async-start(), calls=%async_computation.6 | async-start | bytes 1179648 | tf_op jit(solution)/shard_map/reduce_scatter | solution.py:48
  769.5 623.9 %all-reduce.11.cloned.1.call-start = ((), (), s32[]{:S(2)}) async-start(), calls=%async_computation.13 | async-start | bytes 9437184
  984.5 29.8 %collective-permute-start.51 = (f32[1536,12]{0,1:T(8,128)S(1)}, f32[1536,12]{0,1:T(8,128)S(1)}, u32[]{:S(2)}, u32[]{:S(2)}) collective-permute-start(f32[1536,12]{0,1:T(8,128)S(1)} %slice.29), channel_id=1, source_target_pairs={{0,32},{2,34},{4,36},{6,38},{8,40},{10,42},{12,44},{14,46},{16,48}... | collective-permute-start | bytes 221192
  985.8 31.5 %collective-permute-start.35 = (f32[12,1536]{1,0:T(8,128)S(1)}, f32[12,1536]{1,0:T(8,128)S(1)}, u32[]{:S(2)}, u32[]{:S(2)}) collective-permute-start(f32[12,1536]{1,0:T(8,128)S(1)} %slice.28), channel_id=1, source_target_pairs={{0,32},{2,34},{4,36},{6,38},{8,40},{10,42},{12,44},{14,46},{16,48}... | collective-permute-start | bytes 221192
  1070.9 28.4 %collective-permute-start.30 = (f32[16,1536]{1,0:T(8,128)S(1)}, f32[16,1536]{1,0:T(8,128)}, u32[]{:S(2)}, u32[]{:S(2)}) collective-permute-start(f32[16,1536]{1,0:T(8,128)S(1)} %get-tuple-element.473), channel_id=1, source_target_pairs={{0,22},{2,24},{4,26},{6,28},{8,30},{10,32},{12,34},{14,36},{16,38}... | collective-permute-start | bytes 294920
  1074.4 24.8 %collective-permute-start.31 = (f32[16,1536]{1,0:T(8,128)S(1)}, f32[16,1536]{1,0:T(8,128)}, u32[]{:S(2)}, u32[]{:S(2)}) collective-permute-start(f32[16,1536]{1,0:T(8,128)S(1)} %get-tuple-element.473), channel_id=1, source_target_pairs={{0,24},{2,26},{4,28},{6,30},{8,32},{10,34},{12,36},{14,38},{16,40}... | collective-permute-start | bytes 294920
  1076.4 22.9 %collective-permute-start.32 = (f32[16,1536]{1,0:T(8,128)S(1)}, f32[16,1536]{1,0:T(8,128)}, u32[]{:S(2)}, u32[]{:S(2)}) collective-permute-start(f32[16,1536]{1,0:T(8,128)S(1)} %get-tuple-element.473), channel_id=1, source_target_pairs={{0,26},{2,28},{4,30},{6,32},{8,34},{10,36},{12,38},{14,40},{16,42}... | collective-permute-start | bytes 294920
  (141 other events, 3504.0 us)
Sparse Core Ops, SparseCore 0:
  10.3 107.8 all-gather.11
  122.3 27.8 all-gather.13
  152.4 28.5 all-gather.15
  182.5 104.8 all-gather.19
  289.0 103.8 all-gather.17
  395.6 20.2 reduce-scatter.11
  441.5 21.6 reduce-scatter.15
  764.0 27.2 reduce-scatter.17
  793.7 30.2 reduce-scatter.13
  826.4 567.0 all-reduce.10
where the time goes:
time: 1410 us; the launch traced here: 1400 us
  blocking collectives  535 us (38%)
  waiting for transfers between devices  273 us (19%)
  starting transfers between devices  260 us (18%)
  other arithmetic  118 us (8%)
  matrix products  109 us (8%)
  local copies, waits for them, and re-layouts  90.5 us (6%)
  between operations  17.2 us (1%)
    unnamed x2, blocking collectives  311 us
    unnamed x49, starting transfers between devices  119 us
    unnamed x59, waiting for transfers between devices  116 us
    all_gather x1, waiting for transfers between devices, per_device(): lax.all_gather(w_up, ('dp', 'ctx'), axis=0, tiled=True)  93.2 us
    all_gather x1, blocking collectives, per_device(): lax.all_gather(norm_gains, ('dp', 'ctx'), axis=1, tiled=True)  83.8 us
    all_gather x1, blocking collectives, per_device(): lax.all_gather(w_out, ('dp', 'ctx'), axis=1, tiled=True)  82.1 us
    ppermute x16, starting transfers between devices, from_behind(): return lax.ppermute(array, axis, pairs)  75.7 us
    ppermute x16, starting transfers between devices, passed_along(): lax.ppermute(array, axis, [(i, (i + by) % length) for i in range(length)])  64.7 us
  transfers between devices with their start and end apart: 90, of which 13 were waited for; matrix products, arithmetic and copies ran while one was open for 28% of the time, Pallas kernels for 0%

commit v1 on v0

v1 whole, which is shorter than its diff:
```python
import functools

import jax
import jax.numpy as jnp
import numpy as np
from jax import lax
from jax.experimental import pallas as pl
from jax.experimental.pallas import tpu as pltpu
from jax.sharding import PartitionSpec as P

HEAD_DIM = 64
HEADS = 12
MEMBERS = 16
ROWS = 12
WIDTH = 384
SLOT = 4 * ROWS
ORDERS = (("z", "x", "y"), ("x", "y", "z"), ("y", "z", "x"))
MESH = pl.DeviceIdType.MESH
VMEM_BYTES = 60 * 1024 * 1024
epsilon = 1e-05
neg_large = -1e30


def place():
    dp, ctx, tensor = lax.axis_index("dp"), lax.axis_index("ctx"), lax.axis_index("tensor")
    return dict(x=dp // 2, y=ctx // 2, z=2 * tensor + dp % 2, c=ctx % 2)


def device_at(pos, axis, index):
    at = dict(pos)
    at[axis] = index
    return (at["x"] * 2 + at["z"] % 2, at["y"] * 2 + at["c"], at["z"] // 2)


def beside(pos, axis, by):
    if axis == "c":
        return device_at(pos, "c", 1 - pos["c"])
    return device_at(pos, axis, (pos[axis] + by) % 4)


def greet_axes(pos):
    barrier = pltpu.get_barrier_semaphore()
    for axis in ("x", "y", "z"):
        for by in (1, 2, 3):
            pl.semaphore_signal(
                barrier, inc=1, device_id=beside(pos, axis, by), device_id_type=MESH
            )
    pl.semaphore_signal(barrier, inc=1, device_id=beside(pos, "c", 1), device_id_type=MESH)
    pl.semaphore_wait(barrier, 10)


def remote(src, dst, send, recv, device):
    return pltpu.make_async_remote_copy(
        src_ref=src,
        dst_ref=dst,
        send_sem=send,
        recv_sem=recv,
        device_id=device,
        device_id_type=MESH,
    )


class SmallSum:
    def __init__(self, pos, ring, pair, send, recv):
        self.pos, self.ring, self.pair, self.send, self.recv = pos, ring, pair, send, recv

    def copy(self, n, by, coming=False):
        axis = ("x", "y", "z")[n]
        slot = (self.pos[axis] + 4 - by) % 4 if coming else self.pos[axis]
        ref, sem = self.ring.at[n, slot], n * 3 + by - 1
        return remote(
            ref, ref, self.send.at[sem], self.recv.at[sem], beside(self.pos, axis, by)
        )

    def start(self, n, value):
        self.ring[n, self.pos[("x", "y", "z")[n]]] = value
        for by in (1, 2, 3):
            self.copy(n, by).start()

    def finish(self, n):
        for by in (1, 2, 3):
            self.copy(n, by, coming=True).wait_recv()
            self.copy(n, by).wait_send()
        return (self.ring[n, 0] + self.ring[n, 1]) + (self.ring[n, 2] + self.ring[n, 3])

    def pair_copy(self, slot):
        ref = self.pair.at[slot]
        return remote(ref, ref, self.send.at[9], self.recv.at[9], beside(self.pos, "c", 1))

    def start_pair(self, value):
        self.pair[self.pos["c"]] = value
        self.pair_copy(self.pos["c"]).start()

    def finish_pair(self):
        self.pair_copy(1 - self.pos["c"]).wait_recv()
        self.pair_copy(self.pos["c"]).wait_send()
        return self.pair[0] + self.pair[1]


def half_of(stage, which):
    if stage == 0:
        return pl.ds(0, 32) if which == 0 else pl.ds(32, 16)
    return pl.ds(2 * which, 2)


def block_at(pos, order, stage, index):
    if stage == 2:
        return (pos["c"], index)
    if stage == 1:
        return (pos["c"], pos[order[2]], index)
    return (pos["c"], pos[order[2]], pos[order[1]], index)


def group_slots(k, group, tensor):
    x, z_lo, y_pair = group // 4, (group // 2) % 2, group % 2
    found = []
    for member in range(4):
        at = dict(x=x, z=2 * tensor + z_lo, y=2 * y_pair + member // 2)
        order = ORDERS[k]
        found.append((member % 2, at[order[2]], at[order[1]], at[order[0]]))
    return found


def column_of(k, tensor, piece):
    if k == 0:
        return (0, (piece * 2 + tensor) * WIDTH) if piece < 3 else (1, tensor * WIDTH)
    return (k + 1, (tensor * 4 + piece) * WIDTH)


def gather_kernel(
    a, b, c, gain, shuffle, w_qkv, w_out, w_up, w_down, gain_out,
    g0, g1, g2, ring, pair, send, recv, small_send, small_recv,
):
    pos = place()
    kept = (g0, g1, g2)
    for k, shard in enumerate((a, b, c)):
        order = ORDERS[k]
        kept[k][block_at(pos, order, 0, pos[order[0]])] = shard[...]
    small = SmallSum(pos, ring, pair, small_send, small_recv)
    greet_axes(pos)
    started = []

    def move(k, index, sem, device):
        ref = kept[k].at[index]
        copy = remote(ref, ref, send.at[sem], recv.at[sem], device)
        copy.start()
        started.append(copy)

    def arrived(k, index, sem):
        ref = kept[k].at[index]
        remote(ref, ref, send.at[sem], recv.at[sem], beside(pos, "c", 1)).wait_recv()

    def share(k, by, sem):
        move(
            k, (pos["c"], (pos[ORDERS[k][2]] + by) % 4), 36 + k * 4 + sem, beside(pos, "c", 1)
        )

    small_value = gain[...]
    for stage in range(3):
        small.start(stage, small_value)
        for k in range(3):
            order, base = ORDERS[k], (k * 3 + stage) * 4
            axis = order[stage]
            own = block_at(pos, order, stage, pos[axis])
            move(k, own, base, beside(pos, axis, 1))
            move(k, own, base + 1, beside(pos, axis, 3))
            if stage == 2:
                share(k, 0, 0)
        for k in range(3):
            order, base = ORDERS[k], (k * 3 + stage) * 4
            axis = order[stage]
            behind = block_at(pos, order, stage, (pos[axis] + 3) % 4)
            ahead = block_at(pos, order, stage, (pos[axis] + 1) % 4)
            arrived(k, behind, base)
            move(k, behind + (half_of(stage, 0),), base + 2, beside(pos, axis, 1))
            if stage == 2:
                share(k, 3, 1)
            arrived(k, ahead, base + 1)
            move(k, ahead + (half_of(stage, 1),), base + 3, beside(pos, axis, 3))
            if stage == 2:
                share(k, 1, 2)
        for k in range(3):
            order, base = ORDERS[k], (k * 3 + stage) * 4
            axis = order[stage]
            across = block_at(pos, order, stage, (pos[axis] + 2) % 4)
            arrived(k, across + (half_of(stage, 0),), base + 2)
            arrived(k, across + (half_of(stage, 1),), base + 3)
            if stage == 2:
                share(k, 2, 3)
        small_value = small.finish(stage)
    small.start_pair(small_value)
    for k in range(3):
        for by, sem in ((0, 0), (3, 1), (1, 2), (2, 3)):
            arrived(k, (1 - pos["c"], (pos[ORDERS[k][2]] + by) % 4), 36 + k * 4 + sem)
    gain_out[...] = small.finish_pair()
    for copy in started:
        copy.wait_send()
    whole = (w_qkv, w_out, w_up, w_down)

    def unpack(group, carry):
        rows = pl.ds(pl.multiple_of(group * SLOT, SLOT), SLOT)
        for k in range(3):
            for tensor in range(2):
                held = jnp.concatenate(
                    [kept[k][index] for index in group_slots(k, group, tensor)], axis=0
                )
                sorted_rows = jnp.dot(
                    shuffle[...], held, preferred_element_type=jnp.float32
                ).astype(jnp.bfloat16)
                for piece in range(4):
                    which, column = column_of(k, tensor, piece)
                    whole[which][rows, pl.ds(column, WIDTH)] = sorted_rows[
                        piece * SLOT : (piece + 1) * SLOT
                    ]
        return carry

    lax.fori_loop(0, 16, unpack, 0)


def reduce_kernel(
    w_qkv, w_out, w_up, w_down, gain, shuffle, out_a, out_b, out_c, gain_out,
    r0, r1, r2, cores, halves3, fulls3, halves2, fulls2, half1a, half1b, fulls1,
    ring, pair, send, recv, small_send, small_recv,
):
    pos = place()
    kept = (r0, r1, r2)
    whole = (w_qkv, w_out, w_up, w_down)
    outs = (out_a, out_b, out_c)
    small = SmallSum(pos, ring, pair, small_send, small_recv)
    sibling = beside(pos, "c", 1)
    mine, other = pos["c"], 1 - pos["c"]

    def pack(group, carry):
        rows = pl.ds(pl.multiple_of(group * SLOT, SLOT), SLOT)
        for k in range(3):
            for tensor in range(2):
                held = jnp.concatenate(
                    [
                        whole[which][rows, pl.ds(column, WIDTH)]
                        for which, column in (column_of(k, tensor, piece) for piece in range(4))
                    ],
                    axis=0,
                )
                sorted_rows = jnp.dot(
                    shuffle[...], held, preferred_element_type=jnp.float32
                ).astype(jnp.bfloat16)
                for member, index in enumerate(group_slots(k, group, tensor)):
                    kept[k][index] = sorted_rows[member * SLOT : (member + 1) * SLOT]
        return carry

    lax.fori_loop(0, 16, pack, 0)
    greet_axes(pos)
    started = []

    def move(src, dst, sem, device):
        copy = remote(src, dst, send.at[sem], recv.at[sem], device)
        copy.start()
        started.append(copy)

    def arrived(dst, sem):
        remote(dst, dst, send.at[sem], recv.at[sem], sibling).wait_recv()

    def wide(value):
        return value.astype(jnp.float32)

    def add(target, index, sources, count):
        def body(i, carry):
            slot = (i // 4, i % 4) if count == 16 else (i,)
            total = wide(target[index + slot])
            for source, at in sources:
                total = total + wide(source[at + slot])
            target[index + slot] = total.astype(jnp.bfloat16)
            return carry

        lax.fori_loop(0, count, body, 0)

    small.start(0, gain[...])
    for by, sem in ((2, 0), (1, 1), (3, 2), (0, 3)):
        for k in range(3):
            index = (pos[ORDERS[k][2]] + by) % 4
            move(kept[k].at[other, index], cores.at[k, index], 36 + k * 4 + sem, sibling)

    def take_core(k, by, sem):
        index = (pos[ORDERS[k][2]] + by) % 4
        arrived(cores.at[k, index], 36 + k * 4 + sem)
        add(kept[k], (mine, index), [(cores, (k, index))], 16)

    for k in range(3):
        axis, base = ORDERS[k][2], k * 12
        across = (pos[axis] + 2) % 4
        take_core(k, 2, 0)
        move(
            kept[k].at[mine, across, pl.ds(0, 2)], halves3.at[k, 0], base, beside(pos, axis, 1)
        )
        move(
            kept[k].at[mine, across, pl.ds(2, 2)], halves3.at[k, 1], base + 1, beside(pos, axis, 3)
        )
    for k in range(3):
        take_core(k, 1, 1)
        take_core(k, 3, 2)
    for k in range(3):
        axis, base = ORDERS[k][2], k * 12
        for side, by in ((0, 1), (1, 3)):
            index = (pos[axis] + by) % 4
            arrived(halves3.at[k, side], base + side)

            def body(i, carry, k=k, side=side, index=index):
                a2, a1 = i // 4, i % 4
                at = (mine, index, 2 * side + a2, a1)
                kept[k][at] = (
                    wide(kept[k][at]) + wide(halves3[k, side, a2, a1])
                ).astype(jnp.bfloat16)
                return carry

            lax.fori_loop(0, 8, body, 0)
            move(
                kept[k].at[mine, index], fulls3.at[k, side], base + 2 + side, beside(pos, axis, by)
            )
    small_value = small.finish(0)
    small.start(1, small_value)
    for k in range(3):
        take_core(k, 0, 3)
    for k in range(3):
        axis3, axis, base = ORDERS[k][2], ORDERS[k][1], k * 12
        for side in range(2):
            arrived(fulls3.at[k, side], base + 2 + side)
        add(kept[k], (mine, pos[axis3]), [(fulls3, (k, 0)), (fulls3, (k, 1))], 16)
        across = (pos[axis] + 2) % 4
        for side, by in ((0, 1), (1, 3)):
            move(
                kept[k].at[mine, pos[axis3], across, pl.ds(2 * side, 2)],
                halves2.at[k, side],
                base + 4 + side,
                beside(pos, axis, by),
            )
    for k in range(3):
        axis3, axis, base = ORDERS[k][2], ORDERS[k][1], k * 12
        for side, by in ((0, 1), (1, 3)):
            index = (pos[axis] + by) % 4
            arrived(halves2.at[k, side], base + 4 + side)
            for a1 in range(2):
                at = (mine, pos[axis3], index, 2 * side + a1)
                kept[k][at] = (wide(kept[k][at]) + wide(halves2[k, side, a1])).astype(
                    jnp.bfloat16
                )
            move(
                kept[k].at[mine, pos[axis3], index],
                fulls2.at[k, side],
                base + 6 + side,
                beside(pos, axis, by),
            )
    small_value = small.finish(1)
    small.start(2, small_value)
    for k in range(3):
        axis3, axis2, axis, base = ORDERS[k][2], ORDERS[k][1], ORDERS[k][0], k * 12
        for side in range(2):
            arrived(fulls2.at[k, side], base + 6 + side)
        add(kept[k], (mine, pos[axis3], pos[axis2]), [(fulls2, (k, 0)), (fulls2, (k, 1))], 4)
        lead = (mine, pos[axis3], pos[axis2])
        across = (pos[axis] + 2) % 4
        move(
            kept[k].at[lead + (across, pl.ds(0, 32))], half1a.at[k], base + 8, beside(pos, axis, 1)
        )
        move(
            kept[k].at[lead + (across, pl.ds(32, 16))], half1b.at[k], base + 9, beside(pos, axis, 3)
        )
    for k in range(3):
        axis3, axis2, axis, base = ORDERS[k][2], ORDERS[k][1], ORDERS[k][0], k * 12
        lead = (mine, pos[axis3], pos[axis2])
        ahead, behind = lead + ((pos[axis] + 1) % 4,), lead + ((pos[axis] + 3) % 4,)
        arrived(half1a.at[k], base + 8)
        at = ahead + (pl.ds(0, 32),)
        kept[k][at] = (wide(kept[k][at]) + wide(half1a[k])).astype(jnp.bfloat16)
        move(kept[k].at[ahead], fulls1.at[k, 0], base + 10, beside(pos, axis, 1))
        arrived(half1b.at[k], base + 9)
        at = behind + (pl.ds(32, 16),)
        kept[k][at] = (wide(kept[k][at]) + wide(half1b[k])).astype(jnp.bfloat16)
        move(kept[k].at[behind], fulls1.at[k, 1], base + 11, beside(pos, axis, 3))
    small_value = small.finish(2)
    small.start_pair(small_value)
    for k in range(3):
        axis3, axis2, axis, base = ORDERS[k][2], ORDERS[k][1], ORDERS[k][0], k * 12
        for side in range(2):
            arrived(fulls1.at[k, side], base + 10 + side)
        outs[k][...] = (
            wide(kept[k][mine, pos[axis3], pos[axis2], pos[axis]])
            + wide(fulls1[k, 0])
            + wide(fulls1[k, 1])
        )
    gain_out[...] = small.finish_pair()
    for copy in started:
        copy.wait_send()


def shuffle_matrix():
    matrix = np.zeros((4 * SLOT, 4 * SLOT), np.float32)
    for piece in range(4):
        for member in range(4):
            for row in range(ROWS):
                matrix[piece * SLOT + member * ROWS + row, member * SLOT + piece * ROWS + row] = 1
    return matrix


def vmem_specs(count):
    return [pl.BlockSpec(memory_space=pltpu.VMEM)] * count


SMALL_SCRATCH = [
    pltpu.VMEM((3, 4, 8, 768), jnp.float32),
    pltpu.VMEM((2, 8, 768), jnp.float32),
]
BIG_SEMS = [pltpu.SemaphoreType.DMA((48,))] * 2
SMALL_SEMS = [pltpu.SemaphoreType.DMA((10,))] * 2
BUFFER = (2, 4, 4, 4, SLOT, WIDTH)


def gather_weights(shards, gain):
    low = jnp.bfloat16
    return pl.pallas_call(
        gather_kernel,
        name="gather_weights",
        out_shape=[
            jax.ShapeDtypeStruct((768, 2304), low),
            jax.ShapeDtypeStruct((768, 768), low),
            jax.ShapeDtypeStruct((768, 3072), low),
            jax.ShapeDtypeStruct((768, 3072), low),
            jax.ShapeDtypeStruct((8, 768), jnp.float32),
        ],
        in_specs=vmem_specs(5),
        out_specs=vmem_specs(5),
        scratch_shapes=[pltpu.VMEM(BUFFER, low)] * 3 + SMALL_SCRATCH + BIG_SEMS + SMALL_SEMS,
        compiler_params=pltpu.CompilerParams(
            collective_id=0, has_side_effects=True, vmem_limit_bytes=VMEM_BYTES
        ),
    )(*shards, gain, jnp.asarray(shuffle_matrix(), low))


def reduce_gradients(grads, gain):
    low = jnp.bfloat16
    return pl.pallas_call(
        reduce_kernel,
        name="reduce_gradients",
        out_shape=[jax.ShapeDtypeStruct((SLOT, WIDTH), jnp.float32)] * 3
        + [jax.ShapeDtypeStruct((8, 768), jnp.float32)],
        in_specs=vmem_specs(6),
        out_specs=vmem_specs(4),
        scratch_shapes=[pltpu.VMEM(BUFFER, low)] * 3
        + [
            pltpu.VMEM((3, 4, 4, 4, SLOT, WIDTH), low),
            pltpu.VMEM((3, 2, 2, 4, SLOT, WIDTH), low),
            pltpu.VMEM((3, 2, 4, 4, SLOT, WIDTH), low),
            pltpu.VMEM((3, 2, 2, SLOT, WIDTH), low),
            pltpu.VMEM((3, 2, 4, SLOT, WIDTH), low),
            pltpu.VMEM((3, 32, WIDTH), low),
            pltpu.VMEM((3, 16, WIDTH), low),
            pltpu.VMEM((3, 2, SLOT, WIDTH), low),
        ]
        + SMALL_SCRATCH
        + BIG_SEMS
        + SMALL_SEMS,
        compiler_params=pltpu.CompilerParams(
            collective_id=1, has_side_effects=True, vmem_limit_bytes=VMEM_BYTES
        ),
    )(*grads, gain, jnp.asarray(shuffle_matrix().T, low))


def head_place(head):
    member = head % 6
    return (member * 2) % 8 + (member // 4) * (1 + (member % 4) * 2), head // 6


def own_head(ctx, tensor):
    core, y = ctx % 2, ctx // 2
    return tensor * 6 + (1 - core) * y + core * (4 + y // 2), core * (y % 2) == 0


def greet_sequence(dp, number):
    barrier = pltpu.get_barrier_semaphore()

    def signal(i, carry):
        to = (number + i) % MEMBERS
        pl.semaphore_signal(
            barrier, inc=1, device_id=(dp, to // 2, to % 2), device_id_type=MESH
        )
        return carry

    lax.fori_loop(1, MEMBERS, signal, 0)
    pl.semaphore_wait(barrier, MEMBERS - 1)


def to_heads_kernel(src, dst, send, recv):
    dp, ctx, tensor = lax.axis_index("dp"), lax.axis_index("ctx"), lax.axis_index("tensor")
    number = 2 * ctx + tensor
    head, active = own_head(ctx, tensor)
    greet_sequence(dp, number)

    def out(i):
        to_head = (number + i) % HEADS
        to_ctx, to_tensor = head_place(to_head)
        local = 2 * to_ctx + to_tensor == number
        return local, to_head, (dp, to_ctx, to_tensor)

    def start(i, carry):
        local, to_head, device = out(i)

        @pl.when(local)
        def _():
            pltpu.make_async_copy(src.at[:, to_head], dst.at[number], recv.at[number]).start()

        @pl.when(jnp.logical_not(local))
        def _():
            remote(
                src.at[:, to_head], dst.at[number], send.at[to_head], recv.at[number], device
            ).start()

        return carry

    lax.fori_loop(0, HEADS, start, 0)

    @pl.when(active)
    def _():
        def wait(i, carry):
            @pl.when(i == number)
            def _():
                pltpu.make_async_copy(src.at[:, 0], dst.at[i], recv.at[i]).wait()

            @pl.when(i != number)
            def _():
                remote(
                    src.at[:, 0], dst.at[i], send.at[0], recv.at[i], (dp, i // 2, i % 2)
                ).wait_recv()

            return carry

        lax.fori_loop(0, MEMBERS, wait, 0)

    def sent(i, carry):
        local, to_head, device = out(i)

        @pl.when(jnp.logical_not(local))
        def _():
            remote(
                src.at[:, to_head], dst.at[number], send.at[to_head], recv.at[number], device
            ).wait_send()

        return carry

    lax.fori_loop(0, HEADS, sent, 0)


def from_heads_kernel(src, dst, send, recv):
    dp, ctx, tensor = lax.axis_index("dp"), lax.axis_index("ctx"), lax.axis_index("tensor")
    number = 2 * ctx + tensor
    head, active = own_head(ctx, tensor)
    greet_sequence(dp, number)

    @pl.when(active)
    def _():
        pltpu.make_async_copy(src.at[number], dst.at[:, head], recv.at[head]).start()

        def start(i, carry):
            to = (number + i) % MEMBERS
            remote(
                src.at[to], dst.at[:, head], send.at[to], recv.at[head], (dp, to // 2, to % 2)
            ).start()
            return carry

        lax.fori_loop(1, MEMBERS, start, 0)

    def wait(i, carry):
        from_ctx, from_tensor = head_place(i)
        local = 2 * from_ctx + from_tensor == number

        @pl.when(local)
        def _():
            pltpu.make_async_copy(src.at[0], dst.at[:, i], recv.at[i]).wait()

        @pl.when(jnp.logical_not(local))
        def _():
            remote(
                src.at[0], dst.at[:, i], send.at[0], recv.at[i], (dp, from_ctx, from_tensor)
            ).wait_recv()

        return carry

    lax.fori_loop(0, HEADS, wait, 0)

    @pl.when(active)
    def _():
        def sent(i, carry):
            to = (number + i) % MEMBERS
            remote(
                src.at[to], dst.at[:, head], send.at[to], recv.at[head], (dp, to // 2, to % 2)
            ).wait_send()
            return carry

        lax.fori_loop(1, MEMBERS, sent, 0)


def exchange(kernel, array, shape, name, number):
    return pl.pallas_call(
        kernel,
        name=name,
        out_shape=jax.ShapeDtypeStruct(shape, jnp.bfloat16),
        in_specs=[pl.BlockSpec(memory_space=pl.ANY)],
        out_specs=pl.BlockSpec(memory_space=pl.ANY),
        scratch_shapes=[pltpu.SemaphoreType.DMA((MEMBERS,))] * 2,
        compiler_params=pltpu.CompilerParams(collective_id=number, has_side_effects=True),
    )(array)


def to_heads(array, name, number):
    return exchange(
        to_heads_kernel, array, (MEMBERS, array.shape[0], HEAD_DIM, 256), name, number
    )


def from_heads(array, name, number):
    return exchange(
        from_heads_kernel, array, (array.shape[1], HEADS, HEAD_DIM, 256), name, number
    )


TILE = 512
TILES = 8


def turned(value):
    return jnp.transpose(value.astype(jnp.float32)).astype(jnp.bfloat16)


def allowed_tile():
    key = lax.broadcasted_iota(jnp.int32, (TILE, TILE), 0)
    query = lax.broadcasted_iota(jnp.int32, (TILE, TILE), 1)
    return query >= key


def two(ref, tile, *index):
    return jnp.concatenate([ref[(2 * tile,) + index], ref[(2 * tile + 1,) + index]], axis=1)


def dot(a, b):
    return jnp.dot(a, b, preferred_element_type=jnp.float32)


def dot_right(a, b):
    return lax.dot_general(a, b, (((1,), (1,)), ((), ())), preferred_element_type=jnp.float32)


def forward_kernel(parts, out, lse, keys):
    head, active = own_head(lax.axis_index("ctx"), lax.axis_index("tensor"))

    @pl.when(active)
    def _():
        def prepare(j, carry):
            keys[pl.ds(pl.multiple_of(j * TILE, TILE), TILE), :] = turned(two(parts, j, 1))
            return carry

        lax.fori_loop(0, TILES, prepare, 0)

        def tile_scores(j, query):
            return dot(keys[pl.ds(pl.multiple_of(j * TILE, TILE), TILE), :], query)

        def per_queries(i, carry):
            query = two(parts, i, 0) * jnp.bfloat16(HEAD_DIM ** -0.5)

            def step(scores, j, state):
                top, total, weighted = state
                new_top = jnp.maximum(top, jnp.max(scores, axis=0, keepdims=True))
                fade = jnp.exp(top - new_top)
                raised = jnp.exp(scores - new_top)
                total = total * fade + jnp.sum(raised, axis=0, keepdims=True)
                weighted = weighted * fade + dot(two(parts, j, 2), raised.astype(jnp.bfloat16))
                return new_top, total, weighted

            state = (
                jnp.full((1, TILE), neg_large, jnp.float32),
                jnp.zeros((1, TILE), jnp.float32),
                jnp.zeros((HEAD_DIM, TILE), jnp.float32),
            )
            state = lax.fori_loop(
                0, i, lambda j, state: step(tile_scores(j, query), j, state), state
            )
            masked = jnp.where(allowed_tile(), tile_scores(i, query), neg_large)
            top, total, weighted = step(masked, i, state)
            attended = (weighted / total).astype(jnp.bfloat16)
            out[2 * i, 0] = attended[:, :256]
            out[2 * i + 1, 0] = attended[:, 256:]
            lse[i] = top + jnp.log(total)
            return carry

        lax.fori_loop(0, TILES, per_queries, 0)


def backward_kernel(parts, attended, grad_att, lse, out, query_sum, delta):
    head, active = own_head(lax.axis_index("ctx"), lax.axis_index("tensor"))

    @pl.when(active)
    def _():
        def prepare(i, carry):
            delta[i] = jnp.sum(
                two(attended, i, 0).astype(jnp.float32) * two(grad_att, i, 0).astype(jnp.float32),
                axis=0,
                keepdims=True,
            )
            query_sum[i] = jnp.zeros((HEAD_DIM, TILE), jnp.float32)
            return carry

        lax.fori_loop(0, TILES, prepare, 0)

        def per_keys(j, carry):
            key_cols, value_cols = two(parts, j, 1), two(parts, j, 2)
            key_rows, value_rows = turned(key_cols), turned(value_cols)

            def step(i, state, diagonal):
                key_sum, value_sum = state
                query = two(parts, i, 0) * jnp.bfloat16(HEAD_DIM ** -0.5)
                grad = two(grad_att, i, 0)
                shares = jnp.exp(dot(key_rows, query) - lse[i])
                if diagonal:
                    shares = jnp.where(allowed_tile(), shares, 0.0)
                grad_scores = (shares * (dot(value_rows, grad) - delta[i])).astype(jnp.bfloat16)
                query_sum[i] += dot(key_cols, grad_scores)
                key_sum = key_sum + dot_right(query, grad_scores)
                value_sum = value_sum + dot_right(grad, shares.astype(jnp.bfloat16))
                return key_sum, value_sum

            zero = jnp.zeros((HEAD_DIM, TILE), jnp.float32)
            state = step(j, (zero, zero), True)
            key_sum, value_sum = lax.fori_loop(
                j + 1, TILES, lambda i, state: step(i, state, False), state
            )
            for part, total in ((1, key_sum), (2, value_sum)):
                total = total.astype(jnp.bfloat16)
                out[2 * j, part] = total[:, :256]
                out[2 * j + 1, part] = total[:, 256:]
            return carry

        lax.fori_loop(0, TILES, per_keys, 0)

        def finish(i, carry):
            total = (query_sum[i] * HEAD_DIM ** -0.5).astype(jnp.bfloat16)
            out[2 * i, 0] = total[:, :256]
            out[2 * i + 1, 0] = total[:, 256:]
            return carry

        lax.fori_loop(0, TILES, finish, 0)


def attend(parts):
    return pl.pallas_call(
        forward_kernel,
        name="attend",
        out_shape=[
            jax.ShapeDtypeStruct((MEMBERS, 1, HEAD_DIM, 256), jnp.bfloat16),
            jax.ShapeDtypeStruct((TILES, 1, TILE), jnp.float32),
        ],
        in_specs=vmem_specs(1),
        out_specs=vmem_specs(2),
        scratch_shapes=[pltpu.VMEM((TILES * TILE, HEAD_DIM), jnp.bfloat16)],
        compiler_params=pltpu.CompilerParams(vmem_limit_bytes=VMEM_BYTES),
    )(parts)


def attend_back(parts, attended, grad_att, lse):
    return pl.pallas_call(
        backward_kernel,
        name="attend_back",
        out_shape=jax.ShapeDtypeStruct((MEMBERS, 3, HEAD_DIM, 256), jnp.bfloat16),
        in_specs=vmem_specs(4),
        out_specs=vmem_specs(1)[0],
        scratch_shapes=[
            pltpu.VMEM((TILES, HEAD_DIM, TILE), jnp.float32),
            pltpu.VMEM((TILES, 1, TILE), jnp.float32),
        ],
        compiler_params=pltpu.CompilerParams(vmem_limit_bytes=VMEM_BYTES),
    )(parts, attended, grad_att, lse)


def normalize(values):
    center = values - jnp.mean(values, axis=-1, keepdims=True)
    inv_std = lax.rsqrt(jnp.mean(center * center, axis=-1, keepdims=True) + epsilon)
    return (center * inv_std, inv_std)


def norm_back(upstream, gain_row, normed, inv_std):
    scaled = upstream * gain_row
    return inv_std * (
        scaled
        - jnp.mean(scaled, axis=-1, keepdims=True)
        - normed * jnp.mean(scaled * normed, axis=-1, keepdims=True)
    )


def gelu_tanh(values):
    return jax.nn.gelu(values, approximate=True)


def multiply(form, left, right):
    return jnp.einsum(form, left, right, preferred_element_type=jnp.float32)


def per_device(tokens, cotangent, w_qkv, w_out, w_up, w_down, norm_gains):
    low = jnp.bfloat16
    owner = lax.axis_index("dp") * lax.axis_size("ctx") + lax.axis_index("ctx")
    shards = (
        jnp.concatenate([w_qkv, w_out.T[None]], axis=0).reshape(SLOT, WIDTH),
        w_up.reshape(ROWS, 4, WIDTH).transpose(1, 0, 2).reshape(SLOT, WIDTH),
        w_down.reshape(4, WIDTH, ROWS).transpose(0, 2, 1).reshape(SLOT, WIDTH),
    )
    gain_part = lax.dynamic_update_slice(
        jnp.zeros((8, 768), jnp.float32),
        0.5 * norm_gains.astype(jnp.float32),
        (jnp.int32(0), owner * ROWS),
    )
    qkv, out, up, down, gains = gather_weights(shards, gain_part)
    gain_one, gain_two = gains[0], gains[1]
    inputs = tokens.astype(jnp.float32)
    normed_one, inv_one = normalize(inputs)
    first_in = (normed_one * gain_one).astype(low)
    projected = multiply("dc,bd->cb", qkv, first_in).astype(low).reshape(3, HEADS, HEAD_DIM, 256)
    parts = to_heads(projected, "projections_to_heads", 2)
    head_out, lse = attend(parts)
    attended = from_heads(head_out, "attended_from_heads", 3).reshape(768, 256)
    middle = inputs + multiply("cb,dc->bd", attended, out)
    normed_two, inv_two = normalize(middle)
    second_in = (normed_two * gain_two).astype(low)
    hidden = multiply("bd,df->bf", second_in, up)
    activated, gelu_pull = jax.vjp(gelu_tanh, hidden)
    act_low = activated.astype(low)
    result = (middle + multiply("bf,df->bd", act_low, down)).astype(low)
    grad_down = multiply("bd,bf->df", cotangent, act_low).astype(low)
    grad_act = multiply("bd,df->bf", cotangent, down)
    grad_hidden = gelu_pull(grad_act)[0].astype(low)
    grad_up = multiply("bd,bf->df", second_in, grad_hidden).astype(low)
    grad_second = multiply("bf,df->bd", grad_hidden, up)
    grad_middle = cotangent.astype(jnp.float32) + norm_back(
        grad_second, gain_two, normed_two, inv_two
    )
    gain_two_term = jnp.sum(grad_second * normed_two, axis=0)
    mid_low = grad_middle.astype(low)
    grad_out = multiply("bd,cb->dc", mid_low, attended).astype(low)
    grad_att = multiply("bd,dc->cb", mid_low, out).astype(low).reshape(1, HEADS, HEAD_DIM, 256)
    head_grad = to_heads(grad_att, "gradients_to_heads", 4)
    head_back = attend_back(parts, head_out, head_grad, lse)
    grad_projected = from_heads(head_back, "gradients_from_heads", 5).reshape(2304, 256)
    grad_qkv = multiply("bd,cb->dc", first_in, grad_projected).astype(low)
    grad_first = multiply("cb,dc->bd", grad_projected, qkv)
    grad_tokens = grad_middle + norm_back(grad_first, gain_one, normed_one, inv_one)
    gain_one_term = jnp.sum(grad_first * normed_one, axis=0)
    gain_terms = jnp.concatenate(
        [gain_one_term[None], gain_two_term[None], jnp.zeros((6, 768), jnp.float32)]
    )
    sum_a, sum_b, sum_c, gain_sum = reduce_gradients(
        (grad_qkv, grad_out, grad_up, grad_down), gain_terms
    )
    sum_a = sum_a.reshape(4, ROWS, WIDTH)
    return (
        result,
        grad_tokens,
        sum_a[:3],
        sum_a[3].T,
        sum_b.reshape(4, ROWS, WIDTH).transpose(1, 0, 2).reshape(ROWS, 4 * WIDTH),
        sum_c.reshape(4, ROWS, WIDTH).transpose(0, 2, 1).reshape(4 * WIDTH, ROWS),
        lax.dynamic_slice(gain_sum, (jnp.int32(0), owner * ROWS), (2, ROWS)),
    )


def solution(mesh):
    return jax.shard_map(
        per_device,
        mesh=mesh,
        in_specs=(
            P(("dp", "ctx", "tensor"), None),
            P(("dp", "ctx", "tensor"), None),
            P(None, ("dp", "ctx"), "tensor"),
            P("tensor", ("dp", "ctx")),
            P(("dp", "ctx"), "tensor"),
            P("tensor", ("dp", "ctx")),
            P(None, ("dp", "ctx")),
        ),
        out_specs=(
            P(("dp", "ctx", "tensor"), None),
            P(("dp", "ctx", "tensor"), None),
            P(None, ("dp", "ctx"), "tensor"),
            P("tensor", ("dp", "ctx")),
            P(("dp", "ctx"), "tensor"),
            P("tensor", ("dp", "ctx")),
            P(None, ("dp", "ctx")),
        ),
        check_vma=False,
    )
```

time: 1410 us -> 313 us (0.22)
  blocking collectives: 535 us -> 0 us
  waiting for transfers between devices: 273 us -> 0 us
  starting transfers between devices: 260 us -> 0 us
  Pallas kernels: 0 us -> 257 us
  other arithmetic: 118 us -> 6.27 us
  local copies, waits for them, and re-layouts: 90.5 us -> 13 us
  matrix products: 109 us -> 34.9 us
  between operations: 17.2 us -> 0.98 us
    unnamed x2 -> x0, blocking collectives: 311 us -> none
    pallas_call x0 -> x8, Pallas kernels: none -> 257 us  [the longest x4 75.1 us: exchange(): pl.pallas_call(kernel, name=name, out_shape=jax.ShapeDtypeStruct(shape, j...]
    all_gather x6 -> x0, blocking collectives: 218 us -> none  [the longest x1 83.8 us: per_device(): lax.all_gather(norm_gains, ('dp', 'ctx'), axis=1, tiled=True)]
    ppermute x32 -> x0, starting transfers between devices: 140 us -> none  [the longest x16 75.7 us: from_behind(): return lax.ppermute(array, axis, pairs)]
    unnamed x49 -> x0, starting transfers between devices: 119 us -> none
    unnamed x59 -> x0, waiting for transfers between devices: 116 us -> none
    all_gather x5 -> x0, waiting for transfers between devices: 101 us -> none  [the longest x1 93.2 us: per_device(): lax.all_gather(w_up, ('dp', 'ctx'), axis=0, tiled=True)]
    dot_general x24 -> x12, matrix products: 109 us -> 34.9 us  [multiply(): return jnp.einsum(form, left, right, preferred_element_type=jnp.float32)]
  transfers between devices with their start and end apart: 90 -> 0, of which waited for: 13 -> 0; matrix products, arithmetic and copies ran while one was open for 28% -> 0% of each run, Pallas kernels for 0% -> 0%
where the time goes in v1:
time: 313 us; the launch traced here: 312 us
  Pallas kernels  257 us (82%)
  matrix products  34.9 us (11%)
  local copies, waits for them, and re-layouts  13 us (4%)
  other arithmetic  6.27 us (2%)
    pallas_call x4, Pallas kernels, exchange(): pl.pallas_call(kernel, name=name, out_shape=jax.ShapeDtypeStruct(shape, j...  75.1 us
    pallas_call x1, Pallas kernels, gather_weights(): pl.pallas_call(gather_kernel, name='gather_weights', out_shape=[jax.Shape...  63.5 us
    pallas_call x1, Pallas kernels, reduce_gradients(): pl.pallas_call(reduce_kernel, name='reduce_gradients', out_shape=[jax.Sha...  56.8 us
    pallas_call x1, Pallas kernels, attend_back(): pl.pallas_call(backward_kernel, name='attend_back', out_shape=jax.ShapeDt...  36.1 us
    dot_general x12, matrix products, multiply(): return jnp.einsum(form, left, right, preferred_element_type=jnp.float32)  34.9 us
    pallas_call x1, Pallas kernels, attend(): pl.pallas_call(forward_kernel, name='attend', out_shape=[jax.ShapeDtypeSt...  25.3 us

profile of v1, /device:TPU:1, one launch (start us, length us, event | category | flops | bytes accessed | tf_op | source)
XLA Modules:
  0.0 312.0 jit_solution(301442357006760104)
XLA Ops:
  6.7 63.5 %gather_weights.1 = (bf16[768,2304]{1,0:T(8,128)(2,1)}, bf16[768,768]{1,0:T(8,128)(2,1)}, bf16[768,3072]{1,0:T(8,128)(2,1)}, bf16[768,3072]{1,0:T(8,128)(2,1)}, f32[8,768]{1,0:T(8,128)}) custom-call(bf16[48,384]{1,0:T(8,128)(2,1)} %reshape.97.a, bf16[48,384]{1,0:T(8,128)(2,1)} %reshape.99.b, bf16[48,384]{1,0:T(8,128)(2,1)} %reshape.101.c, ...), custom_call_target="tpu_custom_call" | custom-call | tf_op jit(solution)/shard_map/gather_weights/pallas_call | solution.py:419
  72.3 1.2 fusion.21
  73.5 4.3 %convolution_convert_fusion.3 = bf16[2304,256]{1,0:T(8,128)(2,1)} fusion(bf16[768,2304]{1,0:T(8,128)(2,1)} %get-tuple-element.18, bf16[256,768]{1,0:T(8,128)(2,1)} %param.9, f32[768]{0:T(1024)S(1)} %get-tuple-element.36, f32[256]{0:T(256)S(1)} %add_rsqrt_fusion.1, f32[256]{0:T(256)S(1)} %broadcast_multiply_fusion.5), kind=kOutput, calls=%fused_computation.7 | convolution fusion | flops 907542528 | bytes 5116928 | tf_op jit(solution)/shard_map/dc,bd->cb/dot_general | solution.py:800
  77.8 21.0 %projections_to_heads.1.parts = bf16[16,3,64,256]{3,2,1,0:T(8,128)(2,1)} custom-call(bf16[3,12,64,256]{3,2,1,0:T(8,128)(2,1)} %bitcast.56), custom_call_target="tpu_custom_call" | custom-call | tf_op jit(solution)/shard_map/projections_to_heads/pallas_call | solution.py:601
  98.8 25.3 %attend.1 = (bf16[16,1,64,256]{3,2,1,0:T(8,128)(2,1)}, f32[8,1,512]{2,1,0:T(1,128)}) custom-call(bf16[16,3,64,256]{3,2,1,0:T(8,128)(2,1)} %projections_to_heads.1.parts), custom_call_target="tpu_custom_call" | custom-call | tf_op jit(solution)/shard_map/attend/pallas_call | solution.py:751
  124.1 17.3 %attended_from_heads.1 = bf16[1,12,64,256]{3,2,1,0:T(8,128)(2,1)} custom-call(bf16[16,1,64,256]{3,2,1,0:T(8,128)(2,1)} %get-tuple-element.20.src.attended), custom_call_target="tpu_custom_call" | custom-call | tf_op jit(solution)/shard_map/attended_from_heads/pallas_call | solution.py:601
  141.4 1.6 fusion.27
  143.3 3.9 %fusion.26 = f32[256,3072]{1,0:T(8,128)S(1)} fusion(bf16[768,3072]{1,0:T(8,128)(2,1)} %get-tuple-element.22, f32[256,768]{1,0:T(8,128)S(1)} %get-tuple-element.38, f32[768]{0:T(1024)S(1)} %get-tuple-element.35, f32[256]{0:T(256)S(1)} %add_rsqrt_fusion, f32[256]{0:T(256)S(1)} %broadcast_multiply_fusion.4), kind=kOutput, calls=%fused_computation.64 | convolution fusion | flops 1208745984 | bytes 8655872 | tf_op jit(solution)/shard_map/bd,df->bf/dot_general | solution.py:800
  147.3 2.8 fusion.8
  150.1 3.0 fusion.7
  153.2 2.1 multiply_reduce_fusion
  155.6 1.3 convolution_convert_fusion.5
  156.9 11.2 %gradients_to_heads.1.grad_att = bf16[16,1,64,256]{3,2,1,0:T(8,128)(2,1)} custom-call(bf16[1,12,64,256]{3,2,1,0:T(8,128)(2,1)} %bitcast.55), custom_call_target="tpu_custom_call" | custom-call | tf_op jit(solution)/shard_map/gradients_to_heads/pallas_call | solution.py:601
  168.1 36.1 %attend_back.1.src = bf16[16,3,64,256]{3,2,1,0:T(8,128)(2,1)} custom-call(bf16[16,3,64,256]{3,2,1,0:T(8,128)(2,1)} %projections_to_heads.1.parts, bf16[16,1,64,256]{3,2,1,0:T(8,128)(2,1)} %get-tuple-element.20.src.attended, bf16[16,1,64,256]{3,2,1,0:T(8,128)(2,1)} %gradients_to_heads.1.grad_att, f32[8,1,512]{2,1,0:T(1,128)} %get-tuple-element.24.lse), custom_call_target="tpu_custom_call" | custom-call | tf_op jit(solution)/shard_map/attend_back/pallas_call | solution.py:766
  204.2 25.7 %gradients_from_heads.1 = bf16[3,12,64,256]{3,2,1,0:T(8,128)(2,1)} custom-call(bf16[16,3,64,256]{3,2,1,0:T(8,128)(2,1)} %attend_back.1.src), custom_call_target="tpu_custom_call" | custom-call | tf_op jit(solution)/shard_map/gradients_from_heads/pallas_call | solution.py:601
  229.9 3.7 %fusion.20 = (f32[768]{0:T(1024)S(1)}, f32[256]{0:T(256)S(1)}, f32[256]{0:T(256)S(1)}, f32[256,768]{1,0:T(8,128)S(1)}) fusion(bf16[256,768]{1,0:T(8,128)(2,1)S(1)} %copy-done, f32[256]{0:T(256)S(1)} %copy-done.9, f32[256]{0:T(256)S(1)} %broadcast_multiply_fusion.5, f32[768]{0:T(1024)S(1)} %get-tuple-element.36, bf16[2304,256]{1,0:T(8,128)(2,1)} %bitcast.51, ...), kind=kOutput, calls=%fused_computation.34 | convolution fusion | flops 907737856 | bytes 5908480 | tf_op jit(solution)/shard_map/cb,dc->bd/dot_general | solution.py:800
  233.7 1.2 fusion.19
  235.0 3.1 convolution_convert_fusion.2.w_qkv
  238.0 1.6 convolution_convert_fusion.4.w_out
  239.6 3.7 %convolution_convert_fusion.1.w_up = bf16[768,3072]{1,0:T(8,128)(2,1)} fusion(bf16[256,3072]{1,0:T(8,128)(2,1)S(1)} %copy-done.5, f32[256,768]{1,0:T(8,128)S(1)} %get-tuple-element.38, f32[768]{0:T(1024)S(1)} %get-tuple-element.35, f32[256]{0:T(256)S(1)} %copy-done.11, f32[256]{0:T(256)S(1)} %broadcast_multiply_fusion.4), kind=kOutput, calls=%fused_computation.1 | convolution fusion | flops 1211105280 | bytes 7083008 | tf_op jit(solution)/shard_map/bd,bf->df/dot_general | solution.py:800
  243.3 3.8 %fusion.w_down = bf16[768,3072]{1,0:T(8,128)(2,1)} fusion(bf16[256,768]{1,0:T(8,128)(2,1)S(1)} %copy-done.6, f32[256,3072]{1,0:T(8,128)S(1)} %copy-done.14), kind=kOutput, calls=%fused_computation.5 | convolution fusion | flops 1217396736 | bytes 8257536 | tf_op jit(solution)/shard_map/bd,bf->df/dot_general | solution.py:800
  247.9 56.8 %reduce_gradients.1 = (f32[48,384]{1,0:T(8,128)}, f32[48,384]{1,0:T(8,128)}, f32[48,384]{1,0:T(8,128)}, f32[8,768]{1,0:T(8,128)}) custom-call(bf16[768,2304]{1,0:T(8,128)(2,1)} %convolution_convert_fusion.2.w_qkv, bf16[768,768]{1,0:T(8,128)(2,1)} %convolution_convert_fusion.4.w_out, bf16[768,3072]{1,0:T(8,128)(2,1)} %convolution_convert_fusion.1.w_up, ...), custom_call_target="tpu_custom_call" | custom-call | tf_op jit(solution)/shard_map/reduce_gradients/pallas_call | solution.py:440
  306.2 1.3 slice_bitcast_fusion
  310.7 1.3 constant_dynamic-slice_fusion
  (77 shorter events, 14.2 us)
Async XLA Ops:
  6.1 0.6 copy-start.7
  73.5 4.3 %copy-start.8 = (f32[256]{0:T(256)}, f32[256]{0:T(256)S(1)}, u32[]{:S(2)}) copy-start(f32[256]{0:T(256)S(1)} %add_rsqrt_fusion.1) | copy-start | bytes 3076
  77.8 63.6 %copy-start = (bf16[256,768]{1,0:T(8,128)(2,1)S(1)}, bf16[256,768]{1,0:T(8,128)(2,1)}, u32[]{:S(2)}) copy-start(bf16[256,768]{1,0:T(8,128)(2,1)} %param.9) | copy-start | bytes 1179652
  77.8 63.6 %copy-start.1 = (bf16[768,768]{1,0:T(8,128)(2,1)S(1)}, bf16[768,768]{1,0:T(8,128)(2,1)}, u32[]{:S(2)}) copy-start(bf16[768,768]{1,0:T(8,128)(2,1)} %get-tuple-element.21) | copy-start | bytes 3538948
  143.1 4.2 %slice-start.2 = ((s8[4718592]{0:T(1024)(128)(4,1)}), s8[4194304]{0:T(1024)(128)(4,1)S(1)}, s32[]{:S(2)}) async-start(s8[4718592]{0:T(1024)(128)(4,1)} %bitcast.69), calls=%async_computation.2 | async-start | bytes 8388608
  143.3 12.0 %copy-start.10 = (f32[256]{0:T(256)}, f32[256]{0:T(256)S(1)}, u32[]{:S(2)}) copy-start(f32[256]{0:T(256)S(1)} %add_rsqrt_fusion) | copy-start | bytes 3076
  143.3 4.0 %slice-start.3 = ((s8[4718592]{0:T(1024)(128)(4,1)}), s8[524288]{0:T(1024)(128)(4,1)S(1)}, s32[]{:S(2)}) async-start(s8[4718592]{0:T(1024)(128)(4,1)} %bitcast.69), calls=%async_computation.3 | async-start | bytes 1048576
  147.3 2.8 copy-start.13
  147.3 2.8 copy-start.6
  147.3 5.8 %slice-start = ((s8[4718592]{0:T(1024)(128)(4,1)}), s8[4194304]{0:T(1024)(128)(4,1)S(1)}, s32[]{:S(2)}) async-start(s8[4718592]{0:T(1024)(128)(4,1)} %bitcast.67), calls=%async_computation | async-start | bytes 8388608
  150.1 3.0 slice-start.1
  153.2 2.1 copy-start.4
  168.1 61.8 %copy-start.9 = (f32[256]{0:T(256)S(1)}, f32[256]{0:T(256)}, u32[]{:S(2)}) copy-start(f32[256]{0:T(256)} %copy-done.8) | copy-start | bytes 3076
  233.7 1.3 copy-start.2
  234.9 3.1 copy-start.3
  234.9 4.7 %copy-start.5 = (bf16[256,3072]{1,0:T(8,128)(2,1)S(1)}, bf16[256,3072]{1,0:T(8,128)(2,1)}, u32[]{:S(2)}) copy-start(bf16[256,3072]{1,0:T(8,128)(2,1)} %copy-done.4) | copy-start | bytes 4718596
  235.0 4.7 %copy-start.11 = (f32[256]{0:T(256)S(1)}, f32[256]{0:T(256)}, u32[]{:S(2)}) copy-start(f32[256]{0:T(256)} %copy-done.10) | copy-start | bytes 3076
  239.6 3.7 %copy-start.14 = (f32[256,3072]{1,0:T(8,128)S(1)}, f32[256,3072]{1,0:T(8,128)}, u32[]{:S(2)}) copy-start(f32[256,3072]{1,0:T(8,128)} %copy-done.13) | copy-start | bytes 9437188
  243.3 3.8 %copy-start.12 = (f32[768]{0:T(1024)S(1)}, f32[768]{0:T(1024)}, u32[]{:S(2)}) copy-start(f32[768]{0:T(1024)} %get-tuple-element.29) | copy-start | bytes 9220

commit v2 on v0

v2 whole, which is shorter than its diff:
```python
import functools

import jax
import jax.numpy as jnp
import numpy as np
from jax import lax
from jax.experimental import pallas as pl
from jax.experimental.pallas import tpu as pltpu
from jax.sharding import PartitionSpec as P

HEAD_DIM = 64
HEADS = 12
MEMBERS = 16
ROWS = 12
WIDTH = 384
SLOT = 4 * ROWS
THIRDS = (("z", "x", "y"), ("x", "y", "z"), ("y", "z", "x"))
WHOLES = (("z", "y", "x"), ("z", "x", "y"))
MESH = pl.DeviceIdType.MESH
VMEM_BYTES = 60 * 1024 * 1024
epsilon = 1e-05
neg_large = -1e30


def place():
    dp, ctx, tensor = lax.axis_index("dp"), lax.axis_index("ctx"), lax.axis_index("tensor")
    return dict(x=dp // 2, y=ctx // 2, z=2 * tensor + dp % 2, c=ctx % 2)


def device_at(pos, axis, index):
    at = dict(pos)
    at[axis] = index
    return (at["x"] * 2 + at["z"] % 2, at["y"] * 2 + at["c"], at["z"] // 2)


def beside(pos, axis, by):
    if axis == "c":
        return device_at(pos, "c", 1 - pos["c"])
    return device_at(pos, axis, (pos[axis] + by) % 4)


def greet(pos):
    barrier = pltpu.get_barrier_semaphore()
    dp, number = lax.axis_index("dp"), member_number()

    def signal(i, carry):
        to = (number + i) % MEMBERS
        pl.semaphore_signal(
            barrier, inc=1, device_id=(dp, to // 2, to % 2), device_id_type=MESH
        )
        return carry

    lax.fori_loop(1, MEMBERS, signal, 0)
    for axis, by in (("x", 1), ("x", 2), ("x", 3), ("z", 1), ("z", 3)):
        pl.semaphore_signal(barrier, inc=1, device_id=beside(pos, axis, by), device_id_type=MESH)
    pl.semaphore_wait(barrier, MEMBERS - 1 + 5)


def member_number():
    return 2 * lax.axis_index("ctx") + lax.axis_index("tensor")


def remote(src, dst, send, recv, device):
    return pltpu.make_async_remote_copy(
        src_ref=src,
        dst_ref=dst,
        send_sem=send,
        recv_sem=recv,
        device_id=device,
        device_id_type=MESH,
    )


class SmallSum:
    def __init__(self, pos, ring, pair, send, recv):
        self.pos, self.ring, self.pair, self.send, self.recv = pos, ring, pair, send, recv

    def copy(self, n, by, coming=False):
        axis = ("x", "y", "z")[n]
        slot = (self.pos[axis] + 4 - by) % 4 if coming else self.pos[axis]
        ref, sem = self.ring.at[n, slot], n * 3 + by - 1
        return remote(
            ref, ref, self.send.at[sem], self.recv.at[sem], beside(self.pos, axis, by)
        )

    def start(self, n, value):
        self.ring[n, self.pos[("x", "y", "z")[n]]] = value
        for by in (1, 2, 3):
            self.copy(n, by).start()

    def finish(self, n):
        for by in (1, 2, 3):
            self.copy(n, by, coming=True).wait_recv()
            self.copy(n, by).wait_send()
        return (self.ring[n, 0] + self.ring[n, 1]) + (self.ring[n, 2] + self.ring[n, 3])

    def pair_copy(self, slot):
        ref = self.pair.at[slot]
        return remote(ref, ref, self.send.at[9], self.recv.at[9], beside(self.pos, "c", 1))

    def start_pair(self, value):
        self.pair[self.pos["c"]] = value
        self.pair_copy(self.pos["c"]).start()

    def finish_pair(self):
        self.pair_copy(1 - self.pos["c"]).wait_recv()
        self.pair_copy(self.pos["c"]).wait_send()
        return self.pair[0] + self.pair[1]


class Group:
    def __init__(self, pos, send, recv):
        self.pos, self.send, self.recv = pos, send, recv
        self.member = (pos["y"] % 2) * 2 + pos["c"]
        y = pos["y"] + 1 - 2 * (pos["y"] % 2)
        c = 1 - pos["c"]
        self.partners = []
        for to_y, to_c in ((pos["y"], c), (y, pos["c"]), (y, c)):
            device = device_at({**pos, "y": to_y}, "c", to_c)
            self.partners.append((device, (to_y % 2) * 2 + to_c))

    def copy(self, held, k, i, coming=False):
        device, member = self.partners[i]
        ref = held.at[k, member if coming else self.member]
        return remote(ref, ref, self.send.at[k * 3 + i], self.recv.at[k * 3 + i], device)

    def start(self, held, k):
        for i in range(3):
            self.copy(held, k, i).start()

    def finish(self, held, k):
        for i in range(3):
            self.copy(held, k, i, coming=True).wait_recv()
        return jnp.concatenate([held[k, member] for member in range(4)], axis=0)

    def sent(self, held, k):
        for i in range(3):
            self.copy(held, k, i).wait_send()


class Unit:
    def __init__(self, pos, order, unit, send, recv, started):
        self.pos, self.order, self.unit = pos, order, unit
        self.send, self.recv, self.started = send, recv, started
        self.sibling = beside(pos, "c", 1)

    def move(self, src, dst, sem, device):
        sem = self.unit * 16 + sem
        copy = remote(src, dst, self.send.at[sem], self.recv.at[sem], device)
        copy.start()
        self.started.append(copy)

    def arrived(self, dst, sem):
        sem = self.unit * 16 + sem
        remote(dst, dst, self.send.at[sem], self.recv.at[sem], self.sibling).wait_recv()

    def along(self, stage, by):
        return beside(self.pos, self.order[stage], by)

    def at(self, stage, by):
        index = ((self.pos[self.order[stage]] + by) % 4,)
        for later in range(stage + 1, 3):
            index = (self.pos[self.order[later]],) + index
        return (self.unit, self.pos["c"]) + index


class Gather(Unit):
    def __init__(self, pos, order, unit, held, send, recv, started):
        super().__init__(pos, order, unit, send, recv, started)
        self.held = held

    def halves(self, stage, which):
        return () if stage == 0 else (pl.ds(2 * which, 2),)

    def pass_on(self, index, sem, device):
        self.move(self.held.at[index], self.held.at[index], sem, device)

    def begin(self, stage):
        for side, by in ((0, 1), (1, 3)):
            self.pass_on(self.at(stage, 0), stage * 4 + side, self.along(stage, by))
        if stage == 2:
            self.share(0, 12)

    def relay(self, stage):
        for side, by, back in ((0, 1, 3), (1, 3, 1)):
            block = self.at(stage, back)
            self.arrived(self.held.at[block], stage * 4 + side)
            if stage > 0 or side == 0:
                self.pass_on(
                    block + self.halves(stage, side), stage * 4 + 2 + side, self.along(stage, by)
                )
            if stage == 2:
                self.share(back, 13 + side)

    def finish(self, stage):
        for side in range(2):
            if stage > 0 or side == 0:
                block = self.at(stage, 2) + self.halves(stage, side)
                self.arrived(self.held.at[block], stage * 4 + 2 + side)
        if stage == 2:
            self.share(2, 15)

    def share(self, by, sem):
        self.pass_on(self.at(2, by), sem, self.sibling)

    def settle(self):
        place3 = self.pos[self.order[2]]
        for by, sem in ((0, 12), (3, 13), (1, 14), (2, 15)):
            index = (self.unit, 1 - self.pos["c"], (place3 + by) % 4)
            self.arrived(self.held.at[index], sem)


def wide(value):
    return value.astype(jnp.float32)


class Reduce(Unit):
    def __init__(self, pos, order, unit, held, landing, send, recv, started):
        super().__init__(pos, order, unit, send, recv, started)
        self.held = held
        self.cores, self.halves3, self.fulls3, self.halves2, self.fulls2, self.half1, self.fulls1 = (
            landing
        )

    def add(self, index, sources, *counts):
        held = self.held
        if not counts:
            total = wide(held[index])
            for source, at in sources:
                total = total + wide(source[at])
            held[index] = total.astype(jnp.bfloat16)
            return

        def body(i, carry):
            slot = (i // counts[1], i % counts[1]) if len(counts) == 2 else (i,)
            total = wide(held[index + slot])
            for source, at in sources:
                total = total + wide(source[at + slot])
            held[index + slot] = total.astype(jnp.bfloat16)
            return carry

        lax.fori_loop(0, counts[0] * counts[-1] if len(counts) == 2 else counts[0], body, 0)

    def cross(self):
        place3, u = self.pos[self.order[2]], self.unit
        for by, sem in ((2, 12), (1, 13), (3, 14), (0, 15)):
            index = (place3 + by) % 4
            self.move(
                self.held.at[u, 1 - self.pos["c"], index], self.cores.at[u, index], sem, self.sibling
            )

    def take_core(self, by, sem):
        index = (self.pos[self.order[2]] + by) % 4
        self.arrived(self.cores.at[self.unit, index], sem)
        self.add(self.at(2, by), [(self.cores, (self.unit, index))], 4, 4)

    def begin(self, stage):
        u = self.unit
        if stage == 2:
            self.take_core(2, 12)
        if stage == 0:
            self.move(self.held.at[self.at(0, 2)], self.half1.at[u], 8, self.along(0, 1))
            self.move(self.held.at[self.at(0, 3)], self.fulls1.at[u, 1], 11, self.along(0, 3))
            return
        landing = self.halves3 if stage == 2 else self.halves2
        for side, by in ((0, 1), (1, 3)):
            self.move(
                self.held.at[self.at(stage, 2) + (pl.ds(2 * side, 2),)],
                landing.at[u, side],
                (2 - stage) * 4 + side,
                self.along(stage, by),
            )
        if stage == 2:
            self.take_core(1, 13)
            self.take_core(3, 14)

    def relay(self, stage):
        u = self.unit
        if stage == 0:
            self.arrived(self.half1.at[u], 8)
            self.add(self.at(0, 1), [(self.half1, (u,))])
            self.move(self.held.at[self.at(0, 1)], self.fulls1.at[u, 0], 10, self.along(0, 1))
            return
        halves = self.halves3 if stage == 2 else self.halves2
        fulls = self.fulls3 if stage == 2 else self.fulls2
        base = (2 - stage) * 4
        for side, by in ((0, 1), (1, 3)):
            self.arrived(halves.at[u, side], base + side)
            index = self.at(stage, by)
            for row in range(2):
                if stage == 2:
                    self.add(index + (2 * side + row,), [(halves, (u, side, row))], 4)
                else:
                    self.add(index + (2 * side + row,), [(halves, (u, side, row))])
            self.move(
                self.held.at[index], fulls.at[u, side], base + 2 + side, self.along(stage, by)
            )

    def finish(self, stage):
        u = self.unit
        if stage == 2:
            self.take_core(0, 15)
        fulls = (self.fulls1, self.fulls2, self.fulls3)[stage]
        for side in range(2):
            self.arrived(fulls.at[u, side], (2 - stage) * 4 + 2 + side)
        self.add(
            self.at(stage, 0),
            [(fulls, (u, 0)), (fulls, (u, 1))],
            *((), (4,), (4, 4))[stage],
        )


def landing_scratch(units, rows):
    low, slot = jnp.bfloat16, (rows, WIDTH)
    return [
        pltpu.VMEM((units, 4, 4, 4) + slot, low),
        pltpu.VMEM((units, 2, 2, 4) + slot, low),
        pltpu.VMEM((units, 2, 4, 4) + slot, low),
        pltpu.VMEM((units, 2, 2) + slot, low),
        pltpu.VMEM((units, 2, 4) + slot, low),
        pltpu.VMEM((units,) + slot, low),
        pltpu.VMEM((units, 2) + slot, low),
    ]


def slots_of(group, orders):
    x, z_lo, y_half = group // 4, (group // 2) % 2, group % 2
    for tensor in range(2):
        for piece in range(4):
            at = dict(x=x, z=2 * tensor + z_lo, y=2 * y_half + piece // 2)
            yield tensor, piece, [
                (piece % 2, at[order[2]], at[order[1]], at[order[0]]) for order in orders
            ]


def column_of(tensor, piece):
    return (0, (piece * 2 + tensor) * WIDTH) if piece < 3 else (1, tensor * WIDTH)


def copy_thirds(thirds, whole, to_whole):
    def body(group, carry):
        for tensor, piece, indices in slots_of(group, THIRDS):
            which, column = column_of(tensor, piece)
            for third, index in enumerate(indices):
                rows = pl.ds(pl.multiple_of(group * SLOT + 16 * third, 16), 16)
                if to_whole:
                    whole[which][rows, pl.ds(column, WIDTH)] = thirds[(third,) + index]
                else:
                    thirds[(third,) + index] = whole[which][rows, pl.ds(column, WIDTH)]
        return carry

    lax.fori_loop(0, 16, body, 0)


def copy_wholes(slots, whole, to_whole):
    def body(group, carry):
        rows = pl.ds(pl.multiple_of(group * SLOT, SLOT), SLOT)
        for tensor, piece, indices in slots_of(group, WHOLES):
            columns = pl.ds((tensor * 4 + piece) * WIDTH, WIDTH)
            for k, index in enumerate(indices):
                if to_whole:
                    whole[k][rows, columns] = slots[(k,) + index]
                else:
                    slots[(k,) + index] = whole[k][rows, columns]
        return carry

    lax.fori_loop(0, 16, body, 0)


def head_place(head):
    member = head % 6
    return (member * 2) % 8 + (member // 4) * (1 + (member % 4) * 2), head // 6


def own_head(ctx, tensor):
    core, y = ctx % 2, ctx // 2
    return tensor * 6 + (1 - core) * y + core * (4 + y // 2), core * (y % 2) == 0


class ToHeads:
    def __init__(self, src, dst, send, recv):
        self.src, self.dst, self.send, self.recv = src, dst, send, recv
        self.dp, self.number = lax.axis_index("dp"), member_number()

    def copies(self, i):
        head = (self.number + i) % HEADS
        ctx, tensor = head_place(head)
        local = 2 * ctx + tensor == self.number
        src, dst = self.src.at[:, head], self.dst.at[self.number]
        recv = self.recv.at[self.number]
        return (
            local,
            lambda: pltpu.make_async_copy(src, dst, recv),
            lambda: remote(src, dst, self.send.at[head], recv, (self.dp, ctx, tensor)),
        )

    def start(self):
        def body(i, carry):
            local, inside, outside = self.copies(i)

            @pl.when(local)
            def _():
                inside().start()

            @pl.when(jnp.logical_not(local))
            def _():
                outside().start()

            return carry

        lax.fori_loop(0, HEADS, body, 0)

    def wait(self, first, last):
        def body(i, carry):
            src, dst, recv = self.src.at[:, 0], self.dst.at[i], self.recv.at[i]

            @pl.when(i == self.number)
            def _():
                pltpu.make_async_copy(src, dst, recv).wait()

            @pl.when(i != self.number)
            def _():
                remote(src, dst, self.send.at[0], recv, (self.dp, i // 2, i % 2)).wait_recv()

            return carry

        lax.fori_loop(first, last, body, 0)

    def sent(self):
        def body(i, carry):
            local, inside, outside = self.copies(i)

            @pl.when(jnp.logical_not(local))
            def _():
                outside().wait_send()

            return carry

        lax.fori_loop(0, HEADS, body, 0)


class FromHeads:
    def __init__(self, src, dst, send, recv):
        self.src, self.dst, self.send, self.recv = src, dst, send, recv
        self.dp, self.number = lax.axis_index("dp"), member_number()
        self.head = own_head(lax.axis_index("ctx"), lax.axis_index("tensor"))[0]

    def outside(self, to):
        return remote(
            self.src.at[to],
            self.dst.at[:, self.head],
            self.send.at[to],
            self.recv.at[self.head],
            (self.dp, to // 2, to % 2),
        )

    def start(self, to):
        @pl.when(to == self.number)
        def _():
            pltpu.make_async_copy(
                self.src.at[to], self.dst.at[:, self.head], self.recv.at[self.head]
            ).start()

        @pl.when(to != self.number)
        def _():
            self.outside(to).start()

    def wait(self):
        def body(i, carry):
            ctx, tensor = head_place(i)
            local = 2 * ctx + tensor == self.number
            src, dst, recv = self.src.at[0], self.dst.at[:, i], self.recv.at[i]

            @pl.when(local)
            def _():
                pltpu.make_async_copy(src, dst, recv).wait()

            @pl.when(jnp.logical_not(local))
            def _():
                remote(src, dst, self.send.at[0], recv, (self.dp, ctx, tensor)).wait_recv()

            return carry

        lax.fori_loop(0, HEADS, body, 0)

    def sent(self):
        def body(i, carry):
            self.outside((self.number + i) % MEMBERS).wait_send()
            return carry

        lax.fori_loop(1, MEMBERS, body, 0)


TILE = 512
TILES = 8


def turned(value):
    return jnp.transpose(value.astype(jnp.float32)).astype(jnp.bfloat16)


def allowed_tile():
    key = lax.broadcasted_iota(jnp.int32, (TILE, TILE), 0)
    query = lax.broadcasted_iota(jnp.int32, (TILE, TILE), 1)
    return query >= key


def two(ref, tile, *index):
    return jnp.concatenate([ref[(2 * tile,) + index], ref[(2 * tile + 1,) + index]], axis=1)


def put_two(ref, tile, part, value):
    ref[2 * tile, part] = value[:, :256]
    ref[2 * tile + 1, part] = value[:, 256:]


def dot(a, b):
    return jnp.dot(a, b, preferred_element_type=jnp.float32)


def dot_right(a, b):
    return lax.dot_general(a, b, (((1,), (1,)), ((), ())), preferred_element_type=jnp.float32)


def attend_tile(i, parts, keys, out, lse):
    own_rows = pl.ds(pl.multiple_of(i * TILE, TILE), TILE)
    keys[own_rows, :] = turned(two(parts, i, 1))
    query = two(parts, i, 0) * jnp.bfloat16(HEAD_DIM ** -0.5)

    def step(scores, j, state):
        top, total, weighted = state
        new_top = jnp.maximum(top, jnp.max(scores, axis=0, keepdims=True))
        fade = jnp.exp(top - new_top)
        raised = jnp.exp(scores - new_top)
        total = total * fade + jnp.sum(raised, axis=0, keepdims=True)
        weighted = weighted * fade + dot(two(parts, j, 2), raised.astype(jnp.bfloat16))
        return new_top, total, weighted

    def before(j, state):
        return step(dot(keys[pl.ds(pl.multiple_of(j * TILE, TILE), TILE), :], query), j, state)

    state = (
        jnp.full((1, TILE), neg_large, jnp.float32),
        jnp.zeros((1, TILE), jnp.float32),
        jnp.zeros((HEAD_DIM, TILE), jnp.float32),
    )
    state = lax.fori_loop(0, i, before, state)
    masked = jnp.where(allowed_tile(), dot(keys[own_rows, :], query), neg_large)
    top, total, weighted = step(masked, i, state)
    put_two(out, i, 0, (weighted / total).astype(jnp.bfloat16))
    lse[i] = top + jnp.log(total)


def forward_kernel(
    tokens, a, b, c, gain, shuffle,
    normed_out, inv_out, first_out, parts, head_out, lse, attended, gain_out,
    w_qkv, w_out, w_up, w_down,
    pre, thirds, wholes, qkv, out, up, down, projected, keys, ring, pair,
    third_send, third_recv, whole_send, whole_recv, pre_send, pre_recv, small_send, small_recv,
    to_send, to_recv, from_send, from_recv, write_sem,
):
    pos = place()
    active = own_head(lax.axis_index("ctx"), lax.axis_index("tensor"))[1]
    group = Group(pos, pre_send, pre_recv)
    small = SmallSum(pos, ring, pair, small_send, small_recv)
    started = []
    first = [
        Gather(pos, order, u, thirds, third_send, third_recv, started)
        for u, order in enumerate(THIRDS)
    ]
    later = [
        Gather(pos, order, u, wholes, whole_send, whole_recv, started)
        for u, order in enumerate(WHOLES)
    ]
    spread = ToHeads(projected, parts, to_send, to_recv)
    back = FromHeads(head_out, attended, from_send, from_recv)
    for k, shard in enumerate((a, b, c)):
        pre[k, group.member] = shard[...]
    greet(pos)
    for k in range(3):
        group.start(pre, k)
    small.start(0, gain[...])

    def sorted_piece(k):
        return dot(shuffle[group.member], group.finish(pre, k)).astype(jnp.bfloat16)

    piece = sorted_piece(0)
    for u, unit in enumerate(first):
        thirds[unit.at(0, 0)] = piece[16 * u : 16 * (u + 1)]
        unit.begin(0)
    for u, unit in enumerate(later):
        wholes[unit.at(0, 0)] = sorted_piece(1 + u)
    values = tokens[...].astype(jnp.float32)
    center = values - jnp.mean(values, axis=-1, keepdims=True)
    inv_std = lax.rsqrt(jnp.mean(center * center, axis=-1, keepdims=True) + epsilon)
    normed_out[...] = center * inv_std
    inv_out[...] = inv_std
    for stage in range(3):
        for unit in first:
            unit.relay(stage)
        if stage == 1:
            for unit in later:
                unit.begin(0)
        for unit in first:
            unit.finish(stage)
        if stage < 2:
            for unit in first:
                unit.begin(stage + 1)
        total = small.finish(stage)
        if stage < 2:
            small.start(stage + 1, total)
        else:
            small.start_pair(total)
    for unit in later:
        unit.relay(0)
    for unit in later:
        unit.finish(0)
        unit.begin(1)
    for unit in first:
        unit.settle()
    copy_thirds(thirds, (qkv, out), True)
    writes = [
        pltpu.make_async_copy(src, dst, write_sem.at[n])
        for n, (src, dst) in enumerate(((qkv, w_qkv), (out, w_out), (up, w_up), (down, w_down)))
    ]
    writes[0].start()
    writes[1].start()
    gains = small.finish_pair()
    gain_out[...] = gains
    first_in = (normed_out[...] * gains[0:1]).astype(jnp.bfloat16)
    first_out[...] = first_in
    for part in range(3):
        for tensor in range(2):
            column = (part * 2 + tensor) * WIDTH
            cols = jnp.transpose(dot(first_in, qkv[:, pl.ds(column, WIDTH)])).astype(jnp.bfloat16)
            for head in range(6):
                projected[part, tensor * 6 + head] = cols[head * HEAD_DIM : (head + 1) * HEAD_DIM]
    spread.start()
    for unit in later:
        unit.relay(1)
    for unit in later:
        unit.finish(1)
        unit.begin(2)

    def per_queries(i, carry):
        @pl.when(active)
        def _():
            spread.wait(2 * i, 2 * i + 2)
            attend_tile(i, parts, keys, head_out, lse)
            back.start(2 * i)
            back.start(2 * i + 1)

        return carry

    lax.fori_loop(0, 5, per_queries, 0)
    for unit in later:
        unit.relay(2)
    lax.fori_loop(5, 7, per_queries, 0)
    for unit in later:
        unit.finish(2)
    lax.fori_loop(7, 8, per_queries, 0)
    for unit in later:
        unit.settle()
    copy_wholes(wholes, (up, down), True)
    writes[2].start()
    writes[3].start()
    back.wait()
    spread.sent()

    @pl.when(active)
    def _():
        back.sent()

    for k in range(3):
        group.sent(pre, k)
    for copy in started:
        copy.wait_send()
    for write in writes:
        write.wait()


def back_tile(j, parts, grad_att, lse, delta, query_sum, out):
    key_cols, value_cols = two(parts, j, 1), two(parts, j, 2)
    key_rows, value_rows = turned(key_cols), turned(value_cols)

    def step(i, state, diagonal):
        key_sum, value_sum = state
        query = two(parts, i, 0) * jnp.bfloat16(HEAD_DIM ** -0.5)
        grad = two(grad_att, i, 0)
        shares = jnp.exp(dot(key_rows, query) - lse[i])
        if diagonal:
            shares = jnp.where(allowed_tile(), shares, 0.0)
        grad_scores = (shares * (dot(value_rows, grad) - delta[i])).astype(jnp.bfloat16)
        query_sum[i] += dot(key_cols, grad_scores)
        key_sum = key_sum + dot_right(query, grad_scores)
        value_sum = value_sum + dot_right(grad, shares.astype(jnp.bfloat16))
        return key_sum, value_sum

    zero = jnp.zeros((HEAD_DIM, TILE), jnp.float32)
    state = step(j, (zero, zero), True)
    key_sum, value_sum = lax.fori_loop(
        j + 1, TILES, lambda i, state: step(i, state, False), state
    )
    put_two(out, j, 0, (query_sum[j] * HEAD_DIM ** -0.5).astype(jnp.bfloat16))
    put_two(out, j, 1, key_sum.astype(jnp.bfloat16))
    put_two(out, j, 2, value_sum.astype(jnp.bfloat16))


def backward_kernel(
    grad_att, parts, head_out, lse, grad_up, grad_down, unshuffle,
    grad_projected, out_b, out_c,
    head_grad, head_back, query_sum, delta, wholes, post,
    cores, halves3, fulls3, halves2, fulls2, half1, fulls1,
    whole_send, whole_recv, post_send, post_recv, to_send, to_recv, from_send, from_recv,
):
    pos = place()
    active = own_head(lax.axis_index("ctx"), lax.axis_index("tensor"))[1]
    group = Group(pos, post_send, post_recv)
    started = []
    landing = (cores, halves3, fulls3, halves2, fulls2, half1, fulls1)
    units = [
        Reduce(pos, order, u, wholes, landing, whole_send, whole_recv, started)
        for u, order in enumerate(WHOLES)
    ]
    spread = ToHeads(grad_att, head_grad, to_send, to_recv)
    back = FromHeads(head_back, grad_projected, from_send, from_recv)
    greet(pos)
    spread.start()
    copy_wholes(wholes, (grad_up, grad_down), False)
    for unit in units:
        unit.cross()
    for unit in units:
        unit.begin(2)

    @pl.when(active)
    def _():
        spread.wait(0, MEMBERS)

        def prepare(i, carry):
            delta[i] = jnp.sum(
                wide(two(head_out, i, 0)) * wide(two(head_grad, i, 0)), axis=0, keepdims=True
            )
            query_sum[i] = jnp.zeros((HEAD_DIM, TILE), jnp.float32)
            return carry

        lax.fori_loop(0, TILES, prepare, 0)

    def per_keys(j, carry):
        @pl.when(active)
        def _():
            back_tile(j, parts, head_grad, lse, delta, query_sum, head_back)
            back.start(2 * j)
            back.start(2 * j + 1)

        return carry

    lax.fori_loop(0, 1, per_keys, 0)
    for unit in units:
        unit.relay(2)
    lax.fori_loop(1, 3, per_keys, 0)
    for unit in units:
        unit.finish(2)
        unit.begin(1)
    lax.fori_loop(3, 4, per_keys, 0)
    for unit in units:
        unit.relay(1)
    lax.fori_loop(4, 5, per_keys, 0)
    for unit in units:
        unit.finish(1)
        unit.begin(0)
    lax.fori_loop(5, 6, per_keys, 0)
    for unit in units:
        unit.relay(0)
    lax.fori_loop(6, 7, per_keys, 0)
    for u, unit in enumerate(units):
        unit.finish(0)
        post[u, group.member] = wholes[unit.at(0, 0)]
        group.start(post, u)
    lax.fori_loop(7, 8, per_keys, 0)
    for u, out in enumerate((out_b, out_c)):
        out[...] = dot(unshuffle[group.member], group.finish(post, u))
        group.sent(post, u)
    back.wait()
    spread.sent()

    @pl.when(active)
    def _():
        back.sent()

    for copy in started:
        copy.wait_send()


def reduce_kernel(
    grad_qkv, grad_out, gain, unshuffle, out_a, gain_out,
    thirds, post, cores, halves3, fulls3, halves2, fulls2, half1, fulls1, ring, pair,
    third_send, third_recv, post_send, post_recv, small_send, small_recv,
):
    pos = place()
    group = Group(pos, post_send, post_recv)
    small = SmallSum(pos, ring, pair, small_send, small_recv)
    started = []
    landing = (cores, halves3, fulls3, halves2, fulls2, half1, fulls1)
    units = [
        Reduce(pos, order, u, thirds, landing, third_send, third_recv, started)
        for u, order in enumerate(THIRDS)
    ]
    copy_thirds(thirds, (grad_qkv, grad_out), False)
    greet(pos)
    for unit in units:
        unit.cross()
    small.start(0, gain[...])
    for stage in (2, 1, 0):
        for unit in units:
            unit.begin(stage)
        for unit in units:
            unit.relay(stage)
        total = small.finish(2 - stage)
        if stage > 0:
            small.start(3 - stage, total)
        else:
            small.start_pair(total)
        for unit in units:
            unit.finish(stage)
    for u, unit in enumerate(units):
        post[0, group.member, pl.ds(16 * u, 16)] = thirds[unit.at(0, 0)]
    group.start(post, 0)
    gain_out[...] = small.finish_pair()
    out_a[...] = dot(unshuffle[group.member], group.finish(post, 0))
    group.sent(post, 0)
    for copy in started:
        copy.wait_send()


def shuffle_matrix():
    matrix = np.zeros((4, SLOT, 4 * SLOT), np.float32)
    for piece in range(4):
        for member in range(4):
            for row in range(ROWS):
                matrix[piece, member * ROWS + row, member * SLOT + piece * ROWS + row] = 1
    return jnp.asarray(matrix, jnp.bfloat16)


def unshuffle_matrix():
    matrix = np.zeros((4, SLOT, 4 * SLOT), np.float32)
    for member in range(4):
        for piece in range(4):
            for row in range(ROWS):
                matrix[member, piece * ROWS + row, piece * SLOT + member * ROWS + row] = 1
    return jnp.asarray(matrix, jnp.bfloat16)


def vmem_specs(count):
    return [pl.BlockSpec(memory_space=pltpu.VMEM)] * count


def any_specs(count):
    return [pl.BlockSpec(memory_space=pl.ANY)] * count


def sems(count):
    return [pltpu.SemaphoreType.DMA((count,))] * 2


def low_array(*shape):
    return jax.ShapeDtypeStruct(shape, jnp.bfloat16)


def wide_array(*shape):
    return jax.ShapeDtypeStruct(shape, jnp.float32)


SMALL_SCRATCH = [
    pltpu.VMEM((3, 4, 8, 768), jnp.float32),
    pltpu.VMEM((2, 8, 768), jnp.float32),
]


def kernel_params(number):
    return pltpu.CompilerParams(
        collective_id=number, has_side_effects=True, vmem_limit_bytes=VMEM_BYTES
    )


def forward_attention(tokens, shards, gain):
    low = jnp.bfloat16
    return pl.pallas_call(
        forward_kernel,
        name="forward_attention",
        out_shape=[
            wide_array(256, 768),
            wide_array(256, 1),
            low_array(256, 768),
            low_array(MEMBERS, 3, HEAD_DIM, 256),
            low_array(MEMBERS, 1, HEAD_DIM, 256),
            wide_array(TILES, 1, TILE),
            low_array(1, HEADS, HEAD_DIM, 256),
            wide_array(8, 768),
            low_array(768, 2304),
            low_array(768, 768),
            low_array(768, 3072),
            low_array(768, 3072),
        ],
        in_specs=vmem_specs(6),
        out_specs=vmem_specs(8) + any_specs(4),
        scratch_shapes=[
            pltpu.VMEM((3, 4, SLOT, WIDTH), low),
            pltpu.VMEM((3, 2, 4, 4, 4, 16, WIDTH), low),
            pltpu.VMEM((2, 2, 4, 4, 4, SLOT, WIDTH), low),
            pltpu.VMEM((768, 2304), low),
            pltpu.VMEM((768, 768), low),
            pltpu.VMEM((768, 3072), low),
            pltpu.VMEM((768, 3072), low),
            pltpu.VMEM((3, HEADS, HEAD_DIM, 256), low),
            pltpu.VMEM((TILES * TILE, HEAD_DIM), low),
        ]
        + SMALL_SCRATCH
        + sems(48)
        + sems(32)
        + sems(9)
        + sems(10)
        + sems(MEMBERS)
        + sems(MEMBERS)
        + [pltpu.SemaphoreType.DMA((4,))],
        compiler_params=kernel_params(0),
    )(tokens, *shards, gain, shuffle_matrix())


def backward_attention(grad_att, parts, head_out, lse, grad_up, grad_down, unshuffle):
    low = jnp.bfloat16
    return pl.pallas_call(
        backward_kernel,
        name="backward_attention",
        out_shape=[
            low_array(3, HEADS, HEAD_DIM, 256),
            wide_array(SLOT, WIDTH),
            wide_array(SLOT, WIDTH),
        ],
        in_specs=vmem_specs(7),
        out_specs=vmem_specs(3),
        scratch_shapes=[
            pltpu.VMEM((MEMBERS, 1, HEAD_DIM, 256), low),
            pltpu.VMEM((MEMBERS, 3, HEAD_DIM, 256), low),
            pltpu.VMEM((TILES, HEAD_DIM, TILE), jnp.float32),
            pltpu.VMEM((TILES, 1, TILE), jnp.float32),
            pltpu.VMEM((2, 2, 4, 4, 4, SLOT, WIDTH), low),
            pltpu.VMEM((2, 4, SLOT, WIDTH), low),
        ]
        + landing_scratch(2, SLOT)
        + sems(32)
        + sems(6)
        + sems(MEMBERS)
        + sems(MEMBERS),
        compiler_params=kernel_params(1),
    )(grad_att, parts, head_out, lse, grad_up, grad_down, unshuffle)


def reduce_projections(grad_qkv, grad_out, gain, unshuffle):
    low = jnp.bfloat16
    return pl.pallas_call(
        reduce_kernel,
        name="reduce_projections",
        out_shape=[wide_array(SLOT, WIDTH), wide_array(8, 768)],
        in_specs=vmem_specs(4),
        out_specs=vmem_specs(2),
        scratch_shapes=[
            pltpu.VMEM((3, 2, 4, 4, 4, 16, WIDTH), low),
            pltpu.VMEM((1, 4, SLOT, WIDTH), low),
        ]
        + landing_scratch(3, 16)
        + SMALL_SCRATCH
        + sems(48)
        + sems(3)
        + sems(10),
        compiler_params=kernel_params(2),
    )(grad_qkv, grad_out, gain, unshuffle)


def normalize(values):
    center = values - jnp.mean(values, axis=-1, keepdims=True)
    inv_std = lax.rsqrt(jnp.mean(center * center, axis=-1, keepdims=True) + epsilon)
    return (center * inv_std, inv_std)


def norm_back(upstream, gain_row, normed, inv_std):
    scaled = upstream * gain_row
    return inv_std * (
        scaled
        - jnp.mean(scaled, axis=-1, keepdims=True)
        - normed * jnp.mean(scaled * normed, axis=-1, keepdims=True)
    )


def gelu_tanh(values):
    return jax.nn.gelu(values, approximate=True)


def multiply(form, left, right):
    return jnp.einsum(form, left, right, preferred_element_type=jnp.float32)


def per_device(tokens, cotangent, w_qkv, w_out, w_up, w_down, norm_gains):
    low = jnp.bfloat16
    owner = lax.axis_index("dp") * lax.axis_size("ctx") + lax.axis_index("ctx")
    shards = (
        jnp.concatenate([w_qkv, w_out.T[None]], axis=0).reshape(SLOT, WIDTH),
        w_up.reshape(ROWS, 4, WIDTH).transpose(1, 0, 2).reshape(SLOT, WIDTH),
        w_down.reshape(4, WIDTH, ROWS).transpose(0, 2, 1).reshape(SLOT, WIDTH),
    )
    gain_part = lax.dynamic_update_slice(
        jnp.zeros((8, 768), jnp.float32),
        0.5 * norm_gains.astype(jnp.float32),
        (jnp.int32(0), owner * ROWS),
    )
    (
        normed_one, inv_one, first_in, parts, head_out, lse, attended, gains, qkv, out, up, down
    ) = forward_attention(tokens, shards, gain_part)
    gain_one, gain_two = gains[0], gains[1]
    inputs = tokens.astype(jnp.float32)
    attended = attended.reshape(768, 256)
    middle = inputs + multiply("cb,dc->bd", attended, out)
    normed_two, inv_two = normalize(middle)
    second_in = (normed_two * gain_two).astype(low)
    hidden = multiply("bd,df->bf", second_in, up)
    activated, gelu_pull = jax.vjp(gelu_tanh, hidden)
    act_low = activated.astype(low)
    result = (middle + multiply("bf,df->bd", act_low, down)).astype(low)
    grad_down = multiply("bd,bf->df", cotangent, act_low).astype(low)
    grad_act = multiply("bd,df->bf", cotangent, down)
    grad_hidden = gelu_pull(grad_act)[0].astype(low)
    grad_up = multiply("bd,bf->df", second_in, grad_hidden).astype(low)
    grad_second = multiply("bf,df->bd", grad_hidden, up)
    grad_middle = cotangent.astype(jnp.float32) + norm_back(
        grad_second, gain_two, normed_two, inv_two
    )
    gain_two_term = jnp.sum(grad_second * normed_two, axis=0)
    mid_low = grad_middle.astype(low)
    grad_out = multiply("bd,cb->dc", mid_low, attended).astype(low)
    grad_att = multiply("bd,dc->cb", mid_low, out).astype(low).reshape(1, HEADS, HEAD_DIM, 256)
    unshuffle = unshuffle_matrix()
    grad_projected, sum_b, sum_c = backward_attention(
        grad_att, parts, head_out, lse, grad_up, grad_down, unshuffle
    )
    grad_projected = grad_projected.reshape(2304, 256)
    grad_qkv = multiply("bd,cb->dc", first_in, grad_projected).astype(low)
    grad_first = multiply("cb,dc->bd", grad_projected, qkv)
    grad_tokens = grad_middle + norm_back(grad_first, gain_one, normed_one, inv_one)
    gain_one_term = jnp.sum(grad_first * normed_one, axis=0)
    gain_terms = jnp.concatenate(
        [gain_one_term[None], gain_two_term[None], jnp.zeros((6, 768), jnp.float32)]
    )
    sum_a, gain_sum = reduce_projections(grad_qkv, grad_out, gain_terms, unshuffle)
    sum_a = sum_a.reshape(4, ROWS, WIDTH)
    return (
        result,
        grad_tokens,
        sum_a[:3],
        sum_a[3].T,
        sum_b.reshape(4, ROWS, WIDTH).transpose(1, 0, 2).reshape(ROWS, 4 * WIDTH),
        sum_c.reshape(4, ROWS, WIDTH).transpose(0, 2, 1).reshape(4 * WIDTH, ROWS),
        lax.dynamic_slice(gain_sum, (jnp.int32(0), owner * ROWS), (2, ROWS)),
    )


def solution(mesh):
    return jax.shard_map(
        per_device,
        mesh=mesh,
        in_specs=(
            P(("dp", "ctx", "tensor"), None),
            P(("dp", "ctx", "tensor"), None),
            P(None, ("dp", "ctx"), "tensor"),
            P("tensor", ("dp", "ctx")),
            P(("dp", "ctx"), "tensor"),
            P("tensor", ("dp", "ctx")),
            P(None, ("dp", "ctx")),
        ),
        out_specs=(
            P(("dp", "ctx", "tensor"), None),
            P(("dp", "ctx", "tensor"), None),
            P(None, ("dp", "ctx"), "tensor"),
            P("tensor", ("dp", "ctx")),
            P(("dp", "ctx"), "tensor"),
            P("tensor", ("dp", "ctx")),
            P(None, ("dp", "ctx")),
        ),
        check_vma=False,
    )
```

time: 1410 us -> 275 us (0.20)
  blocking collectives: 535 us -> 0 us
  waiting for transfers between devices: 273 us -> 0 us
  starting transfers between devices: 260 us -> 0 us
  Pallas kernels: 0 us -> 226 us
  other arithmetic: 118 us -> 4.86 us
  local copies, waits for them, and re-layouts: 90.5 us -> 11.5 us
  matrix products: 109 us -> 30.6 us
  between operations: 17.2 us -> 0.97 us
    unnamed x2 -> x0, blocking collectives: 311 us -> none
    pallas_call x0 -> x3, Pallas kernels: none -> 226 us  [the longest x1 100 us: forward_attention(): pl.pallas_call(forward_kernel, name='forward_attention', out_shape=[wide_...]
    all_gather x6 -> x0, blocking collectives: 218 us -> none  [the longest x1 83.8 us: per_device(): lax.all_gather(norm_gains, ('dp', 'ctx'), axis=1, tiled=True)]
    ppermute x32 -> x0, starting transfers between devices: 140 us -> none  [the longest x16 75.7 us: from_behind(): return lax.ppermute(array, axis, pairs)]
    unnamed x49 -> x0, starting transfers between devices: 119 us -> none
    unnamed x59 -> x0, waiting for transfers between devices: 116 us -> none
    all_gather x5 -> x0, waiting for transfers between devices: 101 us -> none  [the longest x1 93.2 us: per_device(): lax.all_gather(w_up, ('dp', 'ctx'), axis=0, tiled=True)]
    dot_general x24 -> x11, matrix products: 109 us -> 30.6 us  [multiply(): return jnp.einsum(form, left, right, preferred_element_type=jnp.float32)]
  transfers between devices with their start and end apart: 90 -> 0, of which waited for: 13 -> 0; matrix products, arithmetic and copies ran while one was open for 28% -> 0% of each run, Pallas kernels for 0% -> 0%
where the time goes in v2:
time: 275 us; the launch traced here: 274 us
  Pallas kernels  226 us (82%)
  matrix products  30.6 us (11%)
  local copies, waits for them, and re-layouts  11.5 us (4%)
  other arithmetic  4.86 us (2%)
    pallas_call x1, Pallas kernels, forward_attention(): pl.pallas_call(forward_kernel, name='forward_attention', out_shape=[wide_...  100 us
    pallas_call x1, Pallas kernels, backward_attention(): pl.pallas_call(backward_kernel, name='backward_attention', out_shape=[low...  80.5 us
    pallas_call x1, Pallas kernels, reduce_projections(): pl.pallas_call(reduce_kernel, name='reduce_projections', out_shape=[wide_...  45.5 us
    dot_general x11, matrix products, multiply(): return jnp.einsum(form, left, right, preferred_element_type=jnp.float32)  30.6 us

profile of v2, /device:TPU:1, one launch (start us, length us, event | category | flops | bytes accessed | tf_op | source)
XLA Modules:
  0.0 274.2 jit_solution(1214282782877733918)
XLA Ops:
  1.9 0.8 reshape.83
  3.3 0.8 reshape.85
  4.8 0.8 pad_maximum_fusion
  6.2 100.4 %forward_attention.1 = (f32[256,768]{1,0:T(8,128)}, f32[256,1]{1,0:T(8,128)}, bf16[256,768]{1,0:T(8,128)(2,1)}, bf16[16,3,64,256]{3,2,1,0:T(8,128)(2,1)}, bf16[1...) custom-call(bf16[256,768]{1,0:T(8,128)(2,1)} %tokens.1, ...), custom_call_target="tpu_custom_call" | custom-call | tf_op jit(solution)/shard_map/forward_attention/pallas_call | solution.py:887
  106.6 1.0 reduce.1
  107.6 0.8 slice_reduce_fusion
  108.5 2.1 fusion.12
  110.8 4.0 %fusion.11 = f32[256,3072]{1,0:T(8,128)S(1)} fusion(bf16[768,3072]{1,0:T(8,128)(2,1)} %get-tuple-element.27, f32[256,768]{1,0:T(8,128)S(1)} %get-tuple-element.50, f32[768]{0:T(1024)S(1)} %get-tuple-element.48, f32[256]{0:T(256)S(1)} %add_rsqrt_fusion, f32[256]{0:T(256)S(1)} %broadcast_multiply_fusion.4), kind=kOutput, calls=%fused_computation.49 | convolution fusion | flops 1208745984 | bytes 8655872 | tf_op jit(solution)/shard_map/bd,df->bf/dot_general | solution.py:999
  114.8 2.8 %fusion.8 = bf16[256,768]{1,0:T(8,128)(2,1)} fusion(f32[256,768]{1,0:T(8,128)S(1)} %get-tuple-element.50, bf16[768,3072]{1,0:T(8,128)(2,1)S(1)} %bitcast.68, f32[256,3072]{1,0:T(8,128)S(1)} %fusion.11), kind=kOutput, calls=%fused_computation.18 | convolution fusion | flops 1215430656 | bytes 9043968 | tf_op jit(solution)/shard_map/bf,df->bd/dot_general | solution.py:999
  117.6 3.2 %fusion.7 = bf16[256,3072]{1,0:T(8,128)(2,1)S(1)} fusion(f32[256,3072]{1,0:T(8,128)S(1)} %fusion.11, bf16[256,768]{1,0:T(8,128)(2,1)S(1)} %copy-done.5, bf16[768,3072]{1,0:T(8,128)(2,1)S(1)} %bitcast.68), kind=kOutput, calls=%fused_computation.13 | convolution fusion | flops 1223688192 | bytes 9830400 | tf_op jit(solution)/shard_map/bd,df->bf/dot_general | solution.py:999
  120.8 1.8 multiply_reduce_fusion
  122.9 0.9 copy-done
  123.9 1.3 convolution_convert_fusion.4
  125.1 1.6 convolution_convert_fusion.3.grad_out
  126.7 3.8 %fusion.grad_down = bf16[768,3072]{1,0:T(8,128)(2,1)} fusion(bf16[256,768]{1,0:T(8,128)(2,1)S(1)} %copy-done.5, f32[256,3072]{1,0:T(8,128)S(1)} %fusion.11), kind=kOutput, calls=%fused_computation.5 | convolution fusion | flops 1217396736 | bytes 8257536 | tf_op jit(solution)/shard_map/bd,bf->df/dot_general | solution.py:999
  130.5 3.7 %convolution_convert_fusion.2.grad_up = bf16[768,3072]{1,0:T(8,128)(2,1)} fusion(bf16[256,3072]{1,0:T(8,128)(2,1)S(1)} %fusion.7, f32[256,768]{1,0:T(8,128)S(1)} %get-tuple-element.50, f32[768]{0:T(1024)S(1)} %get-tuple-element.48, f32[256]{0:T(256)S(1)} %add_rsqrt_fusion, f32[256]{0:T(256)S(1)} %broadcast_multiply_fusion.4), kind=kOutput, calls=%fused_computation.2 | convolution fusion | flops 1211105280 | bytes 7083008 | tf_op jit(solution)/shard_map/bd,bf->df/dot_general | solution.py:999
  134.2 80.5 %backward_attention.1 = (bf16[3,12,64,256]{3,2,1,0:T(8,128)(2,1)}, f32[48,384]{1,0:T(8,128)}, f32[48,384]{1,0:T(8,128)}) custom-call(bf16[1,12,64,256]{3,2,1,0:T(8,128)(2,1)} %bitcast.50, bf16[16,3,64,256]{3,2,1,0:T(8,128)(2,1)} %get-tuple-element.30.parts, bf16[16,1,64,256]{3,2,1,0:T(8,128)(2,1)} %get-tuple-element.31.head_out, ...), custom_call_target="tpu_custom_call" | custom-call | tf_op jit(solution)/shard_map/backward_attention/pallas_call | solution.py:931
  214.7 3.6 %multiply_reduce_fusion.1 = (f32[768]{0:T(1024)S(1)}, f32[256]{0:T(256)S(1)}, f32[256]{0:T(256)S(1)}, f32[256,768]{1,0:T(8,128)S(1)}) fusion(f32[256,768]{1,0:T(8,128)S(1)} %copy-done.4, f32[768]{0:T(1024)S(1)} %get-tuple-element.47, bf16[2304,256]{1,0:T(8,128)(2,1)} %bitcast.53, bf16[768,2304]{1,0:T(8,128)(2,1)} %get-tuple-element.34), kind=kOutput, calls=%fused_computation.21 | convolution fusion | flops 907148032 | bytes 6299648 | tf_op jit(solution)/shard_map/cb,dc->bd/dot_general | solution.py:999
  218.4 1.1 multiply_add_fusion
  221.7 2.9 %convolution_convert_fusion.grad_qkv = bf16[768,2304]{1,0:T(8,128)(2,1)} fusion(bf16[256,768]{1,0:T(8,128)(2,1)S(1)} %copy-done.3, bf16[2304,256]{1,0:T(8,128)(2,1)S(1)} %bitcast.54), kind=kOutput, calls=%fused_computation | convolution fusion | flops 907739136 | bytes 5111808 | tf_op jit(solution)/shard_map/bd,cb->dc/dot_general | solution.py:999
  224.6 45.5 %reduce_projections.1 = (f32[48,384]{1,0:T(8,128)}, f32[8,768]{1,0:T(8,128)}) custom-call(bf16[768,2304]{1,0:T(8,128)(2,1)} %convolution_convert_fusion.grad_qkv, bf16[768,768]{1,0:T(8,128)(2,1)} %convolution_convert_fusion.3.grad_out, f32[8,768]{1,0:T(8,128)} %maximum_maximum_fusion.gain, bf16[4,48,192]{2,1,0:T(8,128)(2,1)} %constant.47.clone.shuffle.unshuffle), custom_call_target="tpu_custom_call" | custom-call | tf_op jit(solution)/shard_map/reduce_projections/pallas_call | solution.py:960
  270.1 1.3 constant_dynamic-slice_fusion
  271.4 1.3 slice_bitcast_fusion
  272.7 0.8 slice.18
  (56 shorter events, 6.5 us)
Async XLA Ops:
  1.9 4.4 %copy-start.6 = (f32[8,768]{1,0:T(8,128)}, f32[8,768]{1,0:T(8,128)S(1)}, u32[]{:S(2)}) copy-start(f32[8,768]{1,0:T(8,128)S(1)} %dynamic_update_slice.3.gain) | copy-start | bytes 73732
  110.6 4.2 %slice-start.2 = ((s8[4718592]{0:T(1024)(128)(4,1)}), s8[4194304]{0:T(1024)(128)(4,1)S(1)}, s32[]{:S(2)}) async-start(s8[4718592]{0:T(1024)(128)(4,1)} %bitcast.67), calls=%async_computation.2 | async-start | bytes 8388608
  110.8 4.0 %slice-start.3 = ((s8[4718592]{0:T(1024)(128)(4,1)}), s8[524288]{0:T(1024)(128)(4,1)S(1)}, s32[]{:S(2)}) async-start(s8[4718592]{0:T(1024)(128)(4,1)} %bitcast.67), calls=%async_computation.3 | async-start | bytes 1048576
  114.8 2.8 %copy-start.5 = (bf16[256,768]{1,0:T(8,128)(2,1)S(1)}, bf16[256,768]{1,0:T(8,128)(2,1)}, u32[]{:S(2)}) copy-start(bf16[256,768]{1,0:T(8,128)(2,1)} %param.10) | copy-start | bytes 1179652
  114.8 6.0 %slice-start = ((s8[4718592]{0:T(1024)(128)(4,1)}), s8[4194304]{0:T(1024)(128)(4,1)S(1)}, s32[]{:S(2)}) async-start(s8[4718592]{0:T(1024)(128)(4,1)} %bitcast.65), calls=%async_computation | async-start | bytes 8388608
  117.6 3.2 %slice-start.1 = ((s8[4718592]{0:T(1024)(128)(4,1)}), s8[524288]{0:T(1024)(128)(4,1)S(1)}, s32[]{:S(2)}) async-start(s8[4718592]{0:T(1024)(128)(4,1)} %bitcast.65), calls=%async_computation.1 | async-start | bytes 1048576
  122.6 1.3 copy-start
  122.6 2.6 copy-start.1
  134.2 80.5 %copy-start.4 = (f32[256,768]{1,0:T(8,128)S(1)}, f32[256,768]{1,0:T(8,128)}, u32[]{:S(2)}) copy-start(f32[256,768]{1,0:T(8,128)} %get-tuple-element.35) | copy-start | bytes 2359300
  218.3 1.9 copy-start.8
  218.3 2.6 copy-start.7
  218.3 3.3 %copy-start.2 = (bf16[3,12,64,256]{3,2,1,0:T(8,128)(2,1)S(1)}, bf16[3,12,64,256]{3,2,1,0:T(8,128)(2,1)}, u32[]{:S(2)}) copy-start(bf16[3,12,64,256]{3,2,1,0:T(8,128)(2,1)} %get-tuple-element.33) | copy-start | bytes 3538948
  218.4 3.3 %copy-start.3 = (bf16[256,768]{1,0:T(8,128)(2,1)S(1)}, bf16[256,768]{1,0:T(8,128)(2,1)}, u32[]{:S(2)}) copy-start(bf16[256,768]{1,0:T(8,128)(2,1)} %get-tuple-element.36) | copy-start | bytes 1179652

commit v3 on v2

--- a/solution.py
+++ b/solution.py
@@ -169,45 +169,29 @@
         super().__init__(pos, order, unit, send, recv, started)
         self.held = held
 
-    def halves(self, stage, which):
-        return () if stage == 0 else (pl.ds(2 * which, 2),)
-
     def pass_on(self, index, sem, device):
         self.move(self.held.at[index], self.held.at[index], sem, device)
 
     def begin(self, stage):
-        for side, by in ((0, 1), (1, 3)):
-            self.pass_on(self.at(stage, 0), stage * 4 + side, self.along(stage, by))
+        for by in (1, 3, 2):
+            self.pass_on(self.at(stage, 0), stage * 3 + by - 1, self.along(stage, by))
         if stage == 2:
-            self.share(0, 12)
-
-    def relay(self, stage):
-        for side, by, back in ((0, 1, 3), (1, 3, 1)):
-            block = self.at(stage, back)
-            self.arrived(self.held.at[block], stage * 4 + side)
-            if stage > 0 or side == 0:
-                self.pass_on(
-                    block + self.halves(stage, side), stage * 4 + 2 + side, self.along(stage, by)
-                )
+            self.share(0)
+
+    def finish(self, stage):
+        for by in (1, 3, 2):
+            self.arrived(self.held.at[self.at(stage, 4 - by)], stage * 3 + by - 1)
             if stage == 2:
-                self.share(back, 13 + side)
-
-    def finish(self, stage):
-        for side in range(2):
-            if stage > 0 or side == 0:
-                block = self.at(stage, 2) + self.halves(stage, side)
-                self.arrived(self.held.at[block], stage * 4 + 2 + side)
-        if stage == 2:
-            self.share(2, 15)
-
-    def share(self, by, sem):
-        self.pass_on(self.at(2, by), sem, self.sibling)
+                self.share(4 - by)
+
+    def share(self, by):
+        self.pass_on(self.at(2, by), 9 + by, self.sibling)
 
     def settle(self):
         place3 = self.pos[self.order[2]]
-        for by, sem in ((0, 12), (3, 13), (1, 14), (2, 15)):
+        for by in (0, 3, 1, 2):
             index = (self.unit, 1 - self.pos["c"], (place3 + by) % 4)
-            self.arrived(self.held.at[index], sem)
+            self.arrived(self.held.at[index], 9 + by)
 
 
 def wide(value):
@@ -217,96 +201,62 @@
 class Reduce(Unit):
     def __init__(self, pos, order, unit, held, landing, send, recv, started):
         super().__init__(pos, order, unit, send, recv, started)
-        self.held = held
-        self.cores, self.halves3, self.fulls3, self.halves2, self.fulls2, self.half1, self.fulls1 = (
-            landing
-        )
+        self.held, self.cores, self.coming = held, landing[0], landing[1:]
 
     def add(self, index, sources, *counts):
         held = self.held
-        if not counts:
-            total = wide(held[index])
-            for source, at in sources:
-                total = total + wide(source[at])
-            held[index] = total.astype(jnp.bfloat16)
-            return
-
-        def body(i, carry):
-            slot = (i // counts[1], i % counts[1]) if len(counts) == 2 else (i,)
+
+        def one(slot):
             total = wide(held[index + slot])
             for source, at in sources:
                 total = total + wide(source[at + slot])
             held[index + slot] = total.astype(jnp.bfloat16)
+
+        def body(i, carry):
+            one((i // 4, i % 4) if len(counts) == 2 else (i,))
             return carry
 
-        lax.fori_loop(0, counts[0] * counts[-1] if len(counts) == 2 else counts[0], body, 0)
+        if counts:
+            lax.fori_loop(0, 4 ** len(counts), body, 0)
+        else:
+            one(())
 
     def cross(self):
         place3, u = self.pos[self.order[2]], self.unit
-        for by, sem in ((2, 12), (1, 13), (3, 14), (0, 15)):
+        for by in (1, 3, 2, 0):
             index = (place3 + by) % 4
             self.move(
-                self.held.at[u, 1 - self.pos["c"], index], self.cores.at[u, index], sem, self.sibling
+                self.held.at[u, 1 - self.pos["c"], index],
+                self.cores.at[u, index],
+                9 + by,
+                self.sibling,
             )
 
-    def take_core(self, by, sem):
+    def take_core(self, by):
         index = (self.pos[self.order[2]] + by) % 4
-        self.arrived(self.cores.at[self.unit, index], sem)
+        self.arrived(self.cores.at[self.unit, index], 9 + by)
         self.add(self.at(2, by), [(self.cores, (self.unit, index))], 4, 4)
 
     def begin(self, stage):
-        u = self.unit
-        if stage == 2:
-            self.take_core(2, 12)
-        if stage == 0:
-            self.move(self.held.at[self.at(0, 2)], self.half1.at[u], 8, self.along(0, 1))
-            self.move(self.held.at[self.at(0, 3)], self.fulls1.at[u, 1], 11, self.along(0, 3))
-            return
-        landing = self.halves3 if stage == 2 else self.halves2
-        for side, by in ((0, 1), (1, 3)):
+        for by in (1, 3, 2):
+            if stage == 2:
+                self.take_core(by)
             self.move(
-                self.held.at[self.at(stage, 2) + (pl.ds(2 * side, 2),)],
-                landing.at[u, side],
-                (2 - stage) * 4 + side,
+                self.held.at[self.at(stage, by)],
+                self.coming[stage].at[self.unit, by - 1],
+                stage * 3 + by - 1,
                 self.along(stage, by),
             )
+
+    def finish(self, stage):
         if stage == 2:
-            self.take_core(1, 13)
-            self.take_core(3, 14)
-
-    def relay(self, stage):
-        u = self.unit
-        if stage == 0:
-            self.arrived(self.half1.at[u], 8)
-            self.add(self.at(0, 1), [(self.half1, (u,))])
-            self.move(self.held.at[self.at(0, 1)], self.fulls1.at[u, 0], 10, self.along(0, 1))
-            return
-        halves = self.halves3 if stage == 2 else self.halves2
-        fulls = self.fulls3 if stage == 2 else self.fulls2
-        base = (2 - stage) * 4
-        for side, by in ((0, 1), (1, 3)):
-            self.arrived(halves.at[u, side], base + side)
-            index = self.at(stage, by)
-            for row in range(2):
-                if stage == 2:
-                    self.add(index + (2 * side + row,), [(halves, (u, side, row))], 4)
-                else:
-                    self.add(index + (2 * side + row,), [(halves, (u, side, row))])
-            self.move(
-                self.held.at[index], fulls.at[u, side], base + 2 + side, self.along(stage, by)
-            )
-
-    def finish(self, stage):
-        u = self.unit
-        if stage == 2:
-            self.take_core(0, 15)
-        fulls = (self.fulls1, self.fulls2, self.fulls3)[stage]
-        for side in range(2):
-            self.arrived(fulls.at[u, side], (2 - stage) * 4 + 2 + side)
+            self.take_core(0)
+        for by in (1, 3, 2):
+            self.arrived(self.coming[stage].at[self.unit, by - 1], stage * 3 + by - 1)
         self.add(
             self.at(stage, 0),
-            [(fulls, (u, 0)), (fulls, (u, 1))],
-            *((), (4,), (4, 4))[stage],
+            [(self.coming[stage], (self.unit, i)) for i in range(3)],
+            *(4,) * stage,
         )
 
 
@@ -314,12 +264,9 @@
     low, slot = jnp.bfloat16, (rows, WIDTH)
     return [
         pltpu.VMEM((units, 4, 4, 4) + slot, low),
-        pltpu.VMEM((units, 2, 2, 4) + slot, low),
-        pltpu.VMEM((units, 2, 4, 4) + slot, low),
-        pltpu.VMEM((units, 2, 2) + slot, low),
-        pltpu.VMEM((units, 2, 4) + slot, low),
-        pltpu.VMEM((units,) + slot, low),
-        pltpu.VMEM((units, 2) + slot, low),
+        pltpu.VMEM((units, 3) + slot, low),
+        pltpu.VMEM((units, 3, 4) + slot, low),
+        pltpu.VMEM((units, 3, 4, 4) + slot, low),
     ]
 
 
@@ -337,34 +284,46 @@
     return (0, (piece * 2 + tensor) * WIDTH) if piece < 3 else (1, tensor * WIDTH)
 
 
-def copy_thirds(thirds, whole, to_whole):
+def copy_thirds(thirds, whole):
     def body(group, carry):
         for tensor, piece, indices in slots_of(group, THIRDS):
             which, column = column_of(tensor, piece)
             for third, index in enumerate(indices):
                 rows = pl.ds(pl.multiple_of(group * SLOT + 16 * third, 16), 16)
-                if to_whole:
-                    whole[which][rows, pl.ds(column, WIDTH)] = thirds[(third,) + index]
-                else:
-                    thirds[(third,) + index] = whole[which][rows, pl.ds(column, WIDTH)]
+                whole[which][rows, pl.ds(column, WIDTH)] = thirds[(third,) + index]
         return carry
 
     lax.fori_loop(0, 16, body, 0)
 
 
-def copy_wholes(slots, whole, to_whole):
+def copy_wholes(slots, whole):
     def body(group, carry):
         rows = pl.ds(pl.multiple_of(group * SLOT, SLOT), SLOT)
         for tensor, piece, indices in slots_of(group, WHOLES):
             columns = pl.ds((tensor * 4 + piece) * WIDTH, WIDTH)
             for k, index in enumerate(indices):
-                if to_whole:
-                    whole[k][rows, columns] = slots[(k,) + index]
-                else:
-                    slots[(k,) + index] = whole[k][rows, columns]
+                whole[k][rows, columns] = slots[(k,) + index]
         return carry
 
     lax.fori_loop(0, 16, body, 0)
+
+
+def slot_index(order, group, tensor, piece):
+    at = dict(x=group // 4, z=2 * tensor + (group // 2) % 2, y=2 * (group % 2) + piece // 2)
+    return (piece % 2, at[order[2]], at[order[1]], at[order[0]])
+
+
+def fill_thirds(thirds, tensor, piece, value):
+    for group in range(16):
+        for third, order in enumerate(THIRDS):
+            row = group * SLOT + 16 * third
+            thirds[(third,) + slot_index(order, group, tensor, piece)] = value[row : row + 16]
+
+
+def fill_wholes(slots, k, tensor, piece, value):
+    for group in range(16):
+        row = group * SLOT
+        slots[(k,) + slot_index(WHOLES[k], group, tensor, piece)] = value[row : row + SLOT]
 
 
 def head_place(head):
@@ -551,11 +510,35 @@
     lse[i] = top + jnp.log(total)
 
 
+def norm_parts(values):
+    center = values - jnp.mean(values, axis=-1, keepdims=True)
+    inv_std = lax.rsqrt(jnp.mean(center * center, axis=-1, keepdims=True) + epsilon)
+    return center * inv_std, inv_std
+
+
+def norm_back(upstream, gain_row, normed, inv_std):
+    scaled = upstream * gain_row
+    return inv_std * (
+        scaled
+        - jnp.mean(scaled, axis=-1, keepdims=True)
+        - normed * jnp.mean(scaled * normed, axis=-1, keepdims=True)
+    )
+
+
+def gelu_and_slope(v):
+    scale, cubic = (2.0 / np.pi) ** 0.5, 0.044715
+    square = v * v
+    bend = jnp.tanh(scale * v * (1.0 + cubic * square))
+    half = 0.5 * (1.0 + bend)
+    slope = half + (0.5 * scale) * v * (1.0 - bend * bend) * (1.0 + 3.0 * cubic * square)
+    return v * half, slope
+
+
 def forward_kernel(
-    tokens, a, b, c, gain, shuffle,
+    tokens, cotangent, a, b, c, gain, shuffle,
     normed_out, inv_out, first_out, parts, head_out, lse, attended, gain_out,
-    w_qkv, w_out, w_up, w_down,
-    pre, thirds, wholes, qkv, out, up, down, projected, keys, ring, pair,
+    result, second_out, act_out, hid_out, middle_grad, grad_att, gain_two_out, w_qkv,
+    pre, thirds, wholes, qkv, out, up, down, projected, keys, ring, pair, forth_sum, back_sum,
     third_send, third_recv, whole_send, whole_recv, pre_send, pre_recv, small_send, small_recv,
     to_send, to_recv, from_send, from_recv, write_sem,
 ):
@@ -590,41 +573,30 @@
         unit.begin(0)
     for u, unit in enumerate(later):
         wholes[unit.at(0, 0)] = sorted_piece(1 + u)
-    values = tokens[...].astype(jnp.float32)
-    center = values - jnp.mean(values, axis=-1, keepdims=True)
-    inv_std = lax.rsqrt(jnp.mean(center * center, axis=-1, keepdims=True) + epsilon)
-    normed_out[...] = center * inv_std
-    inv_out[...] = inv_std
+    normed_one, inv_one = norm_parts(wide(tokens[...]))
+    normed_out[...] = normed_one
+    inv_out[...] = inv_one
     for stage in range(3):
         for unit in first:
-            unit.relay(stage)
-        if stage == 1:
-            for unit in later:
-                unit.begin(0)
-        for unit in first:
             unit.finish(stage)
-        if stage < 2:
-            for unit in first:
+            if stage < 2:
                 unit.begin(stage + 1)
         total = small.finish(stage)
         if stage < 2:
             small.start(stage + 1, total)
         else:
             small.start_pair(total)
-    for unit in later:
-        unit.relay(0)
+        if stage == 1:
+            for unit in later:
+                unit.begin(0)
     for unit in later:
         unit.finish(0)
         unit.begin(1)
     for unit in first:
         unit.settle()
-    copy_thirds(thirds, (qkv, out), True)
-    writes = [
-        pltpu.make_async_copy(src, dst, write_sem.at[n])
-        for n, (src, dst) in enumerate(((qkv, w_qkv), (out, w_out), (up, w_up), (down, w_down)))
-    ]
-    writes[0].start()
-    writes[1].start()
+    copy_thirds(thirds, (qkv, out))
+    write = pltpu.make_async_copy(qkv, w_qkv, write_sem)
+    write.start()
     gains = small.finish_pair()
     gain_out[...] = gains
     first_in = (normed_out[...] * gains[0:1]).astype(jnp.bfloat16)
@@ -637,8 +609,6 @@
                 projected[part, tensor * 6 + head] = cols[head * HEAD_DIM : (head + 1) * HEAD_DIM]
     spread.start()
     for unit in later:
-        unit.relay(1)
-    for unit in later:
         unit.finish(1)
         unit.begin(2)
 
@@ -652,19 +622,44 @@
 
         return carry
 
-    lax.fori_loop(0, 5, per_queries, 0)
-    for unit in later:
-        unit.relay(2)
-    lax.fori_loop(5, 7, per_queries, 0)
+    lax.fori_loop(0, 7, per_queries, 0)
     for unit in later:
         unit.finish(2)
     lax.fori_loop(7, 8, per_queries, 0)
     for unit in later:
         unit.settle()
-    copy_wholes(wholes, (up, down), True)
-    writes[2].start()
-    writes[3].start()
+    copy_wholes(wholes, (up, down))
     back.wait()
+    weighted = jnp.transpose(dot(out[...], attended[0].reshape(768, 256)))
+    middle = wide(tokens[...]) + weighted
+    normed_two, inv_two = norm_parts(middle)
+    second_in = (normed_two * gain_out[1:2]).astype(jnp.bfloat16)
+    second_out[...] = second_in
+    forth_sum[...] = middle
+    back_sum[...] = jnp.zeros_like(back_sum)
+
+    def feed(p, carry):
+        columns = pl.ds(pl.multiple_of(p * 768, 768), 768)
+        act, slope = gelu_and_slope(dot(second_out[...], up[:, columns]))
+        act = act.astype(jnp.bfloat16)
+        act_out[:, columns] = act
+        hid = (dot(cotangent[...], down[:, columns]) * slope).astype(jnp.bfloat16)
+        hid_out[:, columns] = hid
+        forth_sum[...] += dot_right(act, down[:, columns])
+        back_sum[...] += dot_right(hid, up[:, columns])
+        return carry
+
+    lax.fori_loop(0, 4, feed, 0)
+    result[...] = forth_sum[...].astype(jnp.bfloat16)
+    grad_second = back_sum[...]
+    gain_two_out[...] = jnp.sum(grad_second * normed_two, axis=0, keepdims=True)
+    grad_middle = wide(cotangent[...]) + norm_back(
+        grad_second, gain_out[1:2], normed_two, inv_two
+    )
+    middle_grad[...] = grad_middle
+    grads = jnp.transpose(dot(grad_middle.astype(jnp.bfloat16), out[...])).astype(jnp.bfloat16)
+    for head in range(HEADS):
+        grad_att[0, head] = grads[head * HEAD_DIM : (head + 1) * HEAD_DIM]
     spread.sent()
 
     @pl.when(active)
@@ -675,8 +670,7 @@
         group.sent(pre, k)
     for copy in started:
         copy.wait_send()
-    for write in writes:
-        write.wait()
+    write.wait()
 
 
 def back_tile(j, parts, grad_att, lse, delta, query_sum, out):
@@ -707,28 +701,77 @@
 
 
 def backward_kernel(
-    grad_att, parts, head_out, lse, grad_up, grad_down, unshuffle,
-    grad_projected, out_b, out_c,
-    head_grad, head_back, query_sum, delta, wholes, post,
-    cores, halves3, fulls3, halves2, fulls2, half1, fulls1,
-    whole_send, whole_recv, post_send, post_recv, to_send, to_recv, from_send, from_recv,
+    grad_att, unshuffle, gain, gain_two, inv_one, lse_in, parts_in, head_out_in, act_in, hid_in,
+    second_in, cot_in, middle_in, attended_in, first_in, normed_in, w_qkv_in,
+    grad_tokens, out_a, out_b, out_c, gain_out,
+    lse, parts, head_out, act, hid, second, cot, middle, attended, first, normed, w_qkv,
+    turned_in, grad_projected, head_grad, head_back, query_sum, delta, wholes, thirds, post,
+    cores_w, ends1_w, ends2_w, ends3_w, cores_t, ends1_t, ends2_t, ends3_t, ring, pair,
+    load_sem, whole_send, whole_recv, third_send, third_recv, post_send, post_recv,
+    small_send, small_recv, to_send, to_recv, from_send, from_recv,
 ):
     pos = place()
     active = own_head(lax.axis_index("ctx"), lax.axis_index("tensor"))[1]
     group = Group(pos, post_send, post_recv)
+    small = SmallSum(pos, ring, pair, small_send, small_recv)
     started = []
-    landing = (cores, halves3, fulls3, halves2, fulls2, half1, fulls1)
     units = [
-        Reduce(pos, order, u, wholes, landing, whole_send, whole_recv, started)
+        Reduce(
+            pos, order, u, wholes, (cores_w, ends1_w, ends2_w, ends3_w), whole_send, whole_recv,
+            started,
+        )
         for u, order in enumerate(WHOLES)
+    ]
+    last = [
+        Reduce(
+            pos, order, u, thirds, (cores_t, ends1_t, ends2_t, ends3_t), third_send, third_recv,
+            started,
+        )
+        for u, order in enumerate(THIRDS)
     ]
     spread = ToHeads(grad_att, head_grad, to_send, to_recv)
     back = FromHeads(head_back, grad_projected, from_send, from_recv)
+    loads = [
+        pltpu.make_async_copy(src, dst, load_sem.at[n])
+        for n, (src, dst) in enumerate(
+            (
+                (cot_in, cot), (act_in, act), (second_in, second), (hid_in, hid),
+                (middle_in, middle), (attended_in, attended), (lse_in, lse), (parts_in, parts),
+                (head_out_in, head_out), (first_in, first), (normed_in, normed),
+                (w_qkv_in, w_qkv),
+            )
+        )
+    ]
+    for load in loads:
+        load.start()
     greet(pos)
     spread.start()
-    copy_wholes(wholes, (grad_up, grad_down), False)
+    for load in loads[:4]:
+        load.wait()
+
+    def flip(n, value):
+        turned_in[n] = jnp.transpose(value).astype(jnp.bfloat16)
+
+    flip(0, wide(cot[...]))
+    flip(1, wide(second[...]))
+
+    def feed(p, carry):
+        columns = pl.ds(pl.multiple_of(p * WIDTH, WIDTH), WIDTH)
+        for k, (left, right) in enumerate(((1, hid), (0, act))):
+            value = dot(turned_in[left], right[:, columns]).astype(jnp.bfloat16)
+            fill_wholes(wholes, k, p // 4, p % 4, value)
+        return carry
+
+    lax.fori_loop(0, 8, feed, 0)
     for unit in units:
         unit.cross()
+    for load in loads[4:]:
+        load.wait()
+    flip(0, middle[...])
+    flip(1, wide(first[...]))
+    for tensor in range(2):
+        rows = attended[0, 6 * tensor : 6 * (tensor + 1)].reshape(WIDTH, 256)
+        fill_thirds(thirds, tensor, 3, dot_right(turned_in[0], rows).astype(jnp.bfloat16))
     for unit in units:
         unit.begin(2)
 
@@ -754,80 +797,63 @@
 
         return carry
 
-    lax.fori_loop(0, 1, per_keys, 0)
-    for unit in units:
-        unit.relay(2)
-    lax.fori_loop(1, 3, per_keys, 0)
+    lax.fori_loop(0, 2, per_keys, 0)
     for unit in units:
         unit.finish(2)
         unit.begin(1)
-    lax.fori_loop(3, 4, per_keys, 0)
-    for unit in units:
-        unit.relay(1)
-    lax.fori_loop(4, 5, per_keys, 0)
+    lax.fori_loop(2, 4, per_keys, 0)
     for unit in units:
         unit.finish(1)
         unit.begin(0)
-    lax.fori_loop(5, 6, per_keys, 0)
-    for unit in units:
-        unit.relay(0)
-    lax.fori_loop(6, 7, per_keys, 0)
+    lax.fori_loop(4, 6, per_keys, 0)
     for u, unit in enumerate(units):
         unit.finish(0)
         post[u, group.member] = wholes[unit.at(0, 0)]
         group.start(post, u)
-    lax.fori_loop(7, 8, per_keys, 0)
+    lax.fori_loop(6, 8, per_keys, 0)
+    back.wait()
+
+    def project(p, carry):
+        part, tensor = p // 2, p % 2
+        rows = grad_projected[part, pl.ds(6 * tensor, 6)].reshape(WIDTH, 256)
+        fill_thirds(thirds, tensor, part, dot_right(turned_in[1], rows).astype(jnp.bfloat16))
+        return carry
+
+    lax.fori_loop(0, 6, project, 0)
+    for unit in last:
+        unit.cross()
+    grad_first = jnp.transpose(dot(w_qkv[...], grad_projected[...].reshape(2304, 256)))
+    term = jnp.sum(grad_first * normed[...], axis=0, keepdims=True)
+    row = lax.broadcasted_iota(jnp.int32, (8, 768), 0)
+    small.start(0, jnp.where(row == 0, term, jnp.where(row == 1, gain_two[...], 0.0)))
+    for unit in last:
+        unit.begin(2)
+    grad_tokens[...] = middle[...] + norm_back(grad_first, gain[0:1], normed[...], inv_one[...])
     for u, out in enumerate((out_b, out_c)):
         out[...] = dot(unshuffle[group.member], group.finish(post, u))
-        group.sent(post, u)
-    back.wait()
-    spread.sent()
-
-    @pl.when(active)
-    def _():
-        back.sent()
-
-    for copy in started:
-        copy.wait_send()
-
-
-def reduce_kernel(
-    grad_qkv, grad_out, gain, unshuffle, out_a, gain_out,
-    thirds, post, cores, halves3, fulls3, halves2, fulls2, half1, fulls1, ring, pair,
-    third_send, third_recv, post_send, post_recv, small_send, small_recv,
-):
-    pos = place()
-    group = Group(pos, post_send, post_recv)
-    small = SmallSum(pos, ring, pair, small_send, small_recv)
-    started = []
-    landing = (cores, halves3, fulls3, halves2, fulls2, half1, fulls1)
-    units = [
-        Reduce(pos, order, u, thirds, landing, third_send, third_recv, started)
-        for u, order in enumerate(THIRDS)
-    ]
-    copy_thirds(thirds, (grad_qkv, grad_out), False)
-    greet(pos)
-    for unit in units:
-        unit.cross()
-    small.start(0, gain[...])
     for stage in (2, 1, 0):
-        for unit in units:
-            unit.begin(stage)
-        for unit in units:
-            unit.relay(stage)
         total = small.finish(2 - stage)
         if stage > 0:
             small.start(3 - stage, total)
         else:
             small.start_pair(total)
-        for unit in units:
+        for unit in last:
             unit.finish(stage)
-    for u, unit in enumerate(units):
-        post[0, group.member, pl.ds(16 * u, 16)] = thirds[unit.at(0, 0)]
-    group.start(post, 0)
+            if stage > 0:
+                unit.begin(stage - 1)
+    for u, unit in enumerate(last):
+        post[2, group.member, pl.ds(16 * u, 16)] = thirds[unit.at(0, 0)]
+    group.start(post, 2)
     gain_out[...] = small.finish_pair()
-    out_a[...] = dot(unshuffle[group.member], group.finish(post, 0))
-    group.sent(post, 0)
+    out_a[...] = dot(unshuffle[group.member], group.finish(post, 2))
+    for k in range(3):
+        group.sent(post, k)
+    spread.sent()
+
+    @pl.when(active)
+    def _():
+        back.sent()
+
     for copy in started:
         copy.wait_send()
 
@@ -882,11 +908,11 @@
     )
 
 
-def forward_attention(tokens, shards, gain):
+def forward_pass(tokens, cotangent, shards, gain):
     low = jnp.bfloat16
     return pl.pallas_call(
         forward_kernel,
-        name="forward_attention",
+        name="forward_pass",
         out_shape=[
             wide_array(256, 768),
             wide_array(256, 1),
@@ -896,13 +922,17 @@
             wide_array(TILES, 1, TILE),
             low_array(1, HEADS, HEAD_DIM, 256),
             wide_array(8, 768),
+            low_array(256, 768),
+            low_array(256, 768),
+            low_array(256, 3072),
+            low_array(256, 3072),
+            wide_array(256, 768),
+            low_array(1, HEADS, HEAD_DIM, 256),
+            wide_array(1, 768),
             low_array(768, 2304),
-            low_array(768, 768),
-            low_array(768, 3072),
-            low_array(768, 3072),
         ],
-        in_specs=vmem_specs(6),
-        out_specs=vmem_specs(8) + any_specs(4),
+        in_specs=vmem_specs(7),
+        out_specs=vmem_specs(15) + any_specs(1),
         scratch_shapes=[
             pltpu.VMEM((3, 4, SLOT, WIDTH), low),
             pltpu.VMEM((3, 2, 4, 4, 4, 16, WIDTH), low),
@@ -915,92 +945,55 @@
             pltpu.VMEM((TILES * TILE, HEAD_DIM), low),
         ]
         + SMALL_SCRATCH
+        + [pltpu.VMEM((256, 768), jnp.float32)] * 2
         + sems(48)
         + sems(32)
         + sems(9)
         + sems(10)
         + sems(MEMBERS)
         + sems(MEMBERS)
-        + [pltpu.SemaphoreType.DMA((4,))],
+        + [pltpu.SemaphoreType.DMA],
         compiler_params=kernel_params(0),
-    )(tokens, *shards, gain, shuffle_matrix())
-
-
-def backward_attention(grad_att, parts, head_out, lse, grad_up, grad_down, unshuffle):
+    )(tokens, cotangent, *shards, gain, shuffle_matrix())
+
+
+def backward_pass(grad_att, gain, gain_two, inv_one, arrays):
     low = jnp.bfloat16
     return pl.pallas_call(
         backward_kernel,
-        name="backward_attention",
-        out_shape=[
-            low_array(3, HEADS, HEAD_DIM, 256),
-            wide_array(SLOT, WIDTH),
-            wide_array(SLOT, WIDTH),
-        ],
-        in_specs=vmem_specs(7),
-        out_specs=vmem_specs(3),
-        scratch_shapes=[
+        name="backward_pass",
+        out_shape=[wide_array(256, 768)]
+        + [wide_array(SLOT, WIDTH)] * 3
+        + [wide_array(8, 768)],
+        in_specs=any_specs(1) + vmem_specs(4) + any_specs(12),
+        out_specs=vmem_specs(5),
+        scratch_shapes=[pltpu.VMEM(array.shape, array.dtype) for array in arrays]
+        + [
+            pltpu.VMEM((2, 768, 256), low),
+            pltpu.VMEM((3, HEADS, HEAD_DIM, 256), low),
             pltpu.VMEM((MEMBERS, 1, HEAD_DIM, 256), low),
             pltpu.VMEM((MEMBERS, 3, HEAD_DIM, 256), low),
             pltpu.VMEM((TILES, HEAD_DIM, TILE), jnp.float32),
             pltpu.VMEM((TILES, 1, TILE), jnp.float32),
             pltpu.VMEM((2, 2, 4, 4, 4, SLOT, WIDTH), low),
-            pltpu.VMEM((2, 4, SLOT, WIDTH), low),
+            pltpu.VMEM((3, 2, 4, 4, 4, 16, WIDTH), low),
+            pltpu.VMEM((3, 4, SLOT, WIDTH), low),
         ]
         + landing_scratch(2, SLOT)
+        + landing_scratch(3, 16)
+        + SMALL_SCRATCH
+        + [pltpu.SemaphoreType.DMA((12,))]
         + sems(32)
-        + sems(6)
+        + sems(48)
+        + sems(9)
+        + sems(10)
         + sems(MEMBERS)
         + sems(MEMBERS),
         compiler_params=kernel_params(1),
-    )(grad_att, parts, head_out, lse, grad_up, grad_down, unshuffle)
-
-
-def reduce_projections(grad_qkv, grad_out, gain, unshuffle):
-    low = jnp.bfloat16
-    return pl.pallas_call(
-        reduce_kernel,
-        name="reduce_projections",
-        out_shape=[wide_array(SLOT, WIDTH), wide_array(8, 768)],
-        in_specs=vmem_specs(4),
-        out_specs=vmem_specs(2),
-        scratch_shapes=[
-            pltpu.VMEM((3, 2, 4, 4, 4, 16, WIDTH), low),
-            pltpu.VMEM((1, 4, SLOT, WIDTH), low),
-        ]
-        + landing_scratch(3, 16)
-        + SMALL_SCRATCH
-        + sems(48)
-        + sems(3)
-        + sems(10),
-        compiler_params=kernel_params(2),
-    )(grad_qkv, grad_out, gain, unshuffle)
-
-
-def normalize(values):
-    center = values - jnp.mean(values, axis=-1, keepdims=True)
-    inv_std = lax.rsqrt(jnp.mean(center * center, axis=-1, keepdims=True) + epsilon)
-    return (center * inv_std, inv_std)
-
-
-def norm_back(upstream, gain_row, normed, inv_std):
-    scaled = upstream * gain_row
-    return inv_std * (
-        scaled
-        - jnp.mean(scaled, axis=-1, keepdims=True)
-        - normed * jnp.mean(scaled * normed, axis=-1, keepdims=True)
-    )
-
-
-def gelu_tanh(values):
-    return jax.nn.gelu(values, approximate=True)
-
-
-def multiply(form, left, right):
-    return jnp.einsum(form, left, right, preferred_element_type=jnp.float32)
+    )(grad_att, unshuffle_matrix(), gain, gain_two, inv_one, *arrays)
 
 
 def per_device(tokens, cotangent, w_qkv, w_out, w_up, w_down, norm_gains):
-    low = jnp.bfloat16
     owner = lax.axis_index("dp") * lax.axis_size("ctx") + lax.axis_index("ctx")
     shards = (
         jnp.concatenate([w_qkv, w_out.T[None]], axis=0).reshape(SLOT, WIDTH),
@@ -1013,43 +1006,19 @@
         (jnp.int32(0), owner * ROWS),
     )
     (
-        normed_one, inv_one, first_in, parts, head_out, lse, attended, gains, qkv, out, up, down
-    ) = forward_attention(tokens, shards, gain_part)
-    gain_one, gain_two = gains[0], gains[1]
-    inputs = tokens.astype(jnp.float32)
-    attended = attended.reshape(768, 256)
-    middle = inputs + multiply("cb,dc->bd", attended, out)
-    normed_two, inv_two = normalize(middle)
-    second_in = (normed_two * gain_two).astype(low)
-    hidden = multiply("bd,df->bf", second_in, up)
-    activated, gelu_pull = jax.vjp(gelu_tanh, hidden)
-    act_low = activated.astype(low)
-    result = (middle + multiply("bf,df->bd", act_low, down)).astype(low)
-    grad_down = multiply("bd,bf->df", cotangent, act_low).astype(low)
-    grad_act = multiply("bd,df->bf", cotangent, down)
-    grad_hidden = gelu_pull(grad_act)[0].astype(low)
-    grad_up = multiply("bd,bf->df", second_in, grad_hidden).astype(low)
-    grad_second = multiply("bf,df->bd", grad_hidden, up)
-    grad_middle = cotangent.astype(jnp.float32) + norm_back(
-        grad_second, gain_two, normed_two, inv_two
+        normed_one, inv_one, first_in, parts, head_out, lse, attended, gains,
+        result, second_in, act, hid, grad_middle, grad_att, gain_two_term, qkv,
+    ) = forward_pass(tokens, cotangent, shards, gain_part)
+    grad_tokens, sum_a, sum_b, sum_c, gain_sum = backward_pass(
+        grad_att,
+        gains,
+        gain_two_term,
+        inv_one,
+        (
+            lse, parts, head_out, act, hid, second_in, cotangent, grad_middle, attended,
+            first_in, normed_one, qkv,
+        ),
     )
-    gain_two_term = jnp.sum(grad_second * normed_two, axis=0)
-    mid_low = grad_middle.astype(low)
-    grad_out = multiply("bd,cb->dc", mid_low, attended).astype(low)
-    grad_att = multiply("bd,dc->cb", mid_low, out).astype(low).reshape(1, HEADS, HEAD_DIM, 256)
-    unshuffle = unshuffle_matrix()
-    grad_projected, sum_b, sum_c = backward_attention(
-        grad_att, parts, head_out, lse, grad_up, grad_down, unshuffle
-    )
-    grad_projected = grad_projected.reshape(2304, 256)
-    grad_qkv = multiply("bd,cb->dc", first_in, grad_projected).astype(low)
-    grad_first = multiply("cb,dc->bd", grad_projected, qkv)
-    grad_tokens = grad_middle + norm_back(grad_first, gain_one, normed_one, inv_one)
-    gain_one_term = jnp.sum(grad_first * normed_one, axis=0)
-    gain_terms = jnp.concatenate(
-        [gain_one_term[None], gain_two_term[None], jnp.zeros((6, 768), jnp.float32)]
-    )
-    sum_a, gain_sum = reduce_projections(grad_qkv, grad_out, gain_terms, unshuffle)
     sum_a = sum_a.reshape(4, ROWS, WIDTH)
     return (
         result,

time: 275 us -> 251 us (0.913)
  matrix products: 30.6 us -> 0 us
  Pallas kernels: 226 us -> 235 us
  other arithmetic: 4.86 us -> 1.46 us
    dot_general x11 -> x0, matrix products: 30.6 us -> none  [multiply(): return jnp.einsum(form, left, right, preferred_element_type=jnp.float32)]
    pallas_call x3 -> x2, Pallas kernels: 226 us -> 235 us  [the longest x1 126 us: backward_pass(): pl.pallas_call(backward_kernel, name='backward_pass', out_shape=[wide_arr...]
where the time goes in v3:
time: 251 us; the launch traced here: 250 us
  Pallas kernels  235 us (94%)
  local copies, waits for them, and re-layouts  13.1 us (5%)
    pallas_call x1, Pallas kernels, backward_pass(): pl.pallas_call(backward_kernel, name='backward_pass', out_shape=[wide_arr...  126 us
    pallas_call x1, Pallas kernels, forward_pass(): pl.pallas_call(forward_kernel, name='forward_pass', out_shape=[wide_array...  110 us

profile of v3, /device:TPU:1, one launch (start us, length us, event | category | flops | bytes accessed | tf_op | source)
XLA Modules:
  0.0 250.5 jit_solution(3058878242152683369)
XLA Ops:
  0.6 0.7 convert_multiply_fusion
  1.3 0.5 dynamic_update_slice.3.gain
  1.8 0.0 copy-start.2
  1.8 0.8 reshape.46
  2.6 0.6 reshape.47.b
  3.3 0.8 reshape.48
  4.1 0.6 reshape.49.c
  4.7 0.8 pad_maximum_fusion
  5.5 0.6 reshape.45.a
  6.2 0.0 copy-done.2
  6.2 109.5 %forward_pass.1 = (f32[256,768]{1,0:T(8,128)}, f32[256,1]{1,0:T(8,128)}, bf16[256,768]{1,0:T(8,128)(2,1)}, bf16[16,3,64,256]{3,2,1,0:T(8,128)(2,1)}, bf16[16,1,6...) custom-call(bf16[256,768]{1,0:T(8,128)(2,1)} %tokens.1, ...), custom_call_target="tpu_custom_call" | custom-call | tf_op jit(solution)/shard_map/forward_pass/pallas_call | solution.py:913
  115.7 125.7 %backward_pass.1 = (f32[256,768]{1,0:T(8,128)}, f32[48,384]{1,0:T(8,128)}, f32[48,384]{1,0:T(8,128)}, f32[48,384]{1,0:T(8,128)}, f32[8,768]{1,0:T(8,128)}) custom-call(bf16[1,12,64,256]{3,2,1,0:T(8,128)(2,1)} %get-tuple-element.29.grad_att, bf16[4,48,192]{2,1,0:T(8,128)(2,1)} %constant.24.clone.shuffle.unshuffle, f32[8,768]{1,0:T(8,128)} %get-tuple-element.30.gain, ...), custom_call_target="tpu_custom_call" | custom-call | tf_op jit(solution)/shard_map/backward_pass/pallas_call | solution.py:962
  241.4 0.0 copy-start.1
  241.4 0.0 copy-start
  241.4 1.4 constant_dynamic-slice_fusion
  242.8 1.3 slice_bitcast_fusion
  244.2 0.8 slice.10
  245.0 0.6 slice.11
  245.6 0.9 reshape.50
  246.6 0.6 copy.26
  247.2 0.9 reshape.52
  248.2 0.6 copy.27
  248.9 0.7 copy.37
  249.6 0.9 copy.38
  (9 shorter events, 0.1 us)
Async XLA Ops:
  1.8 4.4 %copy-start.2 = (f32[8,768]{1,0:T(8,128)}, f32[8,768]{1,0:T(8,128)S(1)}, u32[]{:S(2)}) copy-start(f32[8,768]{1,0:T(8,128)S(1)} %dynamic_update_slice.3.gain) | copy-start | bytes 73732
  241.4 7.5 %copy-start.1 = (bf16[256,768]{1,0:T(8,128)(2,1)S(1)}, bf16[256,768]{1,0:T(8,128)(2,1)}, u32[]{:S(2)}) copy-start(bf16[256,768]{1,0:T(8,128)(2,1)} %get-tuple-element.56) | copy-start | bytes 1179652
  241.4 8.2 %copy-start = (f32[256,768]{1,0:T(8,128)S(1)}, f32[256,768]{1,0:T(8,128)}, u32[]{:S(2)}) copy-start(f32[256,768]{1,0:T(8,128)} %get-tuple-element.57) | copy-start | bytes 2359300

commit v4 on v3

--- a/solution.py
+++ b/solution.py
@@ -15,7 +15,7 @@
 WIDTH = 384
 SLOT = 4 * ROWS
 THIRDS = (("z", "x", "y"), ("x", "y", "z"), ("y", "z", "x"))
-WHOLES = (("z", "y", "x"), ("z", "x", "y"))
+LATER = THIRDS + (("z", "y", "x"), ("y", "x", "z"), ("z", "y", "x"))
 MESH = pl.DeviceIdType.MESH
 VMEM_BYTES = 60 * 1024 * 1024
 epsilon = 1e-05
@@ -296,13 +296,13 @@
     lax.fori_loop(0, 16, body, 0)
 
 
-def copy_wholes(slots, whole):
+def copy_later(slots, whole):
     def body(group, carry):
-        rows = pl.ds(pl.multiple_of(group * SLOT, SLOT), SLOT)
-        for tensor, piece, indices in slots_of(group, WHOLES):
+        for tensor, piece, indices in slots_of(group, LATER):
             columns = pl.ds((tensor * 4 + piece) * WIDTH, WIDTH)
-            for k, index in enumerate(indices):
-                whole[k][rows, columns] = slots[(k,) + index]
+            for u, index in enumerate(indices):
+                rows = pl.ds(pl.multiple_of(group * SLOT + 16 * (u % 3), 16), 16)
+                whole[u // 3][rows, columns] = slots[(u,) + index]
         return carry
 
     lax.fori_loop(0, 16, body, 0)
@@ -313,17 +313,12 @@
     return (piece % 2, at[order[2]], at[order[1]], at[order[0]])
 
 
-def fill_thirds(thirds, tensor, piece, value):
+def fill(slots, first, orders, tensor, piece, value):
     for group in range(16):
-        for third, order in enumerate(THIRDS):
+        for third, order in enumerate(orders):
             row = group * SLOT + 16 * third
-            thirds[(third,) + slot_index(order, group, tensor, piece)] = value[row : row + 16]
-
-
-def fill_wholes(slots, k, tensor, piece, value):
-    for group in range(16):
-        row = group * SLOT
-        slots[(k,) + slot_index(WHOLES[k], group, tensor, piece)] = value[row : row + SLOT]
+            index = (first + third,) + slot_index(order, group, tensor, piece)
+            slots[index] = value[row : row + 16]
 
 
 def head_place(head):
@@ -486,26 +481,34 @@
     keys[own_rows, :] = turned(two(parts, i, 1))
     query = two(parts, i, 0) * jnp.bfloat16(HEAD_DIM ** -0.5)
 
-    def step(scores, j, state):
+    def step(scores, values, state):
         top, total, weighted = state
         new_top = jnp.maximum(top, jnp.max(scores, axis=0, keepdims=True))
         fade = jnp.exp(top - new_top)
         raised = jnp.exp(scores - new_top)
         total = total * fade + jnp.sum(raised, axis=0, keepdims=True)
-        weighted = weighted * fade + dot(two(parts, j, 2), raised.astype(jnp.bfloat16))
+        weighted = weighted * fade + dot(values, raised.astype(jnp.bfloat16))
         return new_top, total, weighted
 
-    def before(j, state):
-        return step(dot(keys[pl.ds(pl.multiple_of(j * TILE, TILE), TILE), :], query), j, state)
+    def rows_of(j, tiles):
+        return keys[pl.ds(pl.multiple_of(j * TILE, TILE), tiles * TILE), :]
+
+    def pair(n, state):
+        values = jnp.concatenate([two(parts, 2 * n, 2), two(parts, 2 * n + 1, 2)], axis=1)
+        return step(dot(rows_of(2 * n, 2), query), values, state)
+
+    def single(j, state):
+        return step(dot(rows_of(j, 1), query), two(parts, j, 2), state)
 
     state = (
         jnp.full((1, TILE), neg_large, jnp.float32),
         jnp.zeros((1, TILE), jnp.float32),
         jnp.zeros((HEAD_DIM, TILE), jnp.float32),
     )
-    state = lax.fori_loop(0, i, before, state)
-    masked = jnp.where(allowed_tile(), dot(keys[own_rows, :], query), neg_large)
-    top, total, weighted = step(masked, i, state)
+    state = lax.fori_loop(0, i // 2, pair, state)
+    state = lax.fori_loop(2 * (i // 2), i, single, state)
+    masked = jnp.where(allowed_tile(), dot(rows_of(i, 1), query), neg_large)
+    top, total, weighted = step(masked, two(parts, i, 2), state)
     put_two(out, i, 0, (weighted / total).astype(jnp.bfloat16))
     lse[i] = top + jnp.log(total)
 
@@ -534,11 +537,19 @@
     return v * half, slope
 
 
+def owned_columns():
+    owner = lax.axis_index("dp") * 8 + lax.axis_index("ctx")
+    column = lax.broadcasted_iota(jnp.int32, (ROWS, 768), 1)
+    row = lax.broadcasted_iota(jnp.int32, (ROWS, 768), 0)
+    return jnp.where(column == owner * ROWS + row, 1.0, 0.0)
+
+
 def forward_kernel(
-    tokens, cotangent, a, b, c, gain, shuffle,
+    tokens, cotangent, a_qkv, a_out, b, c, gain, select, shuffle,
     normed_out, inv_out, first_out, parts, head_out, lse, attended, gain_out,
     result, second_out, act_out, hid_out, middle_grad, grad_att, gain_two_out, w_qkv,
     pre, thirds, wholes, qkv, out, up, down, projected, keys, ring, pair, forth_sum, back_sum,
+    own_gain,
     third_send, third_recv, whole_send, whole_recv, pre_send, pre_recv, small_send, small_recv,
     to_send, to_recv, from_send, from_recv, write_sem,
 ):
@@ -553,16 +564,23 @@
     ]
     later = [
         Gather(pos, order, u, wholes, whole_send, whole_recv, started)
-        for u, order in enumerate(WHOLES)
+        for u, order in enumerate(LATER)
     ]
     spread = ToHeads(projected, parts, to_send, to_recv)
     back = FromHeads(head_out, attended, from_send, from_recv)
-    for k, shard in enumerate((a, b, c)):
-        pre[k, group.member] = shard[...]
+    slots = (
+        sum(dot(select[j], a_qkv[j]) for j in range(3)) + dot(select[3], a_out[...]),
+        sum(dot(select[j], b[:, j * WIDTH : (j + 1) * WIDTH]) for j in range(4)),
+        sum(dot(select[j], c[:, j * WIDTH : (j + 1) * WIDTH]) for j in range(4)),
+    )
+    for k in range(3):
+        pre[k, group.member] = slots[k].astype(jnp.bfloat16)
+    own_gain[...] = jnp.zeros_like(own_gain)
+    own_gain[0:2] = 0.5 * dot(gain[...], owned_columns().astype(jnp.bfloat16))
     greet(pos)
     for k in range(3):
         group.start(pre, k)
-    small.start(0, gain[...])
+    small.start(0, own_gain[...])
 
     def sorted_piece(k):
         return dot(shuffle[group.member], group.finish(pre, k)).astype(jnp.bfloat16)
@@ -571,8 +589,10 @@
     for u, unit in enumerate(first):
         thirds[unit.at(0, 0)] = piece[16 * u : 16 * (u + 1)]
         unit.begin(0)
-    for u, unit in enumerate(later):
-        wholes[unit.at(0, 0)] = sorted_piece(1 + u)
+    for k in (1, 2):
+        piece = sorted_piece(k)
+        for u in range(3):
+            wholes[later[3 * k - 3 + u].at(0, 0)] = piece[16 * u : 16 * (u + 1)]
     normed_one, inv_one = norm_parts(wide(tokens[...]))
     normed_out[...] = normed_one
     inv_out[...] = inv_one
@@ -628,7 +648,7 @@
     lax.fori_loop(7, 8, per_queries, 0)
     for unit in later:
         unit.settle()
-    copy_wholes(wholes, (up, down))
+    copy_later(wholes, (up, down))
     back.wait()
     weighted = jnp.transpose(dot(out[...], attended[0].reshape(768, 256)))
     middle = wide(tokens[...]) + weighted
@@ -692,8 +712,16 @@
 
     zero = jnp.zeros((HEAD_DIM, TILE), jnp.float32)
     state = step(j, (zero, zero), True)
+    pairs = (TILES - 1 - j) // 2
+    rest = j + 1 + 2 * pairs
+
+    def pair(n, state):
+        i = j + 1 + 2 * n
+        return step(i + 1, step(i, state, False), False)
+
+    state = lax.fori_loop(0, pairs, pair, state)
     key_sum, value_sum = lax.fori_loop(
-        j + 1, TILES, lambda i, state: step(i, state, False), state
+        rest, TILES, lambda i, state: step(i, state, False), state
     )
     put_two(out, j, 0, (query_sum[j] * HEAD_DIM ** -0.5).astype(jnp.bfloat16))
     put_two(out, j, 1, key_sum.astype(jnp.bfloat16))
@@ -703,7 +731,7 @@
 def backward_kernel(
     grad_att, unshuffle, gain, gain_two, inv_one, lse_in, parts_in, head_out_in, act_in, hid_in,
     second_in, cot_in, middle_in, attended_in, first_in, normed_in, w_qkv_in,
-    grad_tokens, out_a, out_b, out_c, gain_out,
+    grad_tokens, grad_qkv, grad_out, grad_up, grad_down, grad_gains,
     lse, parts, head_out, act, hid, second, cot, middle, attended, first, normed, w_qkv,
     turned_in, grad_projected, head_grad, head_back, query_sum, delta, wholes, thirds, post,
     cores_w, ends1_w, ends2_w, ends3_w, cores_t, ends1_t, ends2_t, ends3_t, ring, pair,
@@ -720,7 +748,7 @@
             pos, order, u, wholes, (cores_w, ends1_w, ends2_w, ends3_w), whole_send, whole_recv,
             started,
         )
-        for u, order in enumerate(WHOLES)
+        for u, order in enumerate(LATER)
     ]
     last = [
         Reduce(
@@ -759,7 +787,7 @@
         columns = pl.ds(pl.multiple_of(p * WIDTH, WIDTH), WIDTH)
         for k, (left, right) in enumerate(((1, hid), (0, act))):
             value = dot(turned_in[left], right[:, columns]).astype(jnp.bfloat16)
-            fill_wholes(wholes, k, p // 4, p % 4, value)
+            fill(wholes, 3 * k, LATER[3 * k : 3 * k + 3], p // 4, p % 4, value)
         return carry
 
     lax.fori_loop(0, 8, feed, 0)
@@ -771,9 +799,7 @@
     flip(1, wide(first[...]))
     for tensor in range(2):
         rows = attended[0, 6 * tensor : 6 * (tensor + 1)].reshape(WIDTH, 256)
-        fill_thirds(thirds, tensor, 3, dot_right(turned_in[0], rows).astype(jnp.bfloat16))
-    for unit in units:
-        unit.begin(2)
+        fill(thirds, 0, THIRDS, tensor, 3, dot_right(turned_in[0], rows).astype(jnp.bfloat16))
 
     @pl.when(active)
     def _():
@@ -797,26 +823,23 @@
 
         return carry
 
-    lax.fori_loop(0, 2, per_keys, 0)
+    lax.fori_loop(0, 1, per_keys, 0)
+    for unit in units:
+        unit.begin(2)
+    lax.fori_loop(1, 5, per_keys, 0)
     for unit in units:
         unit.finish(2)
         unit.begin(1)
-    lax.fori_loop(2, 4, per_keys, 0)
+    lax.fori_loop(5, 8, per_keys, 0)
     for unit in units:
         unit.finish(1)
         unit.begin(0)
-    lax.fori_loop(4, 6, per_keys, 0)
-    for u, unit in enumerate(units):
-        unit.finish(0)
-        post[u, group.member] = wholes[unit.at(0, 0)]
-        group.start(post, u)
-    lax.fori_loop(6, 8, per_keys, 0)
     back.wait()
 
     def project(p, carry):
         part, tensor = p // 2, p % 2
         rows = grad_projected[part, pl.ds(6 * tensor, 6)].reshape(WIDTH, 256)
-        fill_thirds(thirds, tensor, part, dot_right(turned_in[1], rows).astype(jnp.bfloat16))
+        fill(thirds, 0, THIRDS, tensor, part, dot_right(turned_in[1], rows).astype(jnp.bfloat16))
         return carry
 
     lax.fori_loop(0, 6, project, 0)
@@ -829,8 +852,11 @@
     for unit in last:
         unit.begin(2)
     grad_tokens[...] = middle[...] + norm_back(grad_first, gain[0:1], normed[...], inv_one[...])
-    for u, out in enumerate((out_b, out_c)):
-        out[...] = dot(unshuffle[group.member], group.finish(post, u))
+    for u, unit in enumerate(units):
+        unit.finish(0)
+        post[u // 3, group.member, pl.ds(16 * (u % 3), 16)] = wholes[unit.at(0, 0)]
+    for k in range(2):
+        group.start(post, k)
     for stage in (2, 1, 0):
         total = small.finish(2 - stage)
         if stage > 0:
@@ -844,8 +870,25 @@
     for u, unit in enumerate(last):
         post[2, group.member, pl.ds(16 * u, 16)] = thirds[unit.at(0, 0)]
     group.start(post, 2)
-    gain_out[...] = small.finish_pair()
-    out_a[...] = dot(unshuffle[group.member], group.finish(post, 2))
+    grad_gains[...] = lax.dot_general(
+        small.finish_pair(),
+        owned_columns(),
+        (((1,), (1,)), ((), ())),
+        precision=lax.Precision.HIGHEST,
+        preferred_element_type=jnp.float32,
+    )[0:2]
+
+    def own_rows(held, piece):
+        return dot(unshuffle[group.member, piece], held)
+
+    for k, out in enumerate((grad_up, grad_down)):
+        held = group.finish(post, k)
+        for piece in range(4):
+            out[:, piece * WIDTH : (piece + 1) * WIDTH] = own_rows(held, piece)[:ROWS]
+    held = group.finish(post, 2)
+    for piece in range(3):
+        grad_qkv[piece] = own_rows(held, piece)[:ROWS]
+    grad_out[...] = own_rows(held, 3)[:ROWS]
     for k in range(3):
         group.sent(post, k)
     spread.sent()
@@ -868,11 +911,19 @@
 
 
 def unshuffle_matrix():
-    matrix = np.zeros((4, SLOT, 4 * SLOT), np.float32)
+    matrix = np.zeros((4, 4, 16, 4 * SLOT), np.float32)
     for member in range(4):
         for piece in range(4):
             for row in range(ROWS):
-                matrix[member, piece * ROWS + row, piece * SLOT + member * ROWS + row] = 1
+                matrix[member, piece, row, piece * SLOT + member * ROWS + row] = 1
+    return jnp.asarray(matrix, jnp.bfloat16)
+
+
+def select_matrix():
+    matrix = np.zeros((4, SLOT, ROWS), np.float32)
+    for piece in range(4):
+        for row in range(ROWS):
+            matrix[piece, piece * ROWS + row, row] = 1
     return jnp.asarray(matrix, jnp.bfloat16)
 
 
@@ -908,7 +959,7 @@
     )
 
 
-def forward_pass(tokens, cotangent, shards, gain):
+def forward_pass(tokens, cotangent, shards):
     low = jnp.bfloat16
     return pl.pallas_call(
         forward_kernel,
@@ -931,12 +982,12 @@
             wide_array(1, 768),
             low_array(768, 2304),
         ],
-        in_specs=vmem_specs(7),
+        in_specs=vmem_specs(9),
         out_specs=vmem_specs(15) + any_specs(1),
         scratch_shapes=[
             pltpu.VMEM((3, 4, SLOT, WIDTH), low),
             pltpu.VMEM((3, 2, 4, 4, 4, 16, WIDTH), low),
-            pltpu.VMEM((2, 2, 4, 4, 4, SLOT, WIDTH), low),
+            pltpu.VMEM((6, 2, 4, 4, 4, 16, WIDTH), low),
             pltpu.VMEM((768, 2304), low),
             pltpu.VMEM((768, 768), low),
             pltpu.VMEM((768, 3072), low),
@@ -946,15 +997,16 @@
         ]
         + SMALL_SCRATCH
         + [pltpu.VMEM((256, 768), jnp.float32)] * 2
+        + [pltpu.VMEM((8, 768), jnp.float32)]
         + sems(48)
-        + sems(32)
+        + sems(96)
         + sems(9)
         + sems(10)
         + sems(MEMBERS)
         + sems(MEMBERS)
         + [pltpu.SemaphoreType.DMA],
         compiler_params=kernel_params(0),
-    )(tokens, cotangent, *shards, gain, shuffle_matrix())
+    )(tokens, cotangent, *shards, select_matrix(), shuffle_matrix())
 
 
 def backward_pass(grad_att, gain, gain_two, inv_one, arrays):
@@ -962,11 +1014,16 @@
     return pl.pallas_call(
         backward_kernel,
         name="backward_pass",
-        out_shape=[wide_array(256, 768)]
-        + [wide_array(SLOT, WIDTH)] * 3
-        + [wide_array(8, 768)],
+        out_shape=[
+            wide_array(256, 768),
+            wide_array(3, ROWS, WIDTH),
+            wide_array(ROWS, WIDTH),
+            wide_array(ROWS, 4 * WIDTH),
+            wide_array(ROWS, 4 * WIDTH),
+            wide_array(2, ROWS),
+        ],
         in_specs=any_specs(1) + vmem_specs(4) + any_specs(12),
-        out_specs=vmem_specs(5),
+        out_specs=vmem_specs(6),
         scratch_shapes=[pltpu.VMEM(array.shape, array.dtype) for array in arrays]
         + [
             pltpu.VMEM((2, 768, 256), low),
@@ -975,15 +1032,15 @@
             pltpu.VMEM((MEMBERS, 3, HEAD_DIM, 256), low),
             pltpu.VMEM((TILES, HEAD_DIM, TILE), jnp.float32),
             pltpu.VMEM((TILES, 1, TILE), jnp.float32),
-            pltpu.VMEM((2, 2, 4, 4, 4, SLOT, WIDTH), low),
+            pltpu.VMEM((6, 2, 4, 4, 4, 16, WIDTH), low),
             pltpu.VMEM((3, 2, 4, 4, 4, 16, WIDTH), low),
             pltpu.VMEM((3, 4, SLOT, WIDTH), low),
         ]
-        + landing_scratch(2, SLOT)
+        + landing_scratch(6, 16)
         + landing_scratch(3, 16)
         + SMALL_SCRATCH
         + [pltpu.SemaphoreType.DMA((12,))]
-        + sems(32)
+        + sems(96)
         + sems(48)
         + sems(9)
         + sems(10)
@@ -994,22 +1051,11 @@
 
 
 def per_device(tokens, cotangent, w_qkv, w_out, w_up, w_down, norm_gains):
-    owner = lax.axis_index("dp") * lax.axis_size("ctx") + lax.axis_index("ctx")
-    shards = (
-        jnp.concatenate([w_qkv, w_out.T[None]], axis=0).reshape(SLOT, WIDTH),
-        w_up.reshape(ROWS, 4, WIDTH).transpose(1, 0, 2).reshape(SLOT, WIDTH),
-        w_down.reshape(4, WIDTH, ROWS).transpose(0, 2, 1).reshape(SLOT, WIDTH),
-    )
-    gain_part = lax.dynamic_update_slice(
-        jnp.zeros((8, 768), jnp.float32),
-        0.5 * norm_gains.astype(jnp.float32),
-        (jnp.int32(0), owner * ROWS),
-    )
     (
         normed_one, inv_one, first_in, parts, head_out, lse, attended, gains,
         result, second_in, act, hid, grad_middle, grad_att, gain_two_term, qkv,
-    ) = forward_pass(tokens, cotangent, shards, gain_part)
-    grad_tokens, sum_a, sum_b, sum_c, gain_sum = backward_pass(
+    ) = forward_pass(tokens, cotangent, (w_qkv, w_out.T, w_up, w_down.T, norm_gains))
+    grad_tokens, grad_qkv, grad_out, grad_up, grad_down, grad_gains = backward_pass(
         grad_att,
         gains,
         gain_two_term,
@@ -1019,16 +1065,7 @@
             first_in, normed_one, qkv,
         ),
     )
-    sum_a = sum_a.reshape(4, ROWS, WIDTH)
-    return (
-        result,
-        grad_tokens,
-        sum_a[:3],
-        sum_a[3].T,
-        sum_b.reshape(4, ROWS, WIDTH).transpose(1, 0, 2).reshape(ROWS, 4 * WIDTH),
-        sum_c.reshape(4, ROWS, WIDTH).transpose(0, 2, 1).reshape(4 * WIDTH, ROWS),
-        lax.dynamic_slice(gain_sum, (jnp.int32(0), owner * ROWS), (2, ROWS)),
-    )
+    return (result, grad_tokens, grad_qkv, grad_out.T, grad_up, grad_down.T, grad_gains)
 
 
 def solution(mesh):

time: 251 us -> 218 us (0.87)
  Pallas kernels: 235 us -> 211 us
  local copies, waits for them, and re-layouts: 13.1 us -> 5.92 us
    pallas_call x1, Pallas kernels: 126 us -> 111 us  [backward_pass(): pl.pallas_call(backward_kernel, name='backward_pass', out_shape=[wide_arr...]
    pallas_call x1, Pallas kernels: 110 us -> 99.9 us  [forward_pass(): pl.pallas_call(forward_kernel, name='forward_pass', out_shape=[wide_array...]
    reshape x9 -> x0, local copies, waits for them, and re-layouts: 5.35 us -> none  [the longest x3 1.47 us: per_device(): w_up.reshape(ROWS, 4, WIDTH).transpose(1, 0, 2).reshape(SLOT, WIDTH)]
    unnamed x12 -> x19, local copies, waits for them, and re-layouts: 2.97 us -> 5.92 us
where the time goes in v4:
time: 218 us
  Pallas kernels  211 us (97%)
  local copies, waits for them, and re-layouts  5.92 us (3%)
    pallas_call x1, Pallas kernels, backward_pass(): pl.pallas_call(backward_kernel, name='backward_pass', out_shape=[wide_arr...  111 us
    pallas_call x1, Pallas kernels, forward_pass(): pl.pallas_call(forward_kernel, name='forward_pass', out_shape=[wide_array...  99.9 us
    unnamed x19, local copies, waits for them, and re-layouts  5.92 us

profile of v4, /device:TPU:1, one launch (start us, length us, event | category | flops | bytes accessed | tf_op | source)
XLA Modules:
  0.0 217.7 jit_solution(17824035789749992716)
XLA Ops:
  0.6 99.9 %forward_pass.1 = (f32[256,768]{1,0:T(8,128)}, f32[256,1]{1,0:T(8,128)}, bf16[256,768]{1,0:T(8,128)(2,1)}, bf16[16,3,64,256]{3,2,1,0:T(8,128)(2,1)}, bf16[16,1,6...) custom-call(bf16[256,768]{1,0:T(8,128)(2,1)} %tokens.1, ...), custom_call_target="tpu_custom_call" | custom-call | tf_op jit(solution)/shard_map/forward_pass/pallas_call | solution.py:964
  100.5 0.0 copy-start
  100.6 111.1 %backward_pass.1 = (f32[256,768]{1,0:T(8,128)}, f32[3,12,384]{2,1,0:T(8,128)}, f32[12,384]{1,0:T(8,128)}, f32[12,1536]{1,0:T(8,128)}, f32[12,1536]{1,0:T(8,128)}, /*index=5*/f32[2,12]{1,0:T(2,128)}) custom-call(bf16[1,12,64,256]{3,2,1,0:T(8,128)(2,1)} %get-tuple-element.30.grad_att, bf16[4,4,16,192]{3,2,1,0:T(8,128)(2,1)} %constant.8.clone.unshuffle, ...), custom_call_target="tpu_custom_call" | custom-call | tf_op jit(solution)/shard_map/backward_pass/pallas_call | solution.py:1014
  211.7 0.0 copy-start.3
  211.7 0.0 copy-start.4
  211.7 0.0 copy-start.2
  211.7 0.0 copy-start.1
  211.8 0.0 copy-start.5
  211.8 0.0 copy-done
  211.8 0.7 copy.24
  212.5 2.1 copy.25
  214.6 0.0 copy-done.3
  214.6 0.6 copy.26
  215.2 0.0 copy-done.4
  215.2 0.6 copy.27
  215.8 0.0 copy-done.2
  215.8 0.6 copy.28
  216.5 0.0 copy-done.1
  216.5 0.6 copy.29
  217.1 0.0 copy-done.5
  217.1 0.6 copy.30
Async XLA Ops:
  100.5 111.2 %copy-start = (bf16[256,768]{1,0:T(8,128)(2,1)S(1)}, bf16[256,768]{1,0:T(8,128)(2,1)}, u32[]{:S(2)}) copy-start(bf16[256,768]{1,0:T(8,128)(2,1)} %get-tuple-element.58) | copy-start | bytes 1179652
  211.7 2.9 %copy-start.3 = (f32[3,12,384]{2,1,0:T(8,128)S(1)}, f32[3,12,384]{2,1,0:T(8,128)}, u32[]{:S(2)}) copy-start(f32[3,12,384]{2,1,0:T(8,128)} %get-tuple-element.60) | copy-start | bytes 165892
  211.7 3.5 %copy-start.4 = (f32[12,384]{1,0:T(8,128)S(1)}, f32[12,384]{1,0:T(8,128)}, u32[]{:S(2)}) copy-start(f32[12,384]{1,0:T(8,128)} %get-tuple-element.47) | copy-start | bytes 55300
  211.7 4.1 %copy-start.2 = (f32[12,1536]{1,0:T(8,128)S(1)}, f32[12,1536]{1,0:T(8,128)}, u32[]{:S(2)}) copy-start(f32[12,1536]{1,0:T(8,128)} %get-tuple-element.62) | copy-start | bytes 221188
  211.7 4.7 %copy-start.1 = (f32[12,1536]{1,0:T(8,128)S(1)}, f32[12,1536]{1,0:T(8,128)}, u32[]{:S(2)}) copy-start(f32[12,1536]{1,0:T(8,128)} %get-tuple-element.49) | copy-start | bytes 221188
  211.8 5.4 %copy-start.5 = (f32[2,12]{1,0:T(2,128)S(1)}, f32[2,12]{1,0:T(2,128)}, u32[]{:S(2)}) copy-start(f32[2,12]{1,0:T(2,128)} %get-tuple-element.64) | copy-start | bytes 292

commit v5 on v4

--- a/solution.py
+++ b/solution.py
@@ -296,21 +296,20 @@
     lax.fori_loop(0, 16, body, 0)
 
 
-def copy_later(slots, whole):
-    def body(group, carry):
-        for tensor, piece, indices in slots_of(group, LATER):
-            columns = pl.ds((tensor * 4 + piece) * WIDTH, WIDTH)
-            for u, index in enumerate(indices):
-                rows = pl.ds(pl.multiple_of(group * SLOT + 16 * (u % 3), 16), 16)
-                whole[u // 3][rows, columns] = slots[(u,) + index]
-        return carry
-
-    lax.fori_loop(0, 16, body, 0)
-
-
 def slot_index(order, group, tensor, piece):
     at = dict(x=group // 4, z=2 * tensor + (group // 2) % 2, y=2 * (group % 2) + piece // 2)
     return (piece % 2, at[order[2]], at[order[1]], at[order[0]])
+
+
+def collect(slots, first, orders, tensor, piece):
+    return jnp.concatenate(
+        [
+            slots[(first + third,) + slot_index(order, group, tensor, piece)]
+            for group in range(16)
+            for third, order in enumerate(orders)
+        ],
+        axis=0,
+    )
 
 
 def fill(slots, first, orders, tensor, piece, value):
@@ -544,19 +543,60 @@
     return jnp.where(column == owner * ROWS + row, 1.0, 0.0)
 
 
-def forward_kernel(
-    tokens, cotangent, a_qkv, a_out, b, c, gain, select, shuffle,
-    normed_out, inv_out, first_out, parts, head_out, lse, attended, gain_out,
-    result, second_out, act_out, hid_out, middle_grad, grad_att, gain_two_out, w_qkv,
-    pre, thirds, wholes, qkv, out, up, down, projected, keys, ring, pair, forth_sum, back_sum,
-    own_gain,
+def back_tile(j, parts, grad_att, lse, delta, query_sum, out):
+    key_cols, value_cols = two(parts, j, 1), two(parts, j, 2)
+    key_rows, value_rows = turned(key_cols), turned(value_cols)
+
+    def step(i, state, diagonal):
+        key_sum, value_sum = state
+        query = two(parts, i, 0) * jnp.bfloat16(HEAD_DIM ** -0.5)
+        grad = two(grad_att, i, 0)
+        shares = jnp.exp(dot(key_rows, query) - lse[i])
+        if diagonal:
+            shares = jnp.where(allowed_tile(), shares, 0.0)
+        grad_scores = (shares * (dot(value_rows, grad) - delta[i])).astype(jnp.bfloat16)
+        query_sum[i] += dot(key_cols, grad_scores)
+        key_sum = key_sum + dot_right(query, grad_scores)
+        value_sum = value_sum + dot_right(grad, shares.astype(jnp.bfloat16))
+        return key_sum, value_sum
+
+    zero = jnp.zeros((HEAD_DIM, TILE), jnp.float32)
+    state = step(j, (zero, zero), True)
+    pairs = (TILES - 1 - j) // 2
+    rest = j + 1 + 2 * pairs
+
+    def pair(n, state):
+        i = j + 1 + 2 * n
+        return step(i + 1, step(i, state, False), False)
+
+    state = lax.fori_loop(0, pairs, pair, state)
+    key_sum, value_sum = lax.fori_loop(
+        rest, TILES, lambda i, state: step(i, state, False), state
+    )
+    put_two(out, j, 0, (query_sum[j] * HEAD_DIM ** -0.5).astype(jnp.bfloat16))
+    put_two(out, j, 1, key_sum.astype(jnp.bfloat16))
+    put_two(out, j, 2, value_sum.astype(jnp.bfloat16))
+
+
+def layer_kernel(
+    tokens, cotangent, a_qkv, a_out, b, c, gain, select, shuffle, unshuffle,
+    result, grad_tokens, grad_qkv, grad_out, grad_up, grad_down, grad_gains,
+    pre, thirds, wholes, qkv, out, projected, keys, ring, pair, last_ring, last_pair,
+    forth_sum, back_sum, own_gain, kept_gains, normed, parts, head_out, lse, attended, second,
+    act, hid, middle_grad, grad_att, turned_in, grad_projected, head_grad, head_back,
+    query_sum, delta, post,
+    cores_w, ends1_w, ends2_w, ends3_w, cores_t, ends1_t, ends2_t, ends3_t,
     third_send, third_recv, whole_send, whole_recv, pre_send, pre_recv, small_send, small_recv,
-    to_send, to_recv, from_send, from_recv, write_sem,
+    to_send, to_recv, from_send, from_recv,
+    back_third_send, back_third_recv, back_whole_send, back_whole_recv, post_send, post_recv,
+    last_small_send, last_small_recv, to_grad_send, to_grad_recv, from_grad_send, from_grad_recv,
 ):
     pos = place()
     active = own_head(lax.axis_index("ctx"), lax.axis_index("tensor"))[1]
     group = Group(pos, pre_send, pre_recv)
+    owners = Group(pos, post_send, post_recv)
     small = SmallSum(pos, ring, pair, small_send, small_recv)
+    last_small = SmallSum(pos, last_ring, last_pair, last_small_send, last_small_recv)
     started = []
     first = [
         Gather(pos, order, u, thirds, third_send, third_recv, started)
@@ -568,6 +608,8 @@
     ]
     spread = ToHeads(projected, parts, to_send, to_recv)
     back = FromHeads(head_out, attended, from_send, from_recv)
+    head_spread = ToHeads(grad_att, head_grad, to_grad_send, to_grad_recv)
+    head_return = FromHeads(head_back, grad_projected, from_grad_send, from_grad_recv)
     slots = (
         sum(dot(select[j], a_qkv[j]) for j in range(3)) + dot(select[3], a_out[...]),
         sum(dot(select[j], b[:, j * WIDTH : (j + 1) * WIDTH]) for j in range(4)),
@@ -594,8 +636,7 @@
         for u in range(3):
             wholes[later[3 * k - 3 + u].at(0, 0)] = piece[16 * u : 16 * (u + 1)]
     normed_one, inv_one = norm_parts(wide(tokens[...]))
-    normed_out[...] = normed_one
-    inv_out[...] = inv_one
+    normed[...] = normed_one
     for stage in range(3):
         for unit in first:
             unit.finish(stage)
@@ -615,12 +656,9 @@
     for unit in first:
         unit.settle()
     copy_thirds(thirds, (qkv, out))
-    write = pltpu.make_async_copy(qkv, w_qkv, write_sem)
-    write.start()
     gains = small.finish_pair()
-    gain_out[...] = gains
-    first_in = (normed_out[...] * gains[0:1]).astype(jnp.bfloat16)
-    first_out[...] = first_in
+    kept_gains[...] = gains
+    first_in = (normed[...] * gains[0:1]).astype(jnp.bfloat16)
     for part in range(3):
         for tensor in range(2):
             column = (part * 2 + tensor) * WIDTH
@@ -632,6 +670,12 @@
         unit.finish(1)
         unit.begin(2)
 
+    def flip(n, value):
+        turned_in[n] = jnp.transpose(value).astype(jnp.bfloat16)
+
+    flip(0, wide(cotangent[...]))
+    flip(1, wide(first_in))
+
     def per_queries(i, carry):
         @pl.when(active)
         def _():
@@ -648,38 +692,43 @@
     lax.fori_loop(7, 8, per_queries, 0)
     for unit in later:
         unit.settle()
-    copy_later(wholes, (up, down))
     back.wait()
     weighted = jnp.transpose(dot(out[...], attended[0].reshape(768, 256)))
     middle = wide(tokens[...]) + weighted
     normed_two, inv_two = norm_parts(middle)
-    second_in = (normed_two * gain_out[1:2]).astype(jnp.bfloat16)
-    second_out[...] = second_in
+    second_in = (normed_two * kept_gains[1:2]).astype(jnp.bfloat16)
+    second[...] = second_in
     forth_sum[...] = middle
     back_sum[...] = jnp.zeros_like(back_sum)
 
     def feed(p, carry):
-        columns = pl.ds(pl.multiple_of(p * 768, 768), 768)
-        act, slope = gelu_and_slope(dot(second_out[...], up[:, columns]))
-        act = act.astype(jnp.bfloat16)
-        act_out[:, columns] = act
-        hid = (dot(cotangent[...], down[:, columns]) * slope).astype(jnp.bfloat16)
-        hid_out[:, columns] = hid
-        forth_sum[...] += dot_right(act, down[:, columns])
-        back_sum[...] += dot_right(hid, up[:, columns])
+        columns = pl.ds(pl.multiple_of(p * WIDTH, WIDTH), WIDTH)
+        up = collect(wholes, 0, LATER[:3], p // 4, p % 4)
+        down = collect(wholes, 3, LATER[3:], p // 4, p % 4)
+        bent, slope = gelu_and_slope(dot(second[...], up))
+        bent = bent.astype(jnp.bfloat16)
+        act[:, columns] = bent
+        low = (dot(cotangent[...], down) * slope).astype(jnp.bfloat16)
+        hid[:, columns] = low
+        forth_sum[...] += dot_right(bent, down)
+        back_sum[...] += dot_right(low, up)
         return carry
 
-    lax.fori_loop(0, 4, feed, 0)
+    lax.fori_loop(0, 8, feed, 0)
     result[...] = forth_sum[...].astype(jnp.bfloat16)
     grad_second = back_sum[...]
-    gain_two_out[...] = jnp.sum(grad_second * normed_two, axis=0, keepdims=True)
+    gain_two_term = jnp.sum(grad_second * normed_two, axis=0, keepdims=True)
     grad_middle = wide(cotangent[...]) + norm_back(
-        grad_second, gain_out[1:2], normed_two, inv_two
+        grad_second, kept_gains[1:2], normed_two, inv_two
     )
     middle_grad[...] = grad_middle
+    kept_gains[2:3] = gain_two_term
     grads = jnp.transpose(dot(grad_middle.astype(jnp.bfloat16), out[...])).astype(jnp.bfloat16)
     for head in range(HEADS):
         grad_att[0, head] = grads[head * HEAD_DIM : (head + 1) * HEAD_DIM]
+    head_spread.start()
+    flip(2, wide(second[...]))
+    flip(3, middle_grad[...])
     spread.sent()
 
     @pl.when(active)
@@ -690,120 +739,38 @@
         group.sent(pre, k)
     for copy in started:
         copy.wait_send()
-    write.wait()
-
-
-def back_tile(j, parts, grad_att, lse, delta, query_sum, out):
-    key_cols, value_cols = two(parts, j, 1), two(parts, j, 2)
-    key_rows, value_rows = turned(key_cols), turned(value_cols)
-
-    def step(i, state, diagonal):
-        key_sum, value_sum = state
-        query = two(parts, i, 0) * jnp.bfloat16(HEAD_DIM ** -0.5)
-        grad = two(grad_att, i, 0)
-        shares = jnp.exp(dot(key_rows, query) - lse[i])
-        if diagonal:
-            shares = jnp.where(allowed_tile(), shares, 0.0)
-        grad_scores = (shares * (dot(value_rows, grad) - delta[i])).astype(jnp.bfloat16)
-        query_sum[i] += dot(key_cols, grad_scores)
-        key_sum = key_sum + dot_right(query, grad_scores)
-        value_sum = value_sum + dot_right(grad, shares.astype(jnp.bfloat16))
-        return key_sum, value_sum
-
-    zero = jnp.zeros((HEAD_DIM, TILE), jnp.float32)
-    state = step(j, (zero, zero), True)
-    pairs = (TILES - 1 - j) // 2
-    rest = j + 1 + 2 * pairs
-
-    def pair(n, state):
-        i = j + 1 + 2 * n
-        return step(i + 1, step(i, state, False), False)
-
-    state = lax.fori_loop(0, pairs, pair, state)
-    key_sum, value_sum = lax.fori_loop(
-        rest, TILES, lambda i, state: step(i, state, False), state
-    )
-    put_two(out, j, 0, (query_sum[j] * HEAD_DIM ** -0.5).astype(jnp.bfloat16))
-    put_two(out, j, 1, key_sum.astype(jnp.bfloat16))
-    put_two(out, j, 2, value_sum.astype(jnp.bfloat16))
-
-
-def backward_kernel(
-    grad_att, unshuffle, gain, gain_two, inv_one, lse_in, parts_in, head_out_in, act_in, hid_in,
-    second_in, cot_in, middle_in, attended_in, first_in, normed_in, w_qkv_in,
-    grad_tokens, grad_qkv, grad_out, grad_up, grad_down, grad_gains,
-    lse, parts, head_out, act, hid, second, cot, middle, attended, first, normed, w_qkv,
-    turned_in, grad_projected, head_grad, head_back, query_sum, delta, wholes, thirds, post,
-    cores_w, ends1_w, ends2_w, ends3_w, cores_t, ends1_t, ends2_t, ends3_t, ring, pair,
-    load_sem, whole_send, whole_recv, third_send, third_recv, post_send, post_recv,
-    small_send, small_recv, to_send, to_recv, from_send, from_recv,
-):
-    pos = place()
-    active = own_head(lax.axis_index("ctx"), lax.axis_index("tensor"))[1]
-    group = Group(pos, post_send, post_recv)
-    small = SmallSum(pos, ring, pair, small_send, small_recv)
     started = []
     units = [
         Reduce(
-            pos, order, u, wholes, (cores_w, ends1_w, ends2_w, ends3_w), whole_send, whole_recv,
+            pos, order, u, wholes, (cores_w, ends1_w, ends2_w, ends3_w), back_whole_send, back_whole_recv,
             started,
         )
         for u, order in enumerate(LATER)
     ]
     last = [
         Reduce(
-            pos, order, u, thirds, (cores_t, ends1_t, ends2_t, ends3_t), third_send, third_recv,
+            pos, order, u, thirds, (cores_t, ends1_t, ends2_t, ends3_t), back_third_send, back_third_recv,
             started,
         )
         for u, order in enumerate(THIRDS)
     ]
-    spread = ToHeads(grad_att, head_grad, to_send, to_recv)
-    back = FromHeads(head_back, grad_projected, from_send, from_recv)
-    loads = [
-        pltpu.make_async_copy(src, dst, load_sem.at[n])
-        for n, (src, dst) in enumerate(
-            (
-                (cot_in, cot), (act_in, act), (second_in, second), (hid_in, hid),
-                (middle_in, middle), (attended_in, attended), (lse_in, lse), (parts_in, parts),
-                (head_out_in, head_out), (first_in, first), (normed_in, normed),
-                (w_qkv_in, w_qkv),
-            )
-        )
-    ]
-    for load in loads:
-        load.start()
-    greet(pos)
-    spread.start()
-    for load in loads[:4]:
-        load.wait()
-
-    def flip(n, value):
-        turned_in[n] = jnp.transpose(value).astype(jnp.bfloat16)
-
-    flip(0, wide(cot[...]))
-    flip(1, wide(second[...]))
-
-    def feed(p, carry):
+    def give(p, carry):
         columns = pl.ds(pl.multiple_of(p * WIDTH, WIDTH), WIDTH)
-        for k, (left, right) in enumerate(((1, hid), (0, act))):
+        for k, (left, right) in enumerate(((2, hid), (0, act))):
             value = dot(turned_in[left], right[:, columns]).astype(jnp.bfloat16)
             fill(wholes, 3 * k, LATER[3 * k : 3 * k + 3], p // 4, p % 4, value)
         return carry
 
-    lax.fori_loop(0, 8, feed, 0)
+    lax.fori_loop(0, 8, give, 0)
     for unit in units:
         unit.cross()
-    for load in loads[4:]:
-        load.wait()
-    flip(0, middle[...])
-    flip(1, wide(first[...]))
     for tensor in range(2):
         rows = attended[0, 6 * tensor : 6 * (tensor + 1)].reshape(WIDTH, 256)
-        fill(thirds, 0, THIRDS, tensor, 3, dot_right(turned_in[0], rows).astype(jnp.bfloat16))
+        fill(thirds, 0, THIRDS, tensor, 3, dot_right(turned_in[3], rows).astype(jnp.bfloat16))
 
     @pl.when(active)
     def _():
-        spread.wait(0, MEMBERS)
+        head_spread.wait(0, MEMBERS)
 
         def prepare(i, carry):
             delta[i] = jnp.sum(
@@ -818,8 +785,8 @@
         @pl.when(active)
         def _():
             back_tile(j, parts, head_grad, lse, delta, query_sum, head_back)
-            back.start(2 * j)
-            back.start(2 * j + 1)
+            head_return.start(2 * j)
+            head_return.start(2 * j + 1)
 
         return carry
 
@@ -834,7 +801,7 @@
     for unit in units:
         unit.finish(1)
         unit.begin(0)
-    back.wait()
+    head_return.wait()
 
     def project(p, carry):
         part, tensor = p // 2, p % 2
@@ -845,33 +812,35 @@
     lax.fori_loop(0, 6, project, 0)
     for unit in last:
         unit.cross()
-    grad_first = jnp.transpose(dot(w_qkv[...], grad_projected[...].reshape(2304, 256)))
+    grad_first = jnp.transpose(dot(qkv[...], grad_projected[...].reshape(2304, 256)))
     term = jnp.sum(grad_first * normed[...], axis=0, keepdims=True)
     row = lax.broadcasted_iota(jnp.int32, (8, 768), 0)
-    small.start(0, jnp.where(row == 0, term, jnp.where(row == 1, gain_two[...], 0.0)))
+    last_small.start(0, jnp.where(row == 0, term, jnp.where(row == 1, kept_gains[2:3], 0.0)))
     for unit in last:
         unit.begin(2)
-    grad_tokens[...] = middle[...] + norm_back(grad_first, gain[0:1], normed[...], inv_one[...])
+    grad_tokens[...] = middle_grad[...] + norm_back(
+        grad_first, kept_gains[0:1], normed[...], inv_one
+    )
     for u, unit in enumerate(units):
         unit.finish(0)
-        post[u // 3, group.member, pl.ds(16 * (u % 3), 16)] = wholes[unit.at(0, 0)]
+        post[u // 3, owners.member, pl.ds(16 * (u % 3), 16)] = wholes[unit.at(0, 0)]
     for k in range(2):
-        group.start(post, k)
+        owners.start(post, k)
     for stage in (2, 1, 0):
-        total = small.finish(2 - stage)
+        total = last_small.finish(2 - stage)
         if stage > 0:
-            small.start(3 - stage, total)
+            last_small.start(3 - stage, total)
         else:
-            small.start_pair(total)
+            last_small.start_pair(total)
         for unit in last:
             unit.finish(stage)
             if stage > 0:
                 unit.begin(stage - 1)
     for u, unit in enumerate(last):
-        post[2, group.member, pl.ds(16 * u, 16)] = thirds[unit.at(0, 0)]
-    group.start(post, 2)
+        post[2, owners.member, pl.ds(16 * u, 16)] = thirds[unit.at(0, 0)]
+    owners.start(post, 2)
     grad_gains[...] = lax.dot_general(
-        small.finish_pair(),
+        last_small.finish_pair(),
         owned_columns(),
         (((1,), (1,)), ((), ())),
         precision=lax.Precision.HIGHEST,
@@ -879,23 +848,23 @@
     )[0:2]
 
     def own_rows(held, piece):
-        return dot(unshuffle[group.member, piece], held)
+        return dot(unshuffle[owners.member, piece], held)
 
     for k, out in enumerate((grad_up, grad_down)):
-        held = group.finish(post, k)
+        held = owners.finish(post, k)
         for piece in range(4):
             out[:, piece * WIDTH : (piece + 1) * WIDTH] = own_rows(held, piece)[:ROWS]
-    held = group.finish(post, 2)
+    held = owners.finish(post, 2)
     for piece in range(3):
         grad_qkv[piece] = own_rows(held, piece)[:ROWS]
     grad_out[...] = own_rows(held, 3)[:ROWS]
     for k in range(3):
-        group.sent(post, k)
-    spread.sent()
+        owners.sent(post, k)
+    head_spread.sent()
 
     @pl.when(active)
     def _():
-        back.sent()
+        head_return.sent()
 
     for copy in started:
         copy.wait_send()
@@ -953,68 +922,13 @@
 ]
 
 
-def kernel_params(number):
-    return pltpu.CompilerParams(
-        collective_id=number, has_side_effects=True, vmem_limit_bytes=VMEM_BYTES
-    )
-
-
-def forward_pass(tokens, cotangent, shards):
+def layer(tokens, cotangent, shards):
     low = jnp.bfloat16
     return pl.pallas_call(
-        forward_kernel,
-        name="forward_pass",
+        layer_kernel,
+        name="layer",
         out_shape=[
-            wide_array(256, 768),
-            wide_array(256, 1),
             low_array(256, 768),
-            low_array(MEMBERS, 3, HEAD_DIM, 256),
-            low_array(MEMBERS, 1, HEAD_DIM, 256),
-            wide_array(TILES, 1, TILE),
-            low_array(1, HEADS, HEAD_DIM, 256),
-            wide_array(8, 768),
-            low_array(256, 768),
-            low_array(256, 768),
-            low_array(256, 3072),
-            low_array(256, 3072),
-            wide_array(256, 768),
-            low_array(1, HEADS, HEAD_DIM, 256),
-            wide_array(1, 768),
-            low_array(768, 2304),
-        ],
-        in_specs=vmem_specs(9),
-        out_specs=vmem_specs(15) + any_specs(1),
-        scratch_shapes=[
-            pltpu.VMEM((3, 4, SLOT, WIDTH), low),
-            pltpu.VMEM((3, 2, 4, 4, 4, 16, WIDTH), low),
-            pltpu.VMEM((6, 2, 4, 4, 4, 16, WIDTH), low),
-            pltpu.VMEM((768, 2304), low),
-            pltpu.VMEM((768, 768), low),
-            pltpu.VMEM((768, 3072), low),
-            pltpu.VMEM((768, 3072), low),
-            pltpu.VMEM((3, HEADS, HEAD_DIM, 256), low),
-            pltpu.VMEM((TILES * TILE, HEAD_DIM), low),
-        ]
-        + SMALL_SCRATCH
-        + [pltpu.VMEM((256, 768), jnp.float32)] * 2
-        + [pltpu.VMEM((8, 768), jnp.float32)]
-        + sems(48)
-        + sems(96)
-        + sems(9)
-        + sems(10)
-        + sems(MEMBERS)
-        + sems(MEMBERS)
-        + [pltpu.SemaphoreType.DMA],
-        compiler_params=kernel_params(0),
-    )(tokens, cotangent, *shards, select_matrix(), shuffle_matrix())
-
-
-def backward_pass(grad_att, gain, gain_two, inv_one, arrays):
-    low = jnp.bfloat16
-    return pl.pallas_call(
-        backward_kernel,
-        name="backward_pass",
-        out_shape=[
             wide_array(256, 768),
             wide_array(3, ROWS, WIDTH),
             wide_array(ROWS, WIDTH),
@@ -1022,48 +936,81 @@
             wide_array(ROWS, 4 * WIDTH),
             wide_array(2, ROWS),
         ],
-        in_specs=any_specs(1) + vmem_specs(4) + any_specs(12),
-        out_specs=vmem_specs(6),
-        scratch_shapes=[pltpu.VMEM(array.shape, array.dtype) for array in arrays]
+        in_specs=vmem_specs(10),
+        out_specs=vmem_specs(7),
+        scratch_shapes=[
+            pltpu.VMEM((3, 4, SLOT, WIDTH), low),
+            pltpu.VMEM((3, 2, 4, 4, 4, 16, WIDTH), low),
+            pltpu.VMEM((6, 2, 4, 4, 4, 16, WIDTH), low),
+            pltpu.VMEM((768, 2304), low),
+            pltpu.VMEM((768, 768), low),
+            pltpu.VMEM((3, HEADS, HEAD_DIM, 256), low),
+            pltpu.VMEM((TILES * TILE, HEAD_DIM), low),
+        ]
+        + SMALL_SCRATCH
+        + SMALL_SCRATCH
         + [
-            pltpu.VMEM((2, 768, 256), low),
+            pltpu.VMEM((256, 768), jnp.float32),
+            pltpu.VMEM((256, 768), jnp.float32),
+            pltpu.VMEM((8, 768), jnp.float32),
+            pltpu.VMEM((8, 768), jnp.float32),
+            pltpu.VMEM((256, 768), jnp.float32),
+            pltpu.VMEM((MEMBERS, 3, HEAD_DIM, 256), low),
+            pltpu.VMEM((MEMBERS, 1, HEAD_DIM, 256), low),
+            pltpu.VMEM((TILES, 1, TILE), jnp.float32),
+            pltpu.VMEM((1, HEADS, HEAD_DIM, 256), low),
+            pltpu.VMEM((256, 768), low),
+            pltpu.VMEM((256, 3072), low),
+            pltpu.VMEM((256, 3072), low),
+            pltpu.VMEM((256, 768), jnp.float32),
+            pltpu.VMEM((1, HEADS, HEAD_DIM, 256), low),
+            pltpu.VMEM((4, 768, 256), low),
             pltpu.VMEM((3, HEADS, HEAD_DIM, 256), low),
             pltpu.VMEM((MEMBERS, 1, HEAD_DIM, 256), low),
             pltpu.VMEM((MEMBERS, 3, HEAD_DIM, 256), low),
             pltpu.VMEM((TILES, HEAD_DIM, TILE), jnp.float32),
             pltpu.VMEM((TILES, 1, TILE), jnp.float32),
-            pltpu.VMEM((6, 2, 4, 4, 4, 16, WIDTH), low),
-            pltpu.VMEM((3, 2, 4, 4, 4, 16, WIDTH), low),
             pltpu.VMEM((3, 4, SLOT, WIDTH), low),
         ]
         + landing_scratch(6, 16)
         + landing_scratch(3, 16)
-        + SMALL_SCRATCH
-        + [pltpu.SemaphoreType.DMA((12,))]
+        + sems(48)
         + sems(96)
+        + sems(9)
+        + sems(10)
+        + sems(MEMBERS)
+        + sems(MEMBERS)
         + sems(48)
+        + sems(96)
         + sems(9)
         + sems(10)
         + sems(MEMBERS)
         + sems(MEMBERS),
-        compiler_params=kernel_params(1),
-    )(grad_att, unshuffle_matrix(), gain, gain_two, inv_one, *arrays)
+        compiler_params=pltpu.CompilerParams(
+            collective_id=0, has_side_effects=True, vmem_limit_bytes=VMEM_BYTES
+        ),
+    )(tokens, cotangent, *shards, select_matrix(), shuffle_matrix(), unshuffle_matrix())
+
+
+def hand_over_kernel(*refs):
+    count = len(refs) // 2
+    for source, target in zip(refs[:count], refs[count:]):
+        target[...] = source[...]
+
+
+def hand_over(arrays):
+    return pl.pallas_call(
+        hand_over_kernel,
+        name="hand_over",
+        out_shape=[jax.ShapeDtypeStruct(array.shape, array.dtype) for array in arrays],
+        in_specs=vmem_specs(len(arrays)),
+        out_specs=vmem_specs(len(arrays)),
+    )(*arrays)
 
 
 def per_device(tokens, cotangent, w_qkv, w_out, w_up, w_down, norm_gains):
-    (
-        normed_one, inv_one, first_in, parts, head_out, lse, attended, gains,
-        result, second_in, act, hid, grad_middle, grad_att, gain_two_term, qkv,
-    ) = forward_pass(tokens, cotangent, (w_qkv, w_out.T, w_up, w_down.T, norm_gains))
-    grad_tokens, grad_qkv, grad_out, grad_up, grad_down, grad_gains = backward_pass(
-        grad_att,
-        gains,
-        gain_two_term,
-        inv_one,
-        (
-            lse, parts, head_out, act, hid, second_in, cotangent, grad_middle, attended,
-            first_in, normed_one, qkv,
-        ),
+    result, grad_tokens, grad_qkv, grad_out, grad_up, grad_down, grad_gains = hand_over(
+        layer(tokens, cotangent, (w_qkv, w_out.T, w_up, w_down.T, norm_gains))
     )
     return (result, grad_tokens, grad_qkv, grad_out.T, grad_up, grad_down.T, grad_gains)
 

time: 218 us -> 207 us (0.950)
  local copies, waits for them, and re-layouts: 5.92 us -> 0 us
  Pallas kernels: 211 us -> 206 us
    unnamed x19 -> x0, local copies, waits for them, and re-layouts: 5.92 us -> none
    pallas_call x2, Pallas kernels: 211 us -> 206 us  [the longest x1 204 us: layer(): pl.pallas_call(layer_kernel, name='layer', out_shape=[low_array(256, 768)...]
where the time goes in v5:
time: 207 us
  Pallas kernels  206 us (100%)
    pallas_call x1, Pallas kernels, layer(): pl.pallas_call(layer_kernel, name='layer', out_shape=[low_array(256, 768)...  204 us

profile of v5, /device:TPU:1, one launch (start us, length us, event | category | flops | bytes accessed | tf_op | source)
XLA Modules:
  0.0 206.7 jit_solution(18350100287085161884)
XLA Ops:
  0.6 203.6 %layer.1 = (bf16[256,768]{1,0:T(8,128)(2,1)}, f32[256,768]{1,0:T(8,128)}, f32[3,12,384]{2,1,0:T(8,128)}, f32[12,384]{1,0:T(8,128)}, f32[12,1536]{1,0:T(8,128)}, /*index=5*/f32[12,1536]{1,0:T(8,128)}, f32[2,12]{1,0:T(2,128)}) custom-call(bf16[256,768]{1,0:T(8,128)(2,1)} %tokens.1, bf16[256,768]{1,0:T(8,128)(2,1)} %cotangent.1, bf16[3,12,384]{2,1,0:T(8,128)(2,1)} %a_qkv.1, ...), custom_call_target="tpu_custom_call" | custom-call | tf_op jit(solution)/shard_map/layer/pallas_call | solution.py:927
  204.2 2.5 %hand_over.1 = (bf16[256,768]{1,0:T(8,128)(2,1)}, f32[256,768]{1,0:T(8,128)}, f32[3,12,384]{2,1,0:T(8,128)}, f32[12,384]{1,0:T(8,128)}, f32[12,1536]{1,0:T(8,128)}, /*index=5*/f32[12,1536]{1,0:T(8,128)}, f32[2,12]{1,0:T(2,128)}) custom-call(bf16[256,768]{1,0:T(8,128)(2,1)} %get-tuple-element.21.refs_0_, f32[256,768]{1,0:T(8,128)} %get-tuple-element.22.refs_1_, ...), custom_call_target="tpu_custom_call" | custom-call | tf_op jit(solution)/shard_map/hand_over/pallas_call | solution.py:1002

commit v6 on v5

--- a/solution.py
+++ b/solution.py
@@ -14,21 +14,27 @@
 ROWS = 12
 WIDTH = 384
 SLOT = 4 * ROWS
-THIRDS = (("z", "x", "y"), ("x", "y", "z"), ("y", "z", "x"))
-LATER = THIRDS + (("z", "y", "x"), ("y", "x", "z"), ("z", "y", "x"))
+THIRDS = (("w", "x", "y"), ("x", "y", "w"), ("y", "w", "x"))
+LATER = (
+    ("z", "x", "y"), ("x", "y", "z"), ("y", "z", "x"),
+    ("z", "y", "x"), ("y", "x", "z"), ("z", "y", "x"),
+)
+SIZES = dict(x=4, y=4, z=4, w=2, c=2)
 MESH = pl.DeviceIdType.MESH
-VMEM_BYTES = 60 * 1024 * 1024
+VMEM_BYTES = 62 * 1024 * 1024
 epsilon = 1e-05
 neg_large = -1e30
 
 
 def place():
     dp, ctx, tensor = lax.axis_index("dp"), lax.axis_index("ctx"), lax.axis_index("tensor")
-    return dict(x=dp // 2, y=ctx // 2, z=2 * tensor + dp % 2, c=ctx % 2)
+    return dict(x=dp // 2, y=ctx // 2, z=2 * tensor + dp % 2, w=dp % 2, c=ctx % 2)
 
 
 def device_at(pos, axis, index):
     at = dict(pos)
+    if axis == "w":
+        axis, index = "z", 2 * (pos["z"] // 2) + index
     at[axis] = index
     return (at["x"] * 2 + at["z"] % 2, at["y"] * 2 + at["c"], at["z"] // 2)
 
@@ -36,7 +42,7 @@
 def beside(pos, axis, by):
     if axis == "c":
         return device_at(pos, "c", 1 - pos["c"])
-    return device_at(pos, axis, (pos[axis] + by) % 4)
+    return device_at(pos, axis, (pos[axis] + by) % SIZES[axis])
 
 
 def greet(pos):
@@ -139,58 +145,62 @@
 
 
 class Unit:
-    def __init__(self, pos, order, unit, send, recv, started):
-        self.pos, self.order, self.unit = pos, order, unit
-        self.send, self.recv, self.started = send, recv, started
+    def __init__(self, pos, order, held, lead, sems, number, started):
+        self.pos, self.order, self.held, self.lead = pos, order, held, lead
+        self.send, self.recv = sems
+        self.number, self.started = number, started
         self.sibling = beside(pos, "c", 1)
+        self.sizes = [SIZES[axis] for axis in order]
 
     def move(self, src, dst, sem, device):
-        sem = self.unit * 16 + sem
+        sem = self.number * 16 + sem
         copy = remote(src, dst, self.send.at[sem], self.recv.at[sem], device)
         copy.start()
         self.started.append(copy)
 
     def arrived(self, dst, sem):
-        sem = self.unit * 16 + sem
+        sem = self.number * 16 + sem
         remote(dst, dst, self.send.at[sem], self.recv.at[sem], self.sibling).wait_recv()
 
     def along(self, stage, by):
         return beside(self.pos, self.order[stage], by)
 
+    def steps(self, stage):
+        return (1, 3, 2) if self.sizes[stage] == 4 else (1,)
+
+    def place3(self, by):
+        return (self.pos[self.order[2]] + by) % self.sizes[2]
+
     def at(self, stage, by):
-        index = ((self.pos[self.order[stage]] + by) % 4,)
+        index = ((self.pos[self.order[stage]] + by) % self.sizes[stage],)
         for later in range(stage + 1, 3):
             index = (self.pos[self.order[later]],) + index
-        return (self.unit, self.pos["c"]) + index
+        return self.lead + (self.pos["c"],) + index
 
 
 class Gather(Unit):
-    def __init__(self, pos, order, unit, held, send, recv, started):
-        super().__init__(pos, order, unit, send, recv, started)
-        self.held = held
-
     def pass_on(self, index, sem, device):
         self.move(self.held.at[index], self.held.at[index], sem, device)
 
     def begin(self, stage):
-        for by in (1, 3, 2):
+        for by in self.steps(stage):
             self.pass_on(self.at(stage, 0), stage * 3 + by - 1, self.along(stage, by))
         if stage == 2:
             self.share(0)
 
     def finish(self, stage):
-        for by in (1, 3, 2):
-            self.arrived(self.held.at[self.at(stage, 4 - by)], stage * 3 + by - 1)
+        for by in self.steps(stage):
+            back = self.sizes[stage] - by
+            self.arrived(self.held.at[self.at(stage, back)], stage * 3 + by - 1)
             if stage == 2:
-                self.share(4 - by)
+                self.share(back)
 
     def share(self, by):
         self.pass_on(self.at(2, by), 9 + by, self.sibling)
 
     def settle(self):
-        place3 = self.pos[self.order[2]]
-        for by in (0, 3, 1, 2):
-            index = (self.unit, 1 - self.pos["c"], (place3 + by) % 4)
+        for by in range(self.sizes[2]):
+            index = self.lead + (1 - self.pos["c"], self.place3(by))
             self.arrived(self.held.at[index], 9 + by)
 
 
@@ -199,51 +209,50 @@
 
 
 class Reduce(Unit):
-    def __init__(self, pos, order, unit, held, landing, send, recv, started):
-        super().__init__(pos, order, unit, send, recv, started)
-        self.held, self.cores, self.coming = held, landing[0], landing[1:]
-
-    def add(self, index, sources, *counts):
-        held = self.held
+    def __init__(self, pos, order, held, lead, landing, sems, number, started):
+        super().__init__(pos, order, held, lead, sems, number, started)
+        self.cores, self.coming = landing[0], landing[1:]
+
+    def add(self, stage, index, sources):
+        held, inner = self.held, self.sizes[:stage]
 
         def one(slot):
-            total = wide(held[index + slot])
-            for source, at in sources:
-                total = total + wide(source[at + slot])
-            held[index + slot] = total.astype(jnp.bfloat16)
+            terms = [held[index + slot]] + [source[at + slot] for source, at in sources]
+            while len(terms) > 1:
+                terms = [sum(terms[n : n + 2][1:], terms[n]) for n in range(0, len(terms), 2)]
+            held[index + slot] = terms[0]
 
         def body(i, carry):
-            one((i // 4, i % 4) if len(counts) == 2 else (i,))
+            one((i // inner[0], i % inner[0]) if stage == 2 else (i,))
             return carry
 
-        if counts:
-            lax.fori_loop(0, 4 ** len(counts), body, 0)
+        if stage:
+            lax.fori_loop(0, int(np.prod(inner)), body, 0)
         else:
             one(())
 
     def cross(self):
-        place3, u = self.pos[self.order[2]], self.unit
-        for by in (1, 3, 2, 0):
-            index = (place3 + by) % 4
+        for by in (*self.steps(2), 0):
+            index = self.place3(by)
             self.move(
-                self.held.at[u, 1 - self.pos["c"], index],
-                self.cores.at[u, index],
+                self.held.at[self.lead + (1 - self.pos["c"], index)],
+                self.cores.at[self.lead + (index,)],
                 9 + by,
                 self.sibling,
             )
 
     def take_core(self, by):
-        index = (self.pos[self.order[2]] + by) % 4
-        self.arrived(self.cores.at[self.unit, index], 9 + by)
-        self.add(self.at(2, by), [(self.cores, (self.unit, index))], 4, 4)
+        index = self.lead + (self.place3(by),)
+        self.arrived(self.cores.at[index], 9 + by)
+        self.add(2, self.at(2, by), [(self.cores, index)])
 
     def begin(self, stage):
-        for by in (1, 3, 2):
+        for by in self.steps(stage):
             if stage == 2:
                 self.take_core(by)
             self.move(
                 self.held.at[self.at(stage, by)],
-                self.coming[stage].at[self.unit, by - 1],
+                self.coming[stage].at[self.lead + (by - 1,)],
                 stage * 3 + by - 1,
                 self.along(stage, by),
             )
@@ -251,53 +260,43 @@
     def finish(self, stage):
         if stage == 2:
             self.take_core(0)
-        for by in (1, 3, 2):
-            self.arrived(self.coming[stage].at[self.unit, by - 1], stage * 3 + by - 1)
-        self.add(
-            self.at(stage, 0),
-            [(self.coming[stage], (self.unit, i)) for i in range(3)],
-            *(4,) * stage,
-        )
-
-
-def landing_scratch(units, rows):
-    low, slot = jnp.bfloat16, (rows, WIDTH)
+        sources = [(self.coming[stage], self.lead + (by - 1,)) for by in self.steps(stage)]
+        for by in self.steps(stage):
+            self.arrived(self.coming[stage].at[self.lead + (by - 1,)], stage * 3 + by - 1)
+        self.add(stage, self.at(stage, 0), sources)
+
+
+def buffer_scratch(order, lead=()):
+    n1, n2, n3 = (SIZES[axis] for axis in order)
+    return pltpu.VMEM(lead + (2, n3, n2, n1, 16, WIDTH), jnp.bfloat16)
+
+
+def landing_scratch(order, lead=()):
+    n1, n2, n3 = (SIZES[axis] for axis in order)
     return [
-        pltpu.VMEM((units, 4, 4, 4) + slot, low),
-        pltpu.VMEM((units, 3) + slot, low),
-        pltpu.VMEM((units, 3, 4) + slot, low),
-        pltpu.VMEM((units, 3, 4, 4) + slot, low),
+        pltpu.VMEM(lead + shape + (16, WIDTH), jnp.bfloat16)
+        for shape in ((n3, n2, n1), (n1 - 1,), (n2 - 1, n1), (n3 - 1, n2, n1))
     ]
 
 
-def slots_of(group, orders):
-    x, z_lo, y_half = group // 4, (group // 2) % 2, group % 2
-    for tensor in range(2):
+def copy_thirds(thirds, qkv, out, tensor):
+    def body(group, carry):
         for piece in range(4):
-            at = dict(x=x, z=2 * tensor + z_lo, y=2 * y_half + piece // 2)
-            yield tensor, piece, [
-                (piece % 2, at[order[2]], at[order[1]], at[order[0]]) for order in orders
-            ]
-
-
-def column_of(tensor, piece):
-    return (0, (piece * 2 + tensor) * WIDTH) if piece < 3 else (1, tensor * WIDTH)
-
-
-def copy_thirds(thirds, whole):
-    def body(group, carry):
-        for tensor, piece, indices in slots_of(group, THIRDS):
-            which, column = column_of(tensor, piece)
-            for third, index in enumerate(indices):
+            for third, order in enumerate(THIRDS):
                 rows = pl.ds(pl.multiple_of(group * SLOT + 16 * third, 16), 16)
-                whole[which][rows, pl.ds(column, WIDTH)] = thirds[(third,) + index]
+                value = thirds[third][slot_index(order, group, 0, piece)]
+                if piece < 3:
+                    qkv[rows, piece * WIDTH : (piece + 1) * WIDTH] = value
+                else:
+                    out[tensor, rows] = value
         return carry
 
     lax.fori_loop(0, 16, body, 0)
 
 
 def slot_index(order, group, tensor, piece):
-    at = dict(x=group // 4, z=2 * tensor + (group // 2) % 2, y=2 * (group % 2) + piece // 2)
+    z_lo = (group // 2) % 2
+    at = dict(x=group // 4, z=2 * tensor + z_lo, w=z_lo, y=2 * (group % 2) + piece // 2)
     return (piece % 2, at[order[2]], at[order[1]], at[order[0]])
 
 
@@ -316,8 +315,11 @@
     for group in range(16):
         for third, order in enumerate(orders):
             row = group * SLOT + 16 * third
-            index = (first + third,) + slot_index(order, group, tensor, piece)
-            slots[index] = value[row : row + 16]
+            index = slot_index(order, group, tensor, piece)
+            if first is None:
+                slots[third][index] = value[row : row + 16]
+            else:
+                slots[(first + third,) + index] = value[row : row + 16]
 
 
 def head_place(head):
@@ -330,21 +332,51 @@
     return tensor * 6 + (1 - core) * y + core * (4 + y // 2), core * (y % 2) == 0
 
 
+class Sequence:
+    members, heads = MEMBERS, HEADS
+
+    def __init__(self):
+        self.dp = lax.axis_index("dp")
+        ctx, tensor = lax.axis_index("ctx"), lax.axis_index("tensor")
+        self.number, self.head = 2 * ctx + tensor, own_head(ctx, tensor)[0]
+
+    def device(self, number):
+        return (self.dp, number // 2, number % 2)
+
+    def of_head(self, head):
+        ctx, tensor = head_place(head)
+        return 2 * ctx + tensor
+
+
+class Half(Sequence):
+    members, heads = MEMBERS // 2, HEADS // 2
+
+    def __init__(self):
+        super().__init__()
+        self.tensor = lax.axis_index("tensor")
+        self.number, self.head = lax.axis_index("ctx"), self.head % 6
+
+    def device(self, number):
+        return (self.dp, number, self.tensor)
+
+    def of_head(self, head):
+        return head_place(head)[0]
+
+
 class ToHeads:
-    def __init__(self, src, dst, send, recv):
-        self.src, self.dst, self.send, self.recv = src, dst, send, recv
-        self.dp, self.number = lax.axis_index("dp"), member_number()
+    def __init__(self, seats, src, dst, sems):
+        self.seats, self.src, self.dst, (self.send, self.recv) = seats, src, dst, sems
 
     def copies(self, i):
-        head = (self.number + i) % HEADS
-        ctx, tensor = head_place(head)
-        local = 2 * ctx + tensor == self.number
-        src, dst = self.src.at[:, head], self.dst.at[self.number]
-        recv = self.recv.at[self.number]
+        seats = self.seats
+        head = (seats.number + i) % seats.heads
+        to = seats.of_head(head)
+        src, dst = self.src.at[:, head], self.dst.at[seats.number]
+        recv = self.recv.at[seats.number]
         return (
-            local,
+            to == seats.number,
             lambda: pltpu.make_async_copy(src, dst, recv),
-            lambda: remote(src, dst, self.send.at[head], recv, (self.dp, ctx, tensor)),
+            lambda: remote(src, dst, self.send.at[head], recv, seats.device(to)),
         )
 
     def start(self):
@@ -361,19 +393,19 @@
 
             return carry
 
-        lax.fori_loop(0, HEADS, body, 0)
+        lax.fori_loop(0, self.seats.heads, body, 0)
 
     def wait(self, first, last):
         def body(i, carry):
             src, dst, recv = self.src.at[:, 0], self.dst.at[i], self.recv.at[i]
 
-            @pl.when(i == self.number)
+            @pl.when(i == self.seats.number)
             def _():
                 pltpu.make_async_copy(src, dst, recv).wait()
 
-            @pl.when(i != self.number)
+            @pl.when(i != self.seats.number)
             def _():
-                remote(src, dst, self.send.at[0], recv, (self.dp, i // 2, i % 2)).wait_recv()
+                remote(src, dst, self.send.at[0], recv, self.seats.device(i)).wait_recv()
 
             return carry
 
@@ -389,59 +421,59 @@
 
             return carry
 
-        lax.fori_loop(0, HEADS, body, 0)
+        lax.fori_loop(0, self.seats.heads, body, 0)
 
 
 class FromHeads:
-    def __init__(self, src, dst, send, recv):
-        self.src, self.dst, self.send, self.recv = src, dst, send, recv
-        self.dp, self.number = lax.axis_index("dp"), member_number()
-        self.head = own_head(lax.axis_index("ctx"), lax.axis_index("tensor"))[0]
+    def __init__(self, seats, src, dst, sems):
+        self.seats, self.src, self.dst, (self.send, self.recv) = seats, src, dst, sems
 
     def outside(self, to):
+        head = self.seats.head
         return remote(
             self.src.at[to],
-            self.dst.at[:, self.head],
+            self.dst.at[:, head],
             self.send.at[to],
-            self.recv.at[self.head],
-            (self.dp, to // 2, to % 2),
+            self.recv.at[head],
+            self.seats.device(to),
         )
 
     def start(self, to):
-        @pl.when(to == self.number)
+        head = self.seats.head
+
+        @pl.when(to == self.seats.number)
         def _():
             pltpu.make_async_copy(
-                self.src.at[to], self.dst.at[:, self.head], self.recv.at[self.head]
+                self.src.at[to], self.dst.at[:, head], self.recv.at[head]
             ).start()
 
-        @pl.when(to != self.number)
+        @pl.when(to != self.seats.number)
         def _():
             self.outside(to).start()
 
     def wait(self):
         def body(i, carry):
-            ctx, tensor = head_place(i)
-            local = 2 * ctx + tensor == self.number
+            owner = self.seats.of_head(i)
             src, dst, recv = self.src.at[0], self.dst.at[:, i], self.recv.at[i]
 
-            @pl.when(local)
+            @pl.when(owner == self.seats.number)
             def _():
                 pltpu.make_async_copy(src, dst, recv).wait()
 
-            @pl.when(jnp.logical_not(local))
+            @pl.when(owner != self.seats.number)
             def _():
-                remote(src, dst, self.send.at[0], recv, (self.dp, ctx, tensor)).wait_recv()
+                remote(src, dst, self.send.at[0], recv, self.seats.device(owner)).wait_recv()
 
             return carry
 
-        lax.fori_loop(0, HEADS, body, 0)
+        lax.fori_loop(0, self.seats.heads, body, 0)
 
     def sent(self):
         def body(i, carry):
-            self.outside((self.number + i) % MEMBERS).wait_send()
+            self.outside((self.seats.number + i) % self.seats.members).wait_send()
             return carry
 
-        lax.fori_loop(1, MEMBERS, body, 0)
+        lax.fori_loop(1, self.seats.members, body, 0)
 
 
 TILE = 512
@@ -477,8 +509,8 @@
 
 def attend_tile(i, parts, keys, out, lse):
     own_rows = pl.ds(pl.multiple_of(i * TILE, TILE), TILE)
-    keys[own_rows, :] = turned(two(parts, i, 1))
-    query = two(parts, i, 0) * jnp.bfloat16(HEAD_DIM ** -0.5)
+    keys[own_rows, :] = turned(parts[i, 1])
+    query = parts[i, 0] * jnp.bfloat16(HEAD_DIM ** -0.5)
 
     def step(scores, values, state):
         top, total, weighted = state
@@ -492,22 +524,26 @@
     def rows_of(j, tiles):
         return keys[pl.ds(pl.multiple_of(j * TILE, TILE), tiles * TILE), :]
 
-    def pair(n, state):
-        values = jnp.concatenate([two(parts, 2 * n, 2), two(parts, 2 * n + 1, 2)], axis=1)
-        return step(dot(rows_of(2 * n, 2), query), values, state)
-
-    def single(j, state):
-        return step(dot(rows_of(j, 1), query), two(parts, j, 2), state)
+    def some(tiles, first):
+        def body(n, state):
+            j = first + tiles * n
+            values = jnp.concatenate([parts[j + m, 2] for m in range(tiles)], axis=1)
+            return step(dot(rows_of(j, tiles), query), values, state)
+
+        return body
 
     state = (
         jnp.full((1, TILE), neg_large, jnp.float32),
         jnp.zeros((1, TILE), jnp.float32),
         jnp.zeros((HEAD_DIM, TILE), jnp.float32),
     )
-    state = lax.fori_loop(0, i // 2, pair, state)
-    state = lax.fori_loop(2 * (i // 2), i, single, state)
+    first = 0
+    for tiles in (4, 2, 1):
+        count = (i - first) // tiles
+        state = lax.fori_loop(0, count, some(tiles, first), state)
+        first = first + count * tiles
     masked = jnp.where(allowed_tile(), dot(rows_of(i, 1), query), neg_large)
-    top, total, weighted = step(masked, two(parts, i, 2), state)
+    top, total, weighted = step(masked, parts[i, 2], state)
     put_two(out, i, 0, (weighted / total).astype(jnp.bfloat16))
     lse[i] = top + jnp.log(total)
 
@@ -544,72 +580,82 @@
 
 
 def back_tile(j, parts, grad_att, lse, delta, query_sum, out):
-    key_cols, value_cols = two(parts, j, 1), two(parts, j, 2)
+    key_cols, value_cols = parts[j, 1], parts[j, 2]
     key_rows, value_rows = turned(key_cols), turned(value_cols)
 
-    def step(i, state, diagonal):
+    def step(i, state, tiles, diagonal=False):
         key_sum, value_sum = state
-        query = two(parts, i, 0) * jnp.bfloat16(HEAD_DIM ** -0.5)
-        grad = two(grad_att, i, 0)
-        shares = jnp.exp(dot(key_rows, query) - lse[i])
+
+        def side_by_side(piece):
+            return jnp.concatenate([piece(i + m) for m in range(tiles)], axis=1)
+
+        query = side_by_side(lambda n: parts[n, 0]) * jnp.bfloat16(HEAD_DIM ** -0.5)
+        grad = side_by_side(lambda n: two(grad_att, n, 0))
+        shares = jnp.exp(dot(key_rows, query) - side_by_side(lambda n: lse[n]))
         if diagonal:
             shares = jnp.where(allowed_tile(), shares, 0.0)
-        grad_scores = (shares * (dot(value_rows, grad) - delta[i])).astype(jnp.bfloat16)
-        query_sum[i] += dot(key_cols, grad_scores)
+        grad_scores = shares * (dot(value_rows, grad) - side_by_side(lambda n: delta[n]))
+        grad_scores = grad_scores.astype(jnp.bfloat16)
+        query_add = dot(key_cols, grad_scores)
+        for m in range(tiles):
+            query_sum[i + m] += query_add[:, m * TILE : (m + 1) * TILE]
         key_sum = key_sum + dot_right(query, grad_scores)
         value_sum = value_sum + dot_right(grad, shares.astype(jnp.bfloat16))
         return key_sum, value_sum
 
     zero = jnp.zeros((HEAD_DIM, TILE), jnp.float32)
-    state = step(j, (zero, zero), True)
+    state = step(j, (zero, zero), 1, True)
     pairs = (TILES - 1 - j) // 2
-    rest = j + 1 + 2 * pairs
-
-    def pair(n, state):
-        i = j + 1 + 2 * n
-        return step(i + 1, step(i, state, False), False)
-
-    state = lax.fori_loop(0, pairs, pair, state)
+    state = lax.fori_loop(0, pairs, lambda n, state: step(j + 1 + 2 * n, state, 2), state)
     key_sum, value_sum = lax.fori_loop(
-        rest, TILES, lambda i, state: step(i, state, False), state
+        j + 1 + 2 * pairs, TILES, lambda i, state: step(i, state, 1), state
     )
-    put_two(out, j, 0, (query_sum[j] * HEAD_DIM ** -0.5).astype(jnp.bfloat16))
-    put_two(out, j, 1, key_sum.astype(jnp.bfloat16))
-    put_two(out, j, 2, value_sum.astype(jnp.bfloat16))
+    out[j, 0] = (query_sum[j] * HEAD_DIM ** -0.5).astype(jnp.bfloat16)
+    out[j, 1] = key_sum.astype(jnp.bfloat16)
+    out[j, 2] = value_sum.astype(jnp.bfloat16)
 
 
 def layer_kernel(
     tokens, cotangent, a_qkv, a_out, b, c, gain, select, shuffle, unshuffle,
     result, grad_tokens, grad_qkv, grad_out, grad_up, grad_down, grad_gains,
-    pre, thirds, wholes, qkv, out, projected, keys, ring, pair, last_ring, last_pair,
+    pre, blocks, thirds, wholes, qkv, out, projected, keys, small_buffers, last_buffers,
     forth_sum, back_sum, own_gain, kept_gains, normed, parts, head_out, lse, attended, second,
-    act, hid, middle_grad, grad_att, turned_in, grad_projected, head_grad, head_back,
-    query_sum, delta, post,
-    cores_w, ends1_w, ends2_w, ends3_w, cores_t, ends1_t, ends2_t, ends3_t,
-    third_send, third_recv, whole_send, whole_recv, pre_send, pre_recv, small_send, small_recv,
-    to_send, to_recv, from_send, from_recv,
-    back_third_send, back_third_recv, back_whole_send, back_whole_recv, post_send, post_recv,
-    last_small_send, last_small_recv, to_grad_send, to_grad_recv, from_grad_send, from_grad_recv,
+    act, hid, middle_grad, grad_att, turned_in, first_turned, grad_projected, head_grad,
+    head_back, query_sum, delta, post, out_grads, out_coming, first_grads, first_coming,
+    landing_w, landing_t,
+    third_sems, whole_sems, pre_sems, small_sems, to_sems, from_sems,
+    back_third_sems, back_whole_sems, post_sems, last_small_sems, to_grad_sems, from_grad_sems,
+    swap_sems,
 ):
     pos = place()
     active = own_head(lax.axis_index("ctx"), lax.axis_index("tensor"))[1]
-    group = Group(pos, pre_send, pre_recv)
-    owners = Group(pos, post_send, post_recv)
-    small = SmallSum(pos, ring, pair, small_send, small_recv)
-    last_small = SmallSum(pos, last_ring, last_pair, last_small_send, last_small_recv)
+    tensor = lax.axis_index("tensor")
+    partner = beside(pos, "z", 2)
+    group, owners = Group(pos, *pre_sems), Group(pos, *post_sems)
+    small = SmallSum(pos, *small_buffers, *small_sems)
+    last_small = SmallSum(pos, *last_buffers, *last_small_sems)
     started = []
     first = [
-        Gather(pos, order, u, thirds, third_send, third_recv, started)
+        Gather(pos, order, thirds[u], (), third_sems, u, started)
         for u, order in enumerate(THIRDS)
     ]
     later = [
-        Gather(pos, order, u, wholes, whole_send, whole_recv, started)
+        Gather(pos, order, wholes, (u,), whole_sems, u, started)
         for u, order in enumerate(LATER)
     ]
-    spread = ToHeads(projected, parts, to_send, to_recv)
-    back = FromHeads(head_out, attended, from_send, from_recv)
-    head_spread = ToHeads(grad_att, head_grad, to_grad_send, to_grad_recv)
-    head_return = FromHeads(head_back, grad_projected, from_grad_send, from_grad_recv)
+    spread = ToHeads(Half(), projected, parts, to_sems)
+    back = FromHeads(Sequence(), head_out, attended, from_sems)
+    head_spread = ToHeads(Sequence(), grad_att, head_grad, to_grad_sems)
+    head_return = FromHeads(Half(), head_back, grad_projected, from_grad_sems)
+
+    def swap(n, src, dst):
+        return remote(src, dst, swap_sems[0].at[n], swap_sems[1].at[n], partner)
+
+    blocks[tensor] = tokens[...]
+    swap_tokens = swap(0, blocks.at[tensor], blocks.at[tensor])
+    swap_out = swap(1, out.at[tensor], out.at[tensor])
+    swap_grads = swap(2, out_grads.at[1 - tensor], out_coming)
+    swap_first = swap(3, first_grads.at[1 - tensor], first_coming)
     slots = (
         sum(dot(select[j], a_qkv[j]) for j in range(3)) + dot(select[3], a_out[...]),
         sum(dot(select[j], b[:, j * WIDTH : (j + 1) * WIDTH]) for j in range(4)),
@@ -622,6 +668,7 @@
     greet(pos)
     for k in range(3):
         group.start(pre, k)
+    swap_tokens.start()
     small.start(0, own_gain[...])
 
     def sorted_piece(k):
@@ -629,14 +676,16 @@
 
     piece = sorted_piece(0)
     for u, unit in enumerate(first):
-        thirds[unit.at(0, 0)] = piece[16 * u : 16 * (u + 1)]
+        thirds[u][unit.at(0, 0)] = piece[16 * u : 16 * (u + 1)]
         unit.begin(0)
     for k in (1, 2):
         piece = sorted_piece(k)
         for u in range(3):
             wholes[later[3 * k - 3 + u].at(0, 0)] = piece[16 * u : 16 * (u + 1)]
     normed_one, inv_one = norm_parts(wide(tokens[...]))
-    normed[...] = normed_one
+    normed[tensor] = normed_one
+    swap(0, blocks.at[1 - tensor], blocks.at[1 - tensor]).wait_recv()
+    normed[1 - tensor] = norm_parts(wide(blocks[1 - tensor]))[0]
     for stage in range(3):
         for unit in first:
             unit.finish(stage)
@@ -655,16 +704,16 @@
         unit.begin(1)
     for unit in first:
         unit.settle()
-    copy_thirds(thirds, (qkv, out))
+    copy_thirds(thirds, qkv, out, tensor)
+    swap_out.start()
     gains = small.finish_pair()
     kept_gains[...] = gains
-    first_in = (normed[...] * gains[0:1]).astype(jnp.bfloat16)
+    first_in = (normed[...].reshape(512, 768) * gains[0:1]).astype(jnp.bfloat16)
     for part in range(3):
-        for tensor in range(2):
-            column = (part * 2 + tensor) * WIDTH
-            cols = jnp.transpose(dot(first_in, qkv[:, pl.ds(column, WIDTH)])).astype(jnp.bfloat16)
-            for head in range(6):
-                projected[part, tensor * 6 + head] = cols[head * HEAD_DIM : (head + 1) * HEAD_DIM]
+        cols = dot(first_in, qkv[:, part * WIDTH : (part + 1) * WIDTH])
+        cols = jnp.transpose(cols).astype(jnp.bfloat16)
+        for head in range(6):
+            projected[part, head] = cols[head * HEAD_DIM : (head + 1) * HEAD_DIM]
     spread.start()
     for unit in later:
         unit.finish(1)
@@ -674,26 +723,33 @@
         turned_in[n] = jnp.transpose(value).astype(jnp.bfloat16)
 
     flip(0, wide(cotangent[...]))
-    flip(1, wide(first_in))
+    first_turned[...] = jnp.transpose(wide(first_in)).astype(jnp.bfloat16)
 
     def per_queries(i, carry):
         @pl.when(active)
         def _():
-            spread.wait(2 * i, 2 * i + 2)
+            spread.wait(i, i + 1)
             attend_tile(i, parts, keys, head_out, lse)
             back.start(2 * i)
             back.start(2 * i + 1)
 
         return carry
 
-    lax.fori_loop(0, 7, per_queries, 0)
-    for unit in later:
+    lax.fori_loop(0, 6, per_queries, 0)
+    later[0].finish(2)
+    lax.fori_loop(6, 7, per_queries, 0)
+    for unit in later[1:]:
         unit.finish(2)
     lax.fori_loop(7, 8, per_queries, 0)
     for unit in later:
         unit.settle()
     back.wait()
-    weighted = jnp.transpose(dot(out[...], attended[0].reshape(768, 256)))
+    swap(1, out.at[1 - tensor], out.at[1 - tensor]).wait_recv()
+
+    def half_attended(half):
+        return attended[0, 6 * half : 6 * (half + 1)].reshape(WIDTH, 256)
+
+    weighted = jnp.transpose(dot(out[0], half_attended(0)) + dot(out[1], half_attended(1)))
     middle = wide(tokens[...]) + weighted
     normed_two, inv_two = norm_parts(middle)
     second_in = (normed_two * kept_gains[1:2]).astype(jnp.bfloat16)
@@ -723,12 +779,14 @@
     )
     middle_grad[...] = grad_middle
     kept_gains[2:3] = gain_two_term
-    grads = jnp.transpose(dot(grad_middle.astype(jnp.bfloat16), out[...])).astype(jnp.bfloat16)
-    for head in range(HEADS):
-        grad_att[0, head] = grads[head * HEAD_DIM : (head + 1) * HEAD_DIM]
+    for half in range(2):
+        grads = dot(grad_middle.astype(jnp.bfloat16), out[half])
+        grads = jnp.transpose(grads).astype(jnp.bfloat16)
+        for head in range(6):
+            grad_att[0, 6 * half + head] = grads[head * HEAD_DIM : (head + 1) * HEAD_DIM]
     head_spread.start()
-    flip(2, wide(second[...]))
-    flip(3, middle_grad[...])
+    flip(1, wide(second[...]))
+    flip(2, middle_grad[...])
     spread.sent()
 
     @pl.when(active)
@@ -741,22 +799,17 @@
         copy.wait_send()
     started = []
     units = [
-        Reduce(
-            pos, order, u, wholes, (cores_w, ends1_w, ends2_w, ends3_w), back_whole_send, back_whole_recv,
-            started,
-        )
+        Reduce(pos, order, wholes, (u,), landing_w, back_whole_sems, u, started)
         for u, order in enumerate(LATER)
     ]
     last = [
-        Reduce(
-            pos, order, u, thirds, (cores_t, ends1_t, ends2_t, ends3_t), back_third_send, back_third_recv,
-            started,
-        )
+        Reduce(pos, order, thirds[u], (), landing_t[u], back_third_sems, u, started)
         for u, order in enumerate(THIRDS)
     ]
+
     def give(p, carry):
         columns = pl.ds(pl.multiple_of(p * WIDTH, WIDTH), WIDTH)
-        for k, (left, right) in enumerate(((2, hid), (0, act))):
+        for k, (left, right) in enumerate(((1, hid), (0, act))):
             value = dot(turned_in[left], right[:, columns]).astype(jnp.bfloat16)
             fill(wholes, 3 * k, LATER[3 * k : 3 * k + 3], p // 4, p % 4, value)
         return carry
@@ -764,9 +817,9 @@
     lax.fori_loop(0, 8, give, 0)
     for unit in units:
         unit.cross()
-    for tensor in range(2):
-        rows = attended[0, 6 * tensor : 6 * (tensor + 1)].reshape(WIDTH, 256)
-        fill(thirds, 0, THIRDS, tensor, 3, dot_right(turned_in[3], rows).astype(jnp.bfloat16))
+    for half in range(2):
+        out_grads[half] = dot_right(turned_in[2], half_attended(half)).astype(jnp.bfloat16)
+    swap_grads.start()
 
     @pl.when(active)
     def _():
@@ -785,41 +838,41 @@
         @pl.when(active)
         def _():
             back_tile(j, parts, head_grad, lse, delta, query_sum, head_back)
-            head_return.start(2 * j)
-            head_return.start(2 * j + 1)
+            head_return.start(j)
 
         return carry
 
     lax.fori_loop(0, 1, per_keys, 0)
     for unit in units:
         unit.begin(2)
-    lax.fori_loop(1, 5, per_keys, 0)
+    lax.fori_loop(1, 8, per_keys, 0)
     for unit in units:
         unit.finish(2)
         unit.begin(1)
-    lax.fori_loop(5, 8, per_keys, 0)
-    for unit in units:
-        unit.finish(1)
-        unit.begin(0)
     head_return.wait()
 
-    def project(p, carry):
-        part, tensor = p // 2, p % 2
-        rows = grad_projected[part, pl.ds(6 * tensor, 6)].reshape(WIDTH, 256)
-        fill(thirds, 0, THIRDS, tensor, part, dot_right(turned_in[1], rows).astype(jnp.bfloat16))
-        return carry
-
-    lax.fori_loop(0, 6, project, 0)
+    swap(2, out_grads.at[0], out_coming).wait_recv()
+    fill(thirds, None, THIRDS, 0, 3, out_grads[tensor] + out_coming[...])
+    for part in range(3):
+        rows = grad_projected[part].reshape(WIDTH, 512)
+        fill(thirds, None, THIRDS, 0, part, dot_right(first_turned[...], rows).astype(jnp.bfloat16))
     for unit in last:
         unit.cross()
-    grad_first = jnp.transpose(dot(qkv[...], grad_projected[...].reshape(2304, 256)))
-    term = jnp.sum(grad_first * normed[...], axis=0, keepdims=True)
+    first_parts = jnp.transpose(dot(qkv[...], grad_projected[...].reshape(3 * WIDTH, 512)))
+    first_grads[...] = first_parts.astype(jnp.bfloat16).reshape(2, 256, 768)
+    swap_first.start()
+    term = jnp.sum(first_parts * normed[...].reshape(512, 768), axis=0, keepdims=True)
     row = lax.broadcasted_iota(jnp.int32, (8, 768), 0)
     last_small.start(0, jnp.where(row == 0, term, jnp.where(row == 1, kept_gains[2:3], 0.0)))
     for unit in last:
         unit.begin(2)
+    for unit in units:
+        unit.finish(1)
+        unit.begin(0)
+    swap(3, first_grads.at[0], first_coming).wait_recv()
+    grad_first = wide(first_grads[tensor]) + wide(first_coming[...])
     grad_tokens[...] = middle_grad[...] + norm_back(
-        grad_first, kept_gains[0:1], normed[...], inv_one
+        grad_first, kept_gains[0:1], normed[tensor], inv_one
     )
     for u, unit in enumerate(units):
         unit.finish(0)
@@ -837,7 +890,7 @@
             if stage > 0:
                 unit.begin(stage - 1)
     for u, unit in enumerate(last):
-        post[2, owners.member, pl.ds(16 * u, 16)] = thirds[unit.at(0, 0)]
+        post[2, owners.member, pl.ds(16 * u, 16)] = thirds[u][unit.at(0, 0)]
     owners.start(post, 2)
     grad_gains[...] = lax.dot_general(
         last_small.finish_pair(),
@@ -861,6 +914,8 @@
     for k in range(3):
         owners.sent(post, k)
     head_spread.sent()
+    for copy in (swap_tokens, swap_out, swap_grads, swap_first):
+        copy.wait_send()
 
     @pl.when(active)
     def _():
@@ -940,22 +995,21 @@
         out_specs=vmem_specs(7),
         scratch_shapes=[
             pltpu.VMEM((3, 4, SLOT, WIDTH), low),
-            pltpu.VMEM((3, 2, 4, 4, 4, 16, WIDTH), low),
-            pltpu.VMEM((6, 2, 4, 4, 4, 16, WIDTH), low),
-            pltpu.VMEM((768, 2304), low),
-            pltpu.VMEM((768, 768), low),
-            pltpu.VMEM((3, HEADS, HEAD_DIM, 256), low),
+            pltpu.VMEM((2, 256, 768), low),
+            [buffer_scratch(order) for order in THIRDS],
+            buffer_scratch(LATER[0], (6,)),
+            pltpu.VMEM((768, 3 * WIDTH), low),
+            pltpu.VMEM((2, 768, WIDTH), low),
+            pltpu.VMEM((3, HEADS // 2, HEAD_DIM, 512), low),
             pltpu.VMEM((TILES * TILE, HEAD_DIM), low),
-        ]
-        + SMALL_SCRATCH
-        + SMALL_SCRATCH
-        + [
+            SMALL_SCRATCH,
+            SMALL_SCRATCH,
             pltpu.VMEM((256, 768), jnp.float32),
             pltpu.VMEM((256, 768), jnp.float32),
             pltpu.VMEM((8, 768), jnp.float32),
             pltpu.VMEM((8, 768), jnp.float32),
-            pltpu.VMEM((256, 768), jnp.float32),
-            pltpu.VMEM((MEMBERS, 3, HEAD_DIM, 256), low),
+            pltpu.VMEM((2, 256, 768), jnp.float32),
+            pltpu.VMEM((TILES, 3, HEAD_DIM, TILE), low),
             pltpu.VMEM((MEMBERS, 1, HEAD_DIM, 256), low),
             pltpu.VMEM((TILES, 1, TILE), jnp.float32),
             pltpu.VMEM((1, HEADS, HEAD_DIM, 256), low),
@@ -964,28 +1018,22 @@
             pltpu.VMEM((256, 3072), low),
             pltpu.VMEM((256, 768), jnp.float32),
             pltpu.VMEM((1, HEADS, HEAD_DIM, 256), low),
-            pltpu.VMEM((4, 768, 256), low),
-            pltpu.VMEM((3, HEADS, HEAD_DIM, 256), low),
+            pltpu.VMEM((3, 768, 256), low),
+            pltpu.VMEM((768, 512), low),
+            pltpu.VMEM((3, HEADS // 2, HEAD_DIM, 512), low),
             pltpu.VMEM((MEMBERS, 1, HEAD_DIM, 256), low),
-            pltpu.VMEM((MEMBERS, 3, HEAD_DIM, 256), low),
+            pltpu.VMEM((TILES, 3, HEAD_DIM, TILE), low),
             pltpu.VMEM((TILES, HEAD_DIM, TILE), jnp.float32),
             pltpu.VMEM((TILES, 1, TILE), jnp.float32),
             pltpu.VMEM((3, 4, SLOT, WIDTH), low),
+            pltpu.VMEM((2, 768, WIDTH), low),
+            pltpu.VMEM((768, WIDTH), low),
+            pltpu.VMEM((2, 256, 768), low),
+            pltpu.VMEM((256, 768), low),
+            landing_scratch(LATER[0], (6,)),
+            [landing_scratch(order) for order in THIRDS],
         ]
-        + landing_scratch(6, 16)
-        + landing_scratch(3, 16)
-        + sems(48)
-        + sems(96)
-        + sems(9)
-        + sems(10)
-        + sems(MEMBERS)
-        + sems(MEMBERS)
-        + sems(48)
-        + sems(96)
-        + sems(9)
-        + sems(10)
-        + sems(MEMBERS)
-        + sems(MEMBERS),
+        + [sems(count) for count in (48, 96, 9, 10, MEMBERS, MEMBERS) * 2 + (4,)],
         compiler_params=pltpu.CompilerParams(
             collective_id=0, has_side_effects=True, vmem_limit_bytes=VMEM_BYTES
         ),

time: 207 us -> 189 us (0.913)
  Pallas kernels: 206 us -> 188 us
    pallas_call x1, Pallas kernels: 204 us -> 186 us  [layer(): pl.pallas_call(layer_kernel, name='layer', out_shape=[low_array(256, 768)...]
where the time goes in v6:
time: 189 us
  Pallas kernels  188 us (99%)
    pallas_call x1, Pallas kernels, layer(): pl.pallas_call(layer_kernel, name='layer', out_shape=[low_array(256, 768)...  186 us

profile of v6, /device:TPU:1, one launch (start us, length us, event | category | flops | bytes accessed | tf_op | source)
XLA Modules:
  0.0 188.9 jit_solution(5104607447837569700)
XLA Ops:
  0.6 185.8 %layer.1 = (bf16[256,768]{1,0:T(8,128)(2,1)}, f32[256,768]{1,0:T(8,128)}, f32[3,12,384]{2,1,0:T(8,128)}, f32[12,384]{1,0:T(8,128)}, f32[12,1536]{1,0:T(8,128)}, /*index=5*/f32[12,1536]{1,0:T(8,128)}, f32[2,12]{1,0:T(2,128)}) custom-call(bf16[256,768]{1,0:T(8,128)(2,1)} %tokens.1, bf16[256,768]{1,0:T(8,128)(2,1)} %cotangent.1, bf16[3,12,384]{2,1,0:T(8,128)(2,1)} %a_qkv.1, ...), custom_call_target="tpu_custom_call" | custom-call | tf_op jit(solution)/shard_map/layer/pallas_call | solution.py:982
  186.5 2.5 %hand_over.1 = (bf16[256,768]{1,0:T(8,128)(2,1)}, f32[256,768]{1,0:T(8,128)}, f32[3,12,384]{2,1,0:T(8,128)}, f32[12,384]{1,0:T(8,128)}, f32[12,1536]{1,0:T(8,128)}, /*index=5*/f32[12,1536]{1,0:T(8,128)}, f32[2,12]{1,0:T(2,128)}) custom-call(bf16[256,768]{1,0:T(8,128)(2,1)} %get-tuple-element.21.refs_0_, f32[256,768]{1,0:T(8,128)} %get-tuple-element.22.refs_1_, ...), custom_call_target="tpu_custom_call" | custom-call | tf_op jit(solution)/shard_map/hand_over/pallas_call | solution.py:1050
